TPU v7x, 32 devices: a whole 2x2x4 slice. The times are simulated.
32 devices in a mesh: groups: 2 (over y), pts: 4 (over z), comp: 2 (over x), sub: 2 (over core).
Axes of the slice: x: 2, y: 2, z: 4, core: 2. Of those that a mesh axis runs over, the one named last changes fastest.
Arguments:
- spectra: float32 [5120, 768], P(('groups', 'pts', 'comp'), 'sub'), parts along dimension 0, may hold values from 0.2 to 2
- wind: float32 [5120], P(('groups', 'pts', 'comp')), parts along dimension 0, may hold values from 0.2 to 1
- growth: float32 [768], P('sub'), may hold values from -0.6 to 0.6
- damping: float32 [768], P('sub'), may hold values from 0.05 to 0.5
- row_cell: int32 [5120], P(('groups', 'pts', 'comp')), parts along dimension 0, may hold values from 0 to 4095, as said below
- land_mask: int32 [64, 128], P(('groups', 'pts', 'comp')), parts along dimension 0, may hold values from 0 to 1, as said below
- group_speed: float32 [64, 32, 128], P(('groups', 'sub'), ('pts', 'comp')), parts along dimension 0, may hold values from 0.4 to 1
- current: float32 [4, 32, 128], P('groups', ('pts', 'comp')), parts along dimension 0, may hold values from -0.3 to 0.3
- turning: float32 [64, 128], P(('groups', 'pts', 'comp')), parts along dimension 0, may hold values from -0.4 to 0.4
Outputs:
- advanced: float32 [2, 384, 64, 128], P('sub', ('pts', 'comp'), 'groups'), parts along dimension 2
There are 2 independent parts, one for each index of `groups`. A program takes and returns all parts, laid end to end along the dimension named above; an argument that names none is the same for every part. Nothing has to cross between parts.
Inputs may be any that keep to these rules, and one draw needn't show every extreme that they name: `row_cell`: 2560 distinct cells, exactly the cells where land_mask is 1. Tile t holds the cells of rows t * 4 to (t + 1) * 4 - 1; the sea cells of one tile are spread over the 8 owners, whose rows are the consecutive blocks of 320 rows, as evenly as possible, so at most 64 rows of one owner lie in one tile, and some tile is all sea. `land_mask`: 2560 sea cells; every tile holds 128 to 512 of them, some tile all sea.
All inputs are finite; a program needn't handle non-finite values.
Results may differ from a plain program's by a relative error of at most 0.00002.
Values sent between devices are 32-bit elements; how exact they have to be, the bound alone decides.
No kernel may reach another device: no remote copies, remote signals or barrier semaphores. Data moves between devices by JAX's collectives and lax.ppermute only.
A program may use at most 128 MiB of HBM per device.

v0:
```python
import jax
import jax.numpy as jnp
from jax import lax
from jax.sharding import PartitionSpec as P

DIR = 24
SUBSTEPS = 2


courant = 0.35


def with_halo(cells, sides, width):
    for axis, dim in sides:
        count = lax.axis_size(axis)
        ends = count - 1
        head = lax.slice_in_dim(cells, 0, width, axis=dim)
        tail = lax.slice_in_dim(cells, cells.shape[dim] - width, cells.shape[dim], axis=dim)
        cells = jnp.concatenate(
            [
                lax.ppermute(tail, axis, [(i, (i + 1) % count) for i in range(ends)]),
                cells,
                lax.ppermute(head, axis, [((i + 1) % count, i) for i in range(ends)]),
            ],
            axis=dim,
        )
    return cells


def take_slice(values, first_index, extent, along_axis):
    return lax.slice_in_dim(values, first_index, first_index + extent, axis=along_axis)


def upwind_divergence(padded, motion, along_axis):
    length = padded.shape[along_axis] - 4
    face_count = length + 1
    behind = take_slice(padded, 0, face_count, along_axis)
    centre = take_slice(padded, 1, face_count, along_axis)
    onward = take_slice(padded, 2, face_count, along_axis)
    beyond = take_slice(padded, 3, face_count, along_axis)
    left_face = (6.0 * centre + 3.0 * onward - behind) * 0.125
    right_face = (3.0 * centre + 6.0 * onward - beyond) * 0.125
    face_speed = 0.5 * (
        take_slice(motion, 1, face_count, along_axis)
        + take_slice(motion, 2, face_count, along_axis)
    )
    fluxes = jnp.maximum(face_speed, 0.0) * left_face + jnp.minimum(face_speed, 0.0) * right_face
    return take_slice(fluxes, 1, length, along_axis) - take_slice(fluxes, 0, length, along_axis)


def substep(extended, speed_x, speed_y, sea_mask):
    across = upwind_divergence(extended, speed_x, 1)
    centre_part = extended[:, 2:-2]
    padding = ((0, 0), (0, 0), (2, 2))
    sideways = upwind_divergence(jnp.pad(centre_part, padding), jnp.pad(speed_y, padding), 2)
    return (centre_part - courant * (across + sideways)) * sea_mask


def direction_tables(directions):
    angles = jnp.arange(directions, dtype=jnp.float32) * (2.0 * jnp.pi / directions)
    return (jnp.cos(angles), jnp.sin(angles))


def source_term(values, wind_speed, growth, damping):
    return values * jnp.exp(wind_speed[:, None] * growth[None, :] - damping[None, :])


def velocities(stacked, freq_count):
    cosine_table, sine_table = direction_tables(DIR)
    celerity = stacked[:freq_count][:, None]
    shape_out = (freq_count * DIR,) + stacked.shape[1:]
    speed_x = (
        celerity * cosine_table[None, :, None, None] + stacked[freq_count][None, None]
    ).reshape(shape_out)
    speed_y = (
        celerity * sine_table[None, :, None, None] + stacked[freq_count + 1][None, None]
    ).reshape(shape_out)
    return (speed_x, speed_y)


def deliver(bulk_rows, small_rows):
    return (
        lax.all_to_all(bulk_rows, ("pts", "comp"), split_axis=0, concat_axis=0, tiled=True),
        lax.all_to_all(small_rows, ("pts", "comp"), split_axis=0, concat_axis=0, tiled=True),
    )


def shards(spectra, wind, growth, damping, row_cell, land_mask, group_speed, current, turning):
    tile_count = lax.axis_size(("pts", "comp"))
    comp_width = spectra.shape[1]
    tile_rows, tile_cols = land_mask.shape
    cell_count = tile_rows * tile_cols
    capacity = cell_count // tile_count
    target = row_cell // cell_count
    local_cell = (row_cell - target * cell_count).astype(jnp.float32)
    matches = (target[:, None] == jnp.arange(tile_count, dtype=jnp.int32)[None, :]).astype(
        jnp.int32
    )
    bucket_slot = jnp.sum((jnp.cumsum(matches, axis=0) - 1) * matches, axis=1)

    def bucket(values, filler):
        shape_out = (tile_count, capacity) + values.shape[1:]
        return jnp.full(shape_out, filler, jnp.float32).at[target, bucket_slot].set(values)

    bulk_rows = bucket(source_term(spectra, wind, growth, damping), 0.0)
    small_rows = bucket(local_cell[:, None], float(cell_count))
    bulk_back, small_back = deliver(bulk_rows, small_rows)
    cell_index = small_back[:, :, 0].reshape(-1).astype(jnp.int32)
    flat_values = bulk_back.reshape((tile_count * capacity,) + bulk_back.shape[2:])
    tile_field = (
        jnp.zeros((cell_count,) + bulk_back.shape[2:], jnp.float32)
        .at[cell_index]
        .set(flat_values, mode="drop")
    )
    spectrum = tile_field.T.reshape(comp_width, tile_rows, tile_cols)
    freq_count = comp_width // DIR
    reach = 2 * SUBSTEPS
    stacked = jnp.concatenate([group_speed, current, land_mask.astype(jnp.float32)[None]], axis=0)
    rimmed = with_halo(stacked, ((("pts", "comp"), 1),), 2 * SUBSTEPS)
    speed_x, speed_y = velocities(rimmed, freq_count)
    sea_rim = rimmed[freq_count + 2 :]

    def window(values, margin):
        return lax.slice_in_dim(values, reach - margin, reach + tile_rows + margin, axis=1)

    for repeat in range(SUBSTEPS):
        extended = with_halo(spectrum, ((("pts", "comp"), 1),), 2)
        spectrum = substep(extended, window(speed_x, 2), window(speed_y, 0), window(sea_rim, 0)[0])
    blocks = spectrum.reshape(freq_count, DIR, tile_rows, tile_cols)
    wrapped = jnp.concatenate([blocks[:, -2:], blocks, blocks[:, :2]], axis=1)
    turning_full = jnp.broadcast_to(turning[None, None], wrapped.shape)
    blocks = blocks - upwind_divergence(wrapped, turning_full, 1)
    spectrum = blocks.reshape(comp_width, tile_rows, tile_cols)
    shipped = lax.all_to_all(spectrum, ("pts", "comp"), split_axis=0, concat_axis=1, tiled=True)
    return shipped[None]


def solution(mesh):
    placed = (
        P(("groups", "pts", "comp"), "sub"),
        P(("groups", "pts", "comp")),
        P("sub"),
        P("sub"),
        P(("groups", "pts", "comp")),
        P(("groups", "pts", "comp"), None),
        P(("groups", "sub"), ("pts", "comp"), None),
        P("groups", ("pts", "comp"), None),
        P(("groups", "pts", "comp"), None),
    )
    return jax.shard_map(
        shards,
        mesh=mesh,
        in_specs=placed,
        out_specs=P("sub", ("pts", "comp"), "groups", None),
        check_vma=False,
    )
```

profile of v0, /device:TPU:0, one launch (start us, length us, event | category | flops | bytes accessed | tf_op | source)
XLA Modules:
  0.0 204.5 jit_solution(2389600916933444912)
XLA Ops:
  0.0 0.7 subtract_convert_fusion
  0.8 0.9 reduce-window.6
  1.7 0.2 slice_reduce_fusion
  1.9 0.1 add_bitcast_fusion
  2.0 0.6 broadcast.199
  2.6 48.7 %scatter_fusion = f32[8,64]{1,0:T(8,128)} fusion(f32[8,64]{1,0:T(8,128)} %broadcast.199, s32[320]{0:T(512)S(1)} %fusion.41, f32[320]{0:T(512)S(1)} %get-tuple-element.5), kind=kCustom, calls=%fused_computation | custom fusion | bytes 6400 | tf_op jit(solution)/shard_map/scatter | solution.py:103
  51.4 7.3 %all-to-all-start = ((f32[8,64,1]{1,2,0:T(1,128)}), f32[8,64,1]{1,2,0:T(1,128)S(1)}, u32[]{:S(2)}, u32[]{:S(2)}) async-start(f32[8,64,1]{1,2,0:T(1,128)} %bitcast.4), calls=%async_computation | async-start | bytes 8192 | tf_op jit(solution)/shard_map/all_to_all | solution.py:84
  58.7 0.2 exponential_multiply_fusion
  58.8 0.9 broadcast_in_dim.18
  59.8 38.9 %scatter_fusion.1 = f32[8,64,384]{2,1,0:T(8,128)} fusion(f32[8,64,384]{2,1,0:T(8,128)} %broadcast_in_dim.18, s32[320]{0:T(512)S(1)} %fusion.41, f32[320,384]{1,0:T(8,128)S(1)} %exponential_multiply_fusion), kind=kCustom, calls=%fused_computation.1 | custom fusion | bytes 1477120 | tf_op jit(solution)/shard_map/scatter | solution.py:103
  98.7 6.5 %all-to-all-start.1 = ((f32[8,64,384]{2,1,0:T(8,128)}), f32[8,64,384]{2,1,0:T(8,128)S(1)}, u32[]{:S(2)}, u32[]{:S(2)}) async-start(f32[8,64,384]{2,1,0:T(8,128)} %scatter_fusion.1), calls=%async_computation.1 | async-start | bytes 1572864 | tf_op jit(solution)/shard_map/all_to_all | solution.py:83
  105.3 1.3 collective-permute-start.1
  106.6 4.5 %collective-permute-start = (f32[19,4,128]{2,1,0:T(4,128)S(1)}, f32[19,4,128]{2,1,0:T(4,128)S(1)}, u32[]{:S(2)}, u32[]{:S(2)}) collective-permute-start(f32[19,4,128]{2,1,0:T(4,128)S(1)} %pad_maximum_fusion.7), channel_id=1, source_target_pairs={{0,2},{2,4},{4,6},{6,8},{8,10},{10,12},{12,14},{1,3},{3,5},{5,7},{... | collective-permute-start | bytes 116744 | tf_op jit(solution)/shard_map/ppermute | solution.py:21
  111.2 0.1 mul.255
  111.4 0.1 mul.242
  111.5 0.1 convert_element_type.28
  111.6 1.8 collective-permute-done.1
  113.5 0.2 mul.238
  113.6 2.0 copy.20
  115.6 1.9 multiply_add_fusion
  117.6 7.8 %all-to-all-done.1 = f32[8,64,384]{2,1,0:T(8,128)S(1)} async-done(((f32[8,64,384]{2,1,0:T(8,128)}), f32[8,64,384]{2,1,0:T(8,128)S(1)}, u32[]{:S(2)}, u32[]{:S(2)}) %all-to-all-start.1) | async-done | bytes 786464 | tf_op jit(solution)/shard_map/all_to_all | solution.py:83
  125.4 0.9 copy-done
  126.2 3.0 %scatter_custom_fusion.2 = f32[512,384]{1,0:T(8,128)S(1)} fusion(s32[512]{0:T(512)S(1)} %bitcast.41, f32[512,384]{1,0:T(8,128)} %bitcast.39, f32[]{:T(128)} %constant.17.clone.1), kind=kCustom, calls=%fused_computation.65 | custom fusion | bytes 786944 | tf_op jit(solution)/shard_map/scatter | solution.py:113
  129.3 0.1 fusion.46
  129.3 1.3 collective-permute-start.3
  130.6 4.6 %collective-permute-start.2 = (f32[384,2,128]{0,2,1:T(8,128)S(1)}, f32[384,2,128]{0,2,1:T(8,128)S(1)}, u32[]{:S(2)}, u32[]{:S(2)}) collective-permute-start(f32[384,2,128]{0,2,1:T(8,128)S(1)} %get-tuple-element.11), channel_id=1, source_target_pairs={{0,2},{2,4},{4,6},{6,8},{8,10},{10,12},{12,14},{1,3},{3,5},{5,7},{... | collective-permute-start | bytes 1179656 | tf_op jit(solution)/shard_map/ppermute | solution.py:21
  135.2 1.3 fusion.33
  136.5 0.7 multiply_add_fusion.2
  137.1 3.3 %collective-permute-done.3 = f32[384,2,128]{0,2,1:T(8,128)S(1)} collective-permute-done((f32[384,2,128]{0,2,1:T(8,128)S(1)}, f32[384,2,128]{0,2,1:T(8,128)S(1)}, u32[]{:S(2)}, u32[]{:S(2)}) %collective-permute-start.3) | collective-permute-done | bytes 393248 | tf_op jit(solution)/shard_map/ppermute | solution.py:23
  140.5 8.6 %collective-permute-done.2 = f32[384,2,128]{0,2,1:T(8,128)S(1)} collective-permute-done((f32[384,2,128]{0,2,1:T(8,128)S(1)}, f32[384,2,128]{0,2,1:T(8,128)S(1)}, u32[]{:S(2)}, u32[]{:S(2)}) %collective-permute-start.2) | collective-permute-done | bytes 393248 | tf_op jit(solution)/shard_map/ppermute | solution.py:21
  149.0 0.5 fusion.19
  149.5 0.2 fusion.32
  149.8 0.1 fusion.45
  149.8 1.3 collective-permute-start.5
  151.1 5.0 %collective-permute-start.4 = (f32[384,2,128]{0,2,1:T(8,128)S(1)}, f32[384,2,128]{0,2,1:T(8,128)S(1)}, u32[]{:S(2)}, u32[]{:S(2)}) collective-permute-start(f32[384,2,128]{0,2,1:T(8,128)S(1)} %get-tuple-element.9), channel_id=1, source_target_pairs={{0,2},{2,4},{4,6},{6,8},{8,10},{10,12},{12,14},{1,3},{3,5},{5,7},{... | collective-permute-start | bytes 1179656 | tf_op jit(solution)/shard_map/ppermute | solution.py:21
  156.2 0.7 multiply_add_fusion.1
  156.9 6.6 %collective-permute-done.5 = f32[384,2,128]{0,2,1:T(8,128)S(1)} collective-permute-done((f32[384,2,128]{0,2,1:T(8,128)S(1)}, f32[384,2,128]{0,2,1:T(8,128)S(1)}, u32[]{:S(2)}, u32[]{:S(2)}) %collective-permute-start.5) | collective-permute-done | bytes 393248 | tf_op jit(solution)/shard_map/ppermute | solution.py:23
  163.5 9.6 %collective-permute-done.4 = f32[384,2,128]{0,2,1:T(8,128)S(1)} collective-permute-done((f32[384,2,128]{0,2,1:T(8,128)S(1)}, f32[384,2,128]{0,2,1:T(8,128)S(1)}, u32[]{:S(2)}, u32[]{:S(2)}) %collective-permute-start.4) | collective-permute-done | bytes 393248 | tf_op jit(solution)/shard_map/ppermute | solution.py:21
  173.1 0.5 fusion.12
  173.6 0.2 fusion.28
  173.8 0.3 copy.22
  174.2 0.7 fusion.2
  174.8 0.2 fusion.24
  175.1 0.5 copy.23
  175.6 27.7 %all_to_all.25 = f32[384,4,128]{2,1,0:T(4,128)S(1)} all-to-all(f32[384,4,128]{2,1,0:T(4,128)S(1)} %copy.23), channel_id=1, replica_groups=mesh['groups'=2,'pts'=4,'comp'=2,'sub'=2] {'pts','comp'}, dimensions={0} | all-to-all | bytes 1572864 | tf_op jit(solution)/shard_map/all_to_all | solution.py:134
  203.3 0.1 copy.24
  203.3 0.1 copy.25
  203.4 1.1 copy.26
  (40 shorter events, 0.4 us)
Async XLA Ops:
  0.0 58.6 %copy-start.1 = (f32[320,384]{1,0:T(8,128)S(1)}, f32[320,384]{1,0:T(8,128)}, u32[]{:S(2)}) copy-start(f32[320,384]{1,0:T(8,128)} %param.9) | copy-start | bytes 1474564
  0.0 58.6 %copy-start.4 = (f32[384]{0:T(512)S(1)}, f32[384]{0:T(512)}, u32[]{:S(2)}) copy-start(f32[384]{0:T(512)} %param.12) | copy-start | bytes 4612
  0.0 58.6 %copy-start.5 = (f32[384]{0:T(512)S(1)}, f32[384]{0:T(512)}, u32[]{:S(2)}) copy-start(f32[384]{0:T(512)} %param.11) | copy-start | bytes 4612
  0.0 58.7 %copy-start.6 = (f32[320]{0:T(512)S(1)}, f32[320]{0:T(512)}, u32[]{:S(2)}) copy-start(f32[320]{0:T(512)} %param.10) | copy-start | bytes 3844
  51.4 47.4 %all-to-all-start = ((f32[8,64,1]{1,2,0:T(1,128)}), f32[8,64,1]{1,2,0:T(1,128)S(1)}, u32[]{:S(2)}, u32[]{:S(2)}) async-start(f32[8,64,1]{1,2,0:T(1,128)} %bitcast.4), calls=%async_computation | async-start | bytes 8192 | tf_op jit(solution)/shard_map/all_to_all | solution.py:84
  59.8 45.5 %copy-start.7 = (s32[4,128]{1,0:T(4,128)S(1)}, s32[4,128]{1,0:T(4,128)}, u32[]{:S(2)}) copy-start(s32[4,128]{1,0:T(4,128)} %param.14) | copy-start | bytes 6148
  59.8 45.5 %copy-start.2 = (f32[16,4,128]{2,1,0:T(4,128)S(1)}, f32[16,4,128]{2,1,0:T(4,128)}, u32[]{:S(2)}) copy-start(f32[16,4,128]{2,1,0:T(4,128)} %param.15) | copy-start | bytes 98308
  59.8 45.5 %copy-start.3 = (f32[2,4,128]{2,1,0:T(4,128)S(1)}, f32[2,4,128]{2,1,0:T(4,128)}, u32[]{:S(2)}) copy-start(f32[2,4,128]{2,1,0:T(4,128)} %param.16) | copy-start | bytes 12292
  98.7 26.6 %all-to-all-start.1 = ((f32[8,64,384]{2,1,0:T(8,128)}), f32[8,64,384]{2,1,0:T(8,128)S(1)}, u32[]{:S(2)}, u32[]{:S(2)}) async-start(f32[8,64,384]{2,1,0:T(8,128)} %scatter_fusion.1), calls=%async_computation.1 | async-start | bytes 1572864 | tf_op jit(solution)/shard_map/all_to_all | solution.py:83
  105.3 8.1 %collective-permute-start.1 = (f32[19,4,128]{2,1,0:T(4,128)S(1)}, f32[19,4,128]{2,1,0:T(4,128)S(1)}, u32[]{:S(2)}, u32[]{:S(2)}) collective-permute-start(f32[19,4,128]{2,1,0:T(4,128)S(1)} %pad_maximum_fusion.7), channel_id=1, source_target_pairs={{2,0},{4,2},{6,4},{8,6},{10,8},{12,10},{14,12},{3,1},{5,3},{7,5},{... | collective-permute-start | bytes 116744 | tf_op jit(solution)/shard_map/ppermute | solution.py:23
  106.6 6.8 %collective-permute-start = (f32[19,4,128]{2,1,0:T(4,128)S(1)}, f32[19,4,128]{2,1,0:T(4,128)S(1)}, u32[]{:S(2)}, u32[]{:S(2)}) collective-permute-start(f32[19,4,128]{2,1,0:T(4,128)S(1)} %pad_maximum_fusion.7), channel_id=1, source_target_pairs={{0,2},{2,4},{4,6},{6,8},{8,10},{10,12},{12,14},{1,3},{3,5},{5,7},{... | collective-permute-start | bytes 116744 | tf_op jit(solution)/shard_map/ppermute | solution.py:21
  125.4 0.9 copy-start
  129.3 11.1 %collective-permute-start.3 = (f32[384,2,128]{0,2,1:T(8,128)S(1)}, f32[384,2,128]{0,2,1:T(8,128)S(1)}, u32[]{:S(2)}, u32[]{:S(2)}) collective-permute-start(f32[384,2,128]{0,2,1:T(8,128)S(1)} %get-tuple-element.12), channel_id=1, source_target_pairs={{2,0},{4,2},{6,4},{8,6},{10,8},{12,10},{14,12},{3,1},{5,3},{7,5},{... | collective-permute-start | bytes 1179656 | tf_op jit(solution)/shard_map/ppermute | solution.py:23
  130.6 18.4 %collective-permute-start.2 = (f32[384,2,128]{0,2,1:T(8,128)S(1)}, f32[384,2,128]{0,2,1:T(8,128)S(1)}, u32[]{:S(2)}, u32[]{:S(2)}) collective-permute-start(f32[384,2,128]{0,2,1:T(8,128)S(1)} %get-tuple-element.11), channel_id=1, source_target_pairs={{0,2},{2,4},{4,6},{6,8},{8,10},{10,12},{12,14},{1,3},{3,5},{5,7},{... | collective-permute-start | bytes 1179656 | tf_op jit(solution)/shard_map/ppermute | solution.py:21
  149.5 6.6 %copy-start.8 = (f32[4,128]{1,0:T(4,128)S(1)}, f32[4,128]{1,0:T(4,128)}, u32[]{:S(2)}) copy-start(f32[4,128]{1,0:T(4,128)} %param.17) | copy-start | bytes 6148
  149.8 13.7 %collective-permute-start.5 = (f32[384,2,128]{0,2,1:T(8,128)S(1)}, f32[384,2,128]{0,2,1:T(8,128)S(1)}, u32[]{:S(2)}, u32[]{:S(2)}) collective-permute-start(f32[384,2,128]{0,2,1:T(8,128)S(1)} %get-tuple-element.10), channel_id=1, source_target_pairs={{2,0},{4,2},{6,4},{8,6},{10,8},{12,10},{14,12},{3,1},{5,3},{7,5},{... | collective-permute-start | bytes 1179656 | tf_op jit(solution)/shard_map/ppermute | solution.py:23
  151.1 22.0 %collective-permute-start.4 = (f32[384,2,128]{0,2,1:T(8,128)S(1)}, f32[384,2,128]{0,2,1:T(8,128)S(1)}, u32[]{:S(2)}, u32[]{:S(2)}) collective-permute-start(f32[384,2,128]{0,2,1:T(8,128)S(1)} %get-tuple-element.9), channel_id=1, source_target_pairs={{0,2},{2,4},{4,6},{6,8},{8,10},{10,12},{12,14},{1,3},{3,5},{5,7},{... | collective-permute-start | bytes 1179656 | tf_op jit(solution)/shard_map/ppermute | solution.py:21
where the time goes:
time: 207 us; the launch traced here: 205 us
  local copies, waits for them, and re-layouts  98 us (47%)
  waiting for transfers between devices  37.7 us (18%)
  starting transfers between devices  31.8 us (15%)
  blocking collectives  27.7 us (13%)
  other arithmetic  8.99 us (4%)
    scatter x2, local copies, waits for them, and re-layouts, bucket(): jnp.full(shape_out, filler, jnp.float32).at[target, bucket_slot].set(values)  87.7 us
    all_to_all x1, blocking collectives, shards(): lax.all_to_all(spectrum, ('pts', 'comp'), split_axis=0, concat_axis=1, ti...  27.7 us
    ppermute x3, waiting for transfers between devices, with_halo(): lax.ppermute(tail, axis, [(i, (i + 1) % count) for i in range(ends)])  18.2 us
    ppermute x3, starting transfers between devices, with_halo(): lax.ppermute(tail, axis, [(i, (i + 1) % count) for i in range(ends)])  14.2 us
    ppermute x3, waiting for transfers between devices, with_halo(): lax.ppermute(head, axis, [((i + 1) % count, i) for i in range(ends)])  11.7 us
    all_to_all x1, waiting for transfers between devices, deliver(): lax.all_to_all(bulk_rows, ('pts', 'comp'), split_axis=0, concat_axis=0, t...  7.78 us
    all_to_all x1, starting transfers between devices, deliver(): lax.all_to_all(small_rows, ('pts', 'comp'), split_axis=0, concat_axis=0,...  7.26 us
    all_to_all x1, starting transfers between devices, deliver(): lax.all_to_all(bulk_rows, ('pts', 'comp'), split_axis=0, concat_axis=0, t...  6.53 us
  transfers between devices with their start and end apart: 8, of which 6 were waited for; matrix products, arithmetic and copies ran while one was open for 23% of the time, Pallas kernels for 0%

commit v1 on v0

--- a/solution.py
+++ b/solution.py
@@ -1,10 +1,15 @@
+import functools
 import jax
 import jax.numpy as jnp
 from jax import lax
+from jax.experimental import pallas as pl
+from jax.experimental.pallas import tpu as pltpu
 from jax.sharding import PartitionSpec as P
 
 DIR = 24
 SUBSTEPS = 2
+LANES = 128
+GROUP = ("pts", "comp")
 
 
 courant = 0.35
@@ -80,13 +85,13 @@
 
 def deliver(bulk_rows, small_rows):
     return (
-        lax.all_to_all(bulk_rows, ("pts", "comp"), split_axis=0, concat_axis=0, tiled=True),
-        lax.all_to_all(small_rows, ("pts", "comp"), split_axis=0, concat_axis=0, tiled=True),
-    )
-
-
-def shards(spectra, wind, growth, damping, row_cell, land_mask, group_speed, current, turning):
-    tile_count = lax.axis_size(("pts", "comp"))
+        lax.all_to_all(bulk_rows, GROUP, split_axis=0, concat_axis=0, tiled=True),
+        lax.all_to_all(small_rows, GROUP, split_axis=0, concat_axis=0, tiled=True),
+    )
+
+
+def tile_plan(spectra, wind, growth, damping, row_cell, land_mask, group_speed, current, turning):
+    tile_count = lax.axis_size(GROUP)
     comp_width = spectra.shape[1]
     tile_rows, tile_cols = land_mask.shape
     cell_count = tile_rows * tile_cols
@@ -116,7 +121,7 @@
     freq_count = comp_width // DIR
     reach = 2 * SUBSTEPS
     stacked = jnp.concatenate([group_speed, current, land_mask.astype(jnp.float32)[None]], axis=0)
-    rimmed = with_halo(stacked, ((("pts", "comp"), 1),), 2 * SUBSTEPS)
+    rimmed = with_halo(stacked, ((GROUP, 1),), 2 * SUBSTEPS)
     speed_x, speed_y = velocities(rimmed, freq_count)
     sea_rim = rimmed[freq_count + 2 :]
 
@@ -124,15 +129,287 @@
         return lax.slice_in_dim(values, reach - margin, reach + tile_rows + margin, axis=1)
 
     for repeat in range(SUBSTEPS):
-        extended = with_halo(spectrum, ((("pts", "comp"), 1),), 2)
+        extended = with_halo(spectrum, ((GROUP, 1),), 2)
         spectrum = substep(extended, window(speed_x, 2), window(speed_y, 0), window(sea_rim, 0)[0])
     blocks = spectrum.reshape(freq_count, DIR, tile_rows, tile_cols)
     wrapped = jnp.concatenate([blocks[:, -2:], blocks, blocks[:, :2]], axis=1)
     turning_full = jnp.broadcast_to(turning[None, None], wrapped.shape)
     blocks = blocks - upwind_divergence(wrapped, turning_full, 1)
     spectrum = blocks.reshape(comp_width, tile_rows, tile_cols)
-    shipped = lax.all_to_all(spectrum, ("pts", "comp"), split_axis=0, concat_axis=1, tiled=True)
+    shipped = lax.all_to_all(spectrum, GROUP, split_axis=0, concat_axis=1, tiled=True)
     return shipped[None]
+
+
+def pack_kernel(parts, spectra_ref, wind_ref, growth_ref, damping_ref, speed_ref, out_ref):
+    rows, comps = spectra_ref.shape
+    half = LANES // 2
+    full = rows // LANES
+    width = comps // parts
+    wind_cols = jnp.broadcast_to(wind_ref[...], (LANES, wind_ref.shape[1])).T
+    low = lax.broadcasted_iota(jnp.int32, (8, LANES), 1) < half
+    groups = []
+    for block in range(comps // LANES):
+        lanes = pl.ds(block * LANES, LANES)
+        growth = growth_ref[:, lanes]
+        damping = damping_ref[:, lanes]
+
+        def source(first, count):
+            span = pl.ds(first, count)
+            return spectra_ref[span, lanes] * jnp.exp(
+                wind_cols[first : first + count] * growth - damping
+            )
+
+        for chunk in range(full):
+            turned = source(chunk * LANES, LANES).T
+            for g in range(LANES // 8):
+                part, within = divmod(block * LANES + g * 8, width)
+                out_ref[part, pl.ds(chunk * width + within, 8), :] = turned[g * 8 : g * 8 + 8]
+        tail = source(full * LANES, half)
+        turned = jnp.concatenate([tail, tail], axis=0).T
+        groups += [turned[g * 8 : g * 8 + 8] for g in range(LANES // 8)]
+    for part in range(parts):
+        for g in range(DIR // 8):
+            first = groups[part * width // 8 + g]
+            second = groups[(part * width + DIR) // 8 + g]
+            out_ref[part, pl.ds(full * width + g * 8, 8), :] = jnp.where(low, first, second)
+        out_ref[part, pl.ds(full * width + DIR, 8), :] = speed_ref[pl.ds(part * 8, 8), :]
+
+
+def slab_kernel(
+    parts, tile_rows, full, recv_ref, small_ref, trig_ref, out_ref, onehot, spread, first, second, table
+):
+    slab_rows = parts * tile_rows
+    freqs = 2
+    width = freqs * DIR
+    half = LANES // 2
+    small_rows = small_ref.shape[0] // parts
+    highs = slab_rows // 2
+    depth = onehot.shape[1] // 2
+    low_lane = lax.broadcasted_iota(jnp.int32, (1, LANES), 1) < half
+    low_lane_wide = lax.broadcasted_iota(jnp.int32, (DIR, LANES), 1) < half
+    cell_iota = lax.broadcasted_iota(jnp.int32, (2 * LANES, LANES), 0)
+
+    def cells_of(owner, chunk):
+        return small_ref[pl.ds(owner * small_rows + 4 * tile_rows + chunk, 1), :].astype(jnp.int32)
+
+    def place(chunk_index, cells, values):
+        high = cells // (2 * LANES)
+        low = cells - high * (2 * LANES)
+        hot = (cell_iota == low).astype(jnp.float32).astype(jnp.bfloat16)
+        onehot[:, pl.ds(chunk_index * LANES, LANES)] = hot
+        onehot[:, pl.ds(depth + chunk_index * LANES, LANES)] = hot
+        head = values.astype(jnp.bfloat16)
+        rest = (values - head.astype(jnp.float32)).astype(jnp.bfloat16)
+        for h in range(highs):
+            pick = jnp.broadcast_to((high == h).astype(jnp.float32), (width, LANES)).astype(jnp.bfloat16)
+            spread[pl.ds(h * width, width), pl.ds(chunk_index * LANES, LANES)] = head * pick
+            spread[pl.ds(h * width, width), pl.ds(depth + chunk_index * LANES, LANES)] = rest * pick
+
+    per_pair = 2 * full + 1
+    for pair in range(parts // 2):
+        even, odd = 2 * pair, 2 * pair + 1
+        for side, owner in enumerate((even, odd)):
+            for chunk in range(full):
+                values = recv_ref[owner, pl.ds(chunk * width, width), :]
+                place(pair * per_pair + side * full + chunk, cells_of(owner, chunk), values)
+        tail_even = recv_ref[even, pl.ds(full * width, DIR), :]
+        tail_odd = recv_ref[odd, pl.ds(full * width, DIR), :]
+        swapped_even = pltpu.roll(tail_even, half, 1)
+        swapped_odd = pltpu.roll(tail_odd, half, 1)
+        values = jnp.concatenate(
+            [
+                jnp.where(low_lane_wide, tail_even, swapped_odd),
+                jnp.where(low_lane_wide, swapped_even, tail_odd),
+            ],
+            axis=0,
+        )
+        cells_even, cells_odd = cells_of(even, full), cells_of(odd, full)
+        cells = jnp.where(low_lane, cells_even, pltpu.roll(cells_odd, half, 1))
+        place(pair * per_pair + 2 * full, cells, values)
+
+    scattered = lax.dot_general(
+        spread[...], onehot[...], (((1,), (1,)), ((), ())), preferred_element_type=jnp.float32
+    )
+    nothing = jnp.zeros((DIR, LANES), jnp.float32)
+    for field in (first, second):
+        for f in range(freqs):
+            for edge in (0, 1, slab_rows + 2, slab_rows + 3):
+                field[f, edge] = nothing
+    for h in range(highs):
+        for f in range(freqs):
+            span = scattered[h * width + f * DIR : h * width + (f + 1) * DIR]
+            first[f, 2 * h + 2] = span[:, :LANES]
+            first[f, 2 * h + 3] = span[:, LANES:]
+
+    lane = lax.broadcasted_iota(jnp.int32, (slab_rows, LANES), 1)
+    zero_rows = jnp.zeros((8, LANES), jnp.float32)
+
+    def gather(read):
+        return jnp.concatenate([read(owner) for owner in range(parts)], axis=0)
+
+    def small(kind):
+        return gather(lambda owner: small_ref[pl.ds(owner * small_rows + kind * tile_rows, tile_rows), :])
+
+    gain = 0.5 * courant / 8.0
+    slots = iter(range(table.shape[0]))
+
+    def keep(rows):
+        slot = next(slots)
+        table[slot, pl.ds(8, slab_rows), :] = rows
+        return slot
+
+    def face_x(rows):
+        slot = next(slots)
+        table[slot, pl.ds(0, 8), :] = zero_rows
+        table[slot, pl.ds(8 + slab_rows, 8), :] = zero_rows
+        table[slot, pl.ds(8, slab_rows), :] = rows
+        faces = gain * (table[slot, pl.ds(7, slab_rows + 8), :] + table[slot, pl.ds(8, slab_rows + 8), :])
+        table[slot, pl.ds(7, slab_rows + 8), :] = faces
+        return slot
+
+    def face_y(rows):
+        after = jnp.where(lane < LANES - 1, pltpu.roll(rows, LANES - 1, 1), 0.0)
+        before = jnp.where(lane > 0, pltpu.roll(rows, 1, 1), 0.0)
+        return keep(gain * (rows + after)), keep(gain * (rows + before))
+
+    current_x, current_y, turning, land = (small(kind) for kind in range(4))
+    current_x_face = face_x(current_x)
+    current_y_faces = face_y(current_y)
+    speeds = [
+        gather(lambda owner: recv_ref[owner, pl.ds(full * width + DIR + f * tile_rows, tile_rows), :])
+        for f in range(freqs)
+    ]
+    speed_x_face = [face_x(s) for s in speeds]
+    speed_y_faces = [face_y(s) for s in speeds]
+    land_slot = keep(land)
+    ahead = jnp.maximum(turning, 0.0) * 0.125
+    back = jnp.minimum(turning, 0.0) * 0.125
+    bend_slots = [
+        keep(rows)
+        for rows in (
+            -ahead,
+            7.0 * ahead + 3.0 * back,
+            1.0 - 3.0 * (ahead - back),
+            -3.0 * ahead - 7.0 * back,
+            back,
+        )
+    ]
+
+    cosine = trig_ref[0]
+    sine = trig_ref[1]
+    lane_wide = lax.broadcasted_iota(jnp.int32, (DIR, LANES), 1)
+
+    def row(slot, x):
+        return table[slot, pl.ds(8 + x, 1), :]
+
+    def flux(speed, behind, centre, onward, beyond):
+        shared = 3.0 * (centre + onward)
+        return jnp.maximum(speed, 0.0) * (shared + 3.0 * centre - behind) + jnp.minimum(speed, 0.0) * (
+            shared + 3.0 * onward - beyond
+        )
+
+    def flux_x(field, f, x):
+        speed = row(speed_x_face[f], x) * cosine + row(current_x_face, x)
+        return flux(speed, field[f, x + 1], field[f, x + 2], field[f, x + 3], field[f, x + 4])
+
+    def advance(field, f, x, entering):
+        leaving = flux_x(field, f, x)
+        centre = field[f, x + 2]
+        up1 = jnp.where(lane_wide < LANES - 1, pltpu.roll(centre, LANES - 1, 1), 0.0)
+        up2 = jnp.where(lane_wide < LANES - 2, pltpu.roll(centre, LANES - 2, 1), 0.0)
+        down1 = jnp.where(lane_wide > 0, pltpu.roll(centre, 1, 1), 0.0)
+        down2 = jnp.where(lane_wide > 1, pltpu.roll(centre, 2, 1), 0.0)
+        right = flux(
+            row(speed_y_faces[f][0], x) * sine + row(current_y_faces[0], x), down1, centre, up1, up2
+        )
+        left = flux(
+            row(speed_y_faces[f][1], x) * sine + row(current_y_faces[1], x), down2, down1, centre, up1
+        )
+        moved = (centre - (leaving - entering) - (right - left)) * row(land_slot, x)
+        return moved, leaving
+
+    def sweep(field, finish):
+        def body(x, carry):
+            out = []
+            for f in range(freqs):
+                moved, leaving = advance(field, f, x, carry[f])
+                finish(f, x, moved)
+                out.append(leaving)
+            return tuple(out)
+
+        lax.fori_loop(0, slab_rows, body, tuple(flux_x(field, f, -1) for f in range(freqs)))
+
+    def store(f, x, moved):
+        second[f, x + 2] = moved
+
+    def refract(f, x, moved):
+        bent = row(bend_slots[2], x) * moved
+        for slot, shift in zip(bend_slots, (2, 1, 0, DIR - 1, DIR - 2)):
+            if shift:
+                bent = bent + row(slot, x) * jnp.roll(moved, shift, axis=0)
+        for g in range(DIR // 8):
+            out_ref[pl.ds((f * DIR + g * 8) * slab_rows + x, 8, stride=slab_rows), :] = bent[g * 8 : g * 8 + 8]
+
+    sweep(first, store)
+    sweep(second, refract)
+
+
+def slab_plan(spectra, wind, growth, damping, row_cell, land_mask, group_speed, current, turning):
+    parts = lax.axis_size(GROUP)
+    rows, comps = spectra.shape
+    tile_rows = land_mask.shape[0]
+    width = comps // parts
+    full = rows // LANES
+    slab_rows = parts * tile_rows
+    spare = -(-rows // LANES) * LANES - rows
+    cells = jnp.pad(row_cell.astype(jnp.float32), (0, spare)).reshape(-1, LANES)
+    small = jnp.concatenate(
+        [current.reshape(-1, LANES), turning, land_mask.astype(jnp.float32), cells], axis=0
+    )
+    small = jnp.pad(small, ((0, -small.shape[0] % 8), (0, 0)))
+    small_all = lax.all_gather(small, GROUP, axis=0, tiled=True)
+    block_rows = full * width + DIR + 2 * tile_rows
+    vmem = pltpu.CompilerParams(vmem_limit_bytes=48 * 1024 * 1024)
+    packed = pl.pallas_call(
+        functools.partial(pack_kernel, parts),
+        out_shape=jax.ShapeDtypeStruct((parts, block_rows, LANES), jnp.float32),
+        compiler_params=vmem,
+        name="pack",
+    )(
+        spectra,
+        jnp.pad(wind, (0, spare))[None],
+        growth[None],
+        damping[None],
+        group_speed.reshape(-1, LANES),
+    )
+    recv = lax.all_to_all(packed, GROUP, split_axis=0, concat_axis=0, tiled=True)
+    trig = jnp.stack([jnp.broadcast_to(t[:, None], (DIR, LANES)) for t in direction_tables(DIR)])
+    depth = parts * rows
+    out = pl.pallas_call(
+        functools.partial(slab_kernel, parts, tile_rows, full),
+        out_shape=jax.ShapeDtypeStruct((width * slab_rows, LANES), jnp.float32),
+        scratch_shapes=[
+            pltpu.VMEM((2 * LANES, 2 * depth), jnp.bfloat16),
+            pltpu.VMEM((slab_rows // 2 * width, 2 * depth), jnp.bfloat16),
+            pltpu.VMEM((2, slab_rows + 4, DIR, LANES), jnp.float32),
+            pltpu.VMEM((2, slab_rows + 4, DIR, LANES), jnp.float32),
+            pltpu.VMEM((15, slab_rows + 16, LANES), jnp.float32),
+        ],
+        compiler_params=vmem,
+        name="slab",
+    )(recv, small_all, trig)
+    return out.reshape(1, width, slab_rows, LANES)
+
+
+def shards(*arrays):
+    spectra, land_mask = arrays[0], arrays[5]
+    parts = lax.axis_size(GROUP)
+    rows, comps = spectra.shape
+    whole_frequencies = comps == parts * 2 * DIR
+    fits = rows % LANES == LANES // 2 and land_mask.shape == (4, LANES) and parts % 2 == 0
+    if whole_frequencies and fits:
+        return slab_plan(*arrays)
+    return tile_plan(*arrays)
 
 
 def solution(mesh):

time: 207 us -> 60.6 us (0.29)
  local copies, waits for them, and re-layouts: 98 us -> 4.67 us
  waiting for transfers between devices: 37.7 us -> 0.01 us
  starting transfers between devices: 31.8 us -> 7.38 us
  Pallas kernels: 0 us -> 12 us
  other arithmetic: 8.99 us -> 0.11 us
  blocking collectives: 27.7 us -> 35.9 us
    scatter x3 -> x0, local copies, waits for them, and re-layouts: 90.7 us -> none  [the longest x2 87.7 us: bucket(): jnp.full(shape_out, filler, jnp.float32).at[target, bucket_slot].set(values)]
    all_gather x0 -> x1, blocking collectives: none -> 35.9 us  [slab_plan(): small_all = lax.all_gather(small, GROUP, axis=0, tiled=True)]
    ppermute x6 -> x0, waiting for transfers between devices: 29.9 us -> none  [the longest x3 18.2 us: with_halo(): lax.ppermute(tail, axis, [(i, (i + 1) % count) for i in range(ends)])]
    all_to_all x1 -> x0, blocking collectives: 27.7 us -> none  [shards(): lax.all_to_all(spectrum, ('pts', 'comp'), split_axis=0, concat_axis=1, ti...]
    ppermute x6 -> x0, starting transfers between devices: 18 us -> none  [the longest x3 14.2 us: with_halo(): lax.ppermute(tail, axis, [(i, (i + 1) % count) for i in range(ends)])]
    pallas_call x0 -> x2, Pallas kernels: none -> 12 us  [the longest x1 10.9 us: slab_plan(): pl.pallas_call(functools.partial(slab_kernel, parts, tile_rows, full), ou...]
    all_to_all x2 -> x1, waiting for transfers between devices: 7.78 us -> 0.01 us  [slab_plan(): lax.all_to_all(packed, GROUP, split_axis=0, concat_axis=0, tiled=True)]
    all_to_all x2 -> x1, starting transfers between devices: 13.8 us -> 7.38 us  [slab_plan(): lax.all_to_all(packed, GROUP, split_axis=0, concat_axis=0, tiled=True)]
  transfers between devices with their start and end apart: 8 -> 1, of which waited for: 6 -> 0; matrix products, arithmetic and copies ran while one was open for 23% -> 0% of each run, Pallas kernels for 0% -> 0%
where the time goes in v1:
time: 60.6 us; the launch traced here: 60.2 us
  blocking collectives  35.9 us (59%)
  Pallas kernels  12 us (20%)
  starting transfers between devices  7.38 us (12%)
  local copies, waits for them, and re-layouts  4.67 us (8%)
    all_gather x1, blocking collectives, slab_plan(): small_all = lax.all_gather(small, GROUP, axis=0, tiled=True)  35.9 us
    pallas_call x1, Pallas kernels, slab_plan(): pl.pallas_call(functools.partial(slab_kernel, parts, tile_rows, full), ou...  10.9 us
    all_to_all x1, starting transfers between devices, slab_plan(): lax.all_to_all(packed, GROUP, split_axis=0, concat_axis=0, tiled=True)  7.38 us
    unnamed x16, local copies, waits for them, and re-layouts  3.82 us
  transfers between devices with their start and end apart: 1, of which 0 were waited for; matrix products, arithmetic and copies ran while one was open for 0% of the time, Pallas kernels for 0%

profile of v1, /device:TPU:0, one launch (start us, length us, event | category | flops | bytes accessed | tf_op | source)
XLA Modules:
  0.0 60.2 jit_solution(12643950149089576093)
XLA Ops:
  0.0 0.0 copy-start.3
  0.0 0.7 %broadcast_in_dim.12.growth_ref = f32[1,384]{1,0:T(1,128)S(1)} reshape(f32[384]{0:T(512)} %param.11) | data formatting | bytes 3072 | tf_op jit(solution)/shard_map/broadcast_in_dim | solution.py:381
  0.7 0.0 copy-done.3
  0.7 0.0 copy-start.4
  0.7 0.7 %copy-done.4 = f32[320]{0:T(512)S(1)} copy-done((f32[320]{0:T(512)S(1)}, f32[320]{0:T(512)}, u32[]{:S(2)}) %copy-start.4) | copy-done | bytes 1304
  1.4 0.0 copy-start
  1.4 1.0 %copy-done = f32[320,384]{1,0:T(8,128)S(1)} copy-done((f32[320,384]{1,0:T(8,128)S(1)}, f32[320,384]{1,0:T(8,128)}, u32[]{:S(2)}) %copy-start) | copy-done | bytes 491544
  2.4 0.0 copy-start.1
  2.4 0.8 %copy-done.1 = f32[16,4,128]{2,1,0:T(4,128)S(1)} copy-done((f32[16,4,128]{2,1,0:T(4,128)S(1)}, f32[16,4,128]{2,1,0:T(4,128)}, u32[]{:S(2)}) %copy-start.1) | copy-done | bytes 32792
  3.2 1.1 %pack.1 = f32[8,128,128]{2,1,0:T(8,128)} custom-call(f32[320,384]{1,0:T(8,128)S(1)} %copy-done, f32[1,384]{1,0:T(1,128)S(1)} %broadcast_in_dim.11.wind_ref, f32[1,384]{1,0:T(1,128)S(1)} %broadcast_in_dim.12.growth_ref, f32[1,384]{1,0:T(1,128)S(1)} %broadcast_in_dim.13.damping_ref, f32[64,128]{1,0:T(8,128)S(1)} %bitcast.5), custom_call_target="tpu_custom_call" | custom-call | tf_op jit(solution)/shard_map/pack/pallas_call | solution.py:373
  4.3 0.0 copy-start.5
  4.3 7.4 %all-to-all-start = ((f32[8,128,128]{2,1,0:T(8,128)}), f32[8,128,128]{2,1,0:T(8,128)S(1)}, u32[]{:S(2)}, u32[]{:S(2)}) async-start(f32[8,128,128]{2,1,0:T(8,128)} %pack.1), calls=%async_computation | async-start | bytes 1048576 | tf_op jit(solution)/shard_map/all_to_all | solution.py:385
  11.7 0.0 copy-done.5
  11.7 0.0 copy-start.6
  11.7 0.7 %copy-done.6 = s32[4,128]{1,0:T(4,128)S(1)} copy-done((s32[4,128]{1,0:T(4,128)S(1)}, s32[4,128]{1,0:T(4,128)}, u32[]{:S(2)}) %copy-start.6) | copy-done | bytes 2072
  12.4 0.0 copy-start.2
  12.4 0.0 copy-start.7
  12.4 0.7 %copy-done.2 = f32[2,4,128]{2,1,0:T(4,128)S(1)} copy-done((f32[2,4,128]{2,1,0:T(4,128)S(1)}, f32[2,4,128]{2,1,0:T(4,128)}, u32[]{:S(2)}) %copy-start.2) | copy-done | bytes 4120
  13.1 0.0 copy-done.7
  13.1 35.9 %all_gather.3.small_ref = f32[192,128]{1,0:T(8,128)S(1)} all-gather(f32[24,128]{1,0:T(8,128)S(1)} %select_maximum_fusion), channel_id=1, replica_groups=mesh['groups'=2,'pts'=4,'comp'=2,'sub'=2] {'pts','comp'}, dimensions={0}, use_global_device_ids=true | all-gather | bytes 110592 | tf_op jit(solution)/shard_map/all_gather | solution.py:370
  49.1 0.1 stack_broadcast_in_dim.5
  49.2 0.1 stack_broadcast_in_dim.4
  49.3 0.0 all-to-all-done.recv_ref
  49.3 10.9 %slab.1 = f32[1536,128]{1,0:T(8,128)} custom-call(f32[8,128,128]{2,1,0:T(8,128)S(1)} %all-to-all-done.recv_ref, f32[192,128]{1,0:T(8,128)S(1)} %all_gather.3.small_ref, f32[2,24,128]{2,1,0:T(8,128)S(1)} %pad_maximum_fusion.trig_ref), custom_call_target="tpu_custom_call" | custom-call | tf_op jit(solution)/shard_map/slab/pallas_call | solution.py:388
  (10 shorter events, 0.1 us)
Async XLA Ops:
  0.0 0.7 %copy-start.3 = (f32[384]{0:T(512)S(1)}, f32[384]{0:T(512)}, u32[]{:S(2)}) copy-start(f32[384]{0:T(512)} %param.12) | copy-start | bytes 4612
  0.7 0.7 %copy-start.4 = (f32[320]{0:T(512)S(1)}, f32[320]{0:T(512)}, u32[]{:S(2)}) copy-start(f32[320]{0:T(512)} %param.10) | copy-start | bytes 3844
  1.4 1.0 %copy-start = (f32[320,384]{1,0:T(8,128)S(1)}, f32[320,384]{1,0:T(8,128)}, u32[]{:S(2)}) copy-start(f32[320,384]{1,0:T(8,128)} %spectra_ref.1) | copy-start | bytes 1474564
  2.4 0.8 %copy-start.1 = (f32[16,4,128]{2,1,0:T(4,128)S(1)}, f32[16,4,128]{2,1,0:T(4,128)}, u32[]{:S(2)}) copy-start(f32[16,4,128]{2,1,0:T(4,128)} %param.15) | copy-start | bytes 98308
  4.3 7.4 %copy-start.5 = (s32[320]{0:T(512)S(1)}, s32[320]{0:T(512)}, u32[]{:S(2)}) copy-start(s32[320]{0:T(512)} %param.13) | copy-start | bytes 3844
  4.3 45.0 %all-to-all-start = ((f32[8,128,128]{2,1,0:T(8,128)}), f32[8,128,128]{2,1,0:T(8,128)S(1)}, u32[]{:S(2)}, u32[]{:S(2)}) async-start(f32[8,128,128]{2,1,0:T(8,128)} %pack.1), calls=%async_computation | async-start | bytes 1048576 | tf_op jit(solution)/shard_map/all_to_all | solution.py:385
  11.7 0.7 %copy-start.6 = (s32[4,128]{1,0:T(4,128)S(1)}, s32[4,128]{1,0:T(4,128)}, u32[]{:S(2)}) copy-start(s32[4,128]{1,0:T(4,128)} %param.14) | copy-start | bytes 6148
  12.4 0.7 %copy-start.2 = (f32[2,4,128]{2,1,0:T(4,128)S(1)}, f32[2,4,128]{2,1,0:T(4,128)}, u32[]{:S(2)}) copy-start(f32[2,4,128]{2,1,0:T(4,128)} %param.16) | copy-start | bytes 12292
  12.4 0.7 %copy-start.7 = (f32[4,128]{1,0:T(4,128)S(1)}, f32[4,128]{1,0:T(4,128)}, u32[]{:S(2)}) copy-start(f32[4,128]{1,0:T(4,128)} %param.17) | copy-start | bytes 6148

commit v2 on v1

--- a/solution.py
+++ b/solution.py
@@ -1,4 +1,5 @@
 import functools
+import math
 import jax
 import jax.numpy as jnp
 from jax import lax
@@ -140,18 +141,33 @@
     return shipped[None]
 
 
-def pack_kernel(parts, spectra_ref, wind_ref, growth_ref, damping_ref, speed_ref, out_ref):
+def pack_kernel(
+    parts,
+    spectra_ref,
+    wind_ref,
+    growth_ref,
+    damping_ref,
+    cell_ref,
+    land_ref,
+    speed_ref,
+    current_ref,
+    turning_ref,
+    out_ref,
+):
     rows, comps = spectra_ref.shape
+    tile_rows = land_ref.shape[0]
     half = LANES // 2
     full = rows // LANES
     width = comps // parts
-    wind_cols = jnp.broadcast_to(wind_ref[...], (LANES, wind_ref.shape[1])).T
+    spare = jnp.zeros((1, half), jnp.float32)
+    wind_row = jnp.concatenate([wind_ref[...][None], spare], axis=1)
+    wind_cols = jnp.broadcast_to(wind_row, (LANES, rows + half)).T
     low = lax.broadcasted_iota(jnp.int32, (8, LANES), 1) < half
     groups = []
     for block in range(comps // LANES):
         lanes = pl.ds(block * LANES, LANES)
-        growth = growth_ref[:, lanes]
-        damping = damping_ref[:, lanes]
+        growth = growth_ref[lanes][None]
+        damping = damping_ref[lanes][None]
 
         def source(first, count):
             span = pl.ds(first, count)
@@ -167,22 +183,31 @@
         tail = source(full * LANES, half)
         turned = jnp.concatenate([tail, tail], axis=0).T
         groups += [turned[g * 8 : g * 8 + 8] for g in range(LANES // 8)]
+    cell_row = jnp.concatenate([cell_ref[...].astype(jnp.float32)[None], spare], axis=1)
+    shared = jnp.concatenate(
+        [current_ref[0], current_ref[1], turning_ref[...], land_ref[...].astype(jnp.float32)]
+        + [cell_row[:, c * LANES : (c + 1) * LANES] for c in range(full + 1)],
+        axis=0,
+    )
+    base = full * width + DIR
     for part in range(parts):
         for g in range(DIR // 8):
             first = groups[part * width // 8 + g]
             second = groups[(part * width + DIR) // 8 + g]
             out_ref[part, pl.ds(full * width + g * 8, 8), :] = jnp.where(low, first, second)
-        out_ref[part, pl.ds(full * width + DIR, 8), :] = speed_ref[pl.ds(part * 8, 8), :]
+        for f in range(2):
+            out_ref[part, pl.ds(base + f * tile_rows, tile_rows), :] = speed_ref[2 * part + f]
+        out_ref[part, pl.ds(base + 2 * tile_rows, shared.shape[0]), :] = shared
 
 
 def slab_kernel(
-    parts, tile_rows, full, recv_ref, small_ref, trig_ref, out_ref, onehot, spread, first, second, table
+    parts, tile_rows, full, recv_ref, out_ref, onehot, spread, first, second, table
 ):
     slab_rows = parts * tile_rows
     freqs = 2
     width = freqs * DIR
     half = LANES // 2
-    small_rows = small_ref.shape[0] // parts
+    base = full * width + DIR
     highs = slab_rows // 2
     depth = onehot.shape[1] // 2
     low_lane = lax.broadcasted_iota(jnp.int32, (1, LANES), 1) < half
@@ -190,7 +215,7 @@
     cell_iota = lax.broadcasted_iota(jnp.int32, (2 * LANES, LANES), 0)
 
     def cells_of(owner, chunk):
-        return small_ref[pl.ds(owner * small_rows + 4 * tile_rows + chunk, 1), :].astype(jnp.int32)
+        return recv_ref[owner, pl.ds(base + 6 * tile_rows + chunk, 1), :].astype(jnp.int32)
 
     def place(chunk_index, cells, values):
         high = cells // (2 * LANES)
@@ -248,7 +273,7 @@
         return jnp.concatenate([read(owner) for owner in range(parts)], axis=0)
 
     def small(kind):
-        return gather(lambda owner: small_ref[pl.ds(owner * small_rows + kind * tile_rows, tile_rows), :])
+        return gather(lambda owner: recv_ref[owner, pl.ds(base + kind * tile_rows, tile_rows), :])
 
     gain = 0.5 * courant / 8.0
     slots = iter(range(table.shape[0]))
@@ -272,13 +297,10 @@
         before = jnp.where(lane > 0, pltpu.roll(rows, 1, 1), 0.0)
         return keep(gain * (rows + after)), keep(gain * (rows + before))
 
-    current_x, current_y, turning, land = (small(kind) for kind in range(4))
+    speeds = [small(f) for f in range(freqs)]
+    current_x, current_y, turning, land = (small(freqs + kind) for kind in range(4))
     current_x_face = face_x(current_x)
     current_y_faces = face_y(current_y)
-    speeds = [
-        gather(lambda owner: recv_ref[owner, pl.ds(full * width + DIR + f * tile_rows, tile_rows), :])
-        for f in range(freqs)
-    ]
     speed_x_face = [face_x(s) for s in speeds]
     speed_y_faces = [face_y(s) for s in speeds]
     land_slot = keep(land)
@@ -295,8 +317,9 @@
         )
     ]
 
-    cosine = trig_ref[0]
-    sine = trig_ref[1]
+    angles = lax.broadcasted_iota(jnp.int32, (DIR, LANES), 0).astype(jnp.float32) * (2.0 * math.pi / DIR)
+    cosine = jnp.cos(angles)
+    sine = jnp.sin(angles)
     lane_wide = lax.broadcasted_iota(jnp.int32, (DIR, LANES), 1)
 
     def row(slot, x):
@@ -361,29 +384,16 @@
     width = comps // parts
     full = rows // LANES
     slab_rows = parts * tile_rows
-    spare = -(-rows // LANES) * LANES - rows
-    cells = jnp.pad(row_cell.astype(jnp.float32), (0, spare)).reshape(-1, LANES)
-    small = jnp.concatenate(
-        [current.reshape(-1, LANES), turning, land_mask.astype(jnp.float32), cells], axis=0
-    )
-    small = jnp.pad(small, ((0, -small.shape[0] % 8), (0, 0)))
-    small_all = lax.all_gather(small, GROUP, axis=0, tiled=True)
-    block_rows = full * width + DIR + 2 * tile_rows
-    vmem = pltpu.CompilerParams(vmem_limit_bytes=48 * 1024 * 1024)
+    shared_rows = 6 * tile_rows + full + 1
+    block_rows = -(-(full * width + DIR + shared_rows) // 8) * 8
+    vmem = pltpu.CompilerParams(vmem_limit_bytes=56 * 1024 * 1024)
     packed = pl.pallas_call(
         functools.partial(pack_kernel, parts),
         out_shape=jax.ShapeDtypeStruct((parts, block_rows, LANES), jnp.float32),
         compiler_params=vmem,
         name="pack",
-    )(
-        spectra,
-        jnp.pad(wind, (0, spare))[None],
-        growth[None],
-        damping[None],
-        group_speed.reshape(-1, LANES),
-    )
+    )(spectra, wind, growth, damping, row_cell, land_mask, group_speed, current, turning)
     recv = lax.all_to_all(packed, GROUP, split_axis=0, concat_axis=0, tiled=True)
-    trig = jnp.stack([jnp.broadcast_to(t[:, None], (DIR, LANES)) for t in direction_tables(DIR)])
     depth = parts * rows
     out = pl.pallas_call(
         functools.partial(slab_kernel, parts, tile_rows, full),
@@ -397,7 +407,7 @@
         ],
         compiler_params=vmem,
         name="slab",
-    )(recv, small_all, trig)
+    )(recv)
     return out.reshape(1, width, slab_rows, LANES)
 
 

time: 60.6 us -> 38.9 us (0.64)
  blocking collectives: 35.9 us -> 24.5 us
  starting transfers between devices: 7.38 us -> 0 us
  local copies, waits for them, and re-layouts: 4.67 us -> 0 us
  Pallas kernels: 12 us -> 14.2 us
    all_gather x1 -> x0, blocking collectives: 35.9 us -> none  [slab_plan(): small_all = lax.all_gather(small, GROUP, axis=0, tiled=True)]
    all_to_all x0 -> x1, blocking collectives: none -> 24.5 us  [slab_plan(): lax.all_to_all(packed, GROUP, split_axis=0, concat_axis=0, tiled=True)]
    all_to_all x1 -> x0, starting transfers between devices: 7.38 us -> none  [slab_plan(): lax.all_to_all(packed, GROUP, split_axis=0, concat_axis=0, tiled=True)]
    unnamed x16 -> x0, local copies, waits for them, and re-layouts: 3.82 us -> none
    pallas_call x1, Pallas kernels: 1.11 us -> 2.24 us  [slab_plan(): pl.pallas_call(functools.partial(pack_kernel, parts), out_shape=jax.Shape...]
    pallas_call x1, Pallas kernels: 10.9 us -> 11.9 us  [slab_plan(): pl.pallas_call(functools.partial(slab_kernel, parts, tile_rows, full), ou...]
    broadcast_in_dim x3 -> x0, local copies, waits for them, and re-layouts: 0.7 us -> none  [the longest x1 0.7 us: slab_plan(): growth[None]]
  transfers between devices with their start and end apart: 1 -> 0, of which waited for: 0 -> 0; matrix products, arithmetic and copies ran while one was open for 0% -> 0% of each run, Pallas kernels for 0% -> 0%
where the time goes in v2:
time: 38.9 us; the launch traced here: 38.7 us
  blocking collectives  24.5 us (63%)
  Pallas kernels  14.2 us (37%)
    all_to_all x1, blocking collectives, slab_plan(): lax.all_to_all(packed, GROUP, split_axis=0, concat_axis=0, tiled=True)  24.5 us
    pallas_call x1, Pallas kernels, slab_plan(): pl.pallas_call(functools.partial(slab_kernel, parts, tile_rows, full), ou...  11.9 us
    pallas_call x1, Pallas kernels, slab_plan(): pl.pallas_call(functools.partial(pack_kernel, parts), out_shape=jax.Shape...  2.24 us

profile of v2, /device:TPU:0, one launch (start us, length us, event | category | flops | bytes accessed | tf_op | source)
XLA Modules:
  0.0 38.7 jit_solution(468935693507584475)
XLA Ops:
  0.0 2.2 %pack.1 = f32[8,152,128]{2,1,0:T(8,128)} custom-call(f32[320,384]{1,0:T(8,128)} %spectra_ref.1, f32[320]{0:T(512)} %wind_ref.1, f32[384]{0:T(512)} %growth_ref.1, f32[384]{0:T(512)} %damping_ref.1, s32[320]{0:T(512)} %cell_ref.1, s32[4,128]{1,0:T(4,128)} %land_ref.1, f32[16,4,128]{2,1,0:T(4,128)} %speed_ref.1, f32[2,4,128]{2,1,0:T(4,128)} %current_ref.1, ...), custom_call_target="tpu_custom_call" | custom-call | tf_op jit(solution)/shard_map/pack/pallas_call | solution.py:390
  2.2 24.5 %all_to_all.5.recv_ref = f32[8,152,128]{2,1,0:T(8,128)} all-to-all(f32[8,152,128]{2,1,0:T(8,128)} %pack.1), channel_id=1, replica_groups=mesh['groups'=2,'pts'=4,'comp'=2,'sub'=2] {'pts','comp'}, dimensions={0} | all-to-all | bytes 1245184 | tf_op jit(solution)/shard_map/all_to_all | solution.py:396
  26.7 11.9 %slab.1 = f32[1536,128]{1,0:T(8,128)} custom-call(f32[8,152,128]{2,1,0:T(8,128)} %all_to_all.5.recv_ref), custom_call_target="tpu_custom_call" | custom-call | tf_op jit(solution)/shard_map/slab/pallas_call | solution.py:398

commit v3 on v2

--- a/solution.py
+++ b/solution.py
@@ -152,18 +152,18 @@
     speed_ref,
     current_ref,
     turning_ref,
-    out_ref,
+    *out_refs,
 ):
     rows, comps = spectra_ref.shape
     tile_rows = land_ref.shape[0]
     half = LANES // 2
     full = rows // LANES
-    width = comps // parts
     spare = jnp.zeros((1, half), jnp.float32)
     wind_row = jnp.concatenate([wind_ref[...][None], spare], axis=1)
     wind_cols = jnp.broadcast_to(wind_row, (LANES, rows + half)).T
     low = lax.broadcasted_iota(jnp.int32, (8, LANES), 1) < half
-    groups = []
+    per_freq = DIR // 8
+    tails = []
     for block in range(comps // LANES):
         lanes = pl.ds(block * LANES, LANES)
         growth = growth_ref[lanes][None]
@@ -178,78 +178,79 @@
         for chunk in range(full):
             turned = source(chunk * LANES, LANES).T
             for g in range(LANES // 8):
-                part, within = divmod(block * LANES + g * 8, width)
-                out_ref[part, pl.ds(chunk * width + within, 8), :] = turned[g * 8 : g * 8 + 8]
+                freq, within = divmod(block * (LANES // 8) + g, per_freq)
+                part, f = divmod(freq, len(out_refs))
+                out_refs[f][part, pl.ds(chunk * DIR + within * 8, 8), :] = turned[g * 8 : g * 8 + 8]
         tail = source(full * LANES, half)
         turned = jnp.concatenate([tail, tail], axis=0).T
-        groups += [turned[g * 8 : g * 8 + 8] for g in range(LANES // 8)]
+        tails += [turned[g * 8 : g * 8 + 8] for g in range(LANES // 8)]
     cell_row = jnp.concatenate([cell_ref[...].astype(jnp.float32)[None], spare], axis=1)
     shared = jnp.concatenate(
         [current_ref[0], current_ref[1], turning_ref[...], land_ref[...].astype(jnp.float32)]
         + [cell_row[:, c * LANES : (c + 1) * LANES] for c in range(full + 1)],
         axis=0,
     )
-    base = full * width + DIR
+    base = full * DIR
     for part in range(parts):
-        for g in range(DIR // 8):
-            first = groups[part * width // 8 + g]
-            second = groups[(part * width + DIR) // 8 + g]
-            out_ref[part, pl.ds(full * width + g * 8, 8), :] = jnp.where(low, first, second)
-        for f in range(2):
-            out_ref[part, pl.ds(base + f * tile_rows, tile_rows), :] = speed_ref[2 * part + f]
-        out_ref[part, pl.ds(base + 2 * tile_rows, shared.shape[0]), :] = shared
-
-
-def slab_kernel(
-    parts, tile_rows, full, recv_ref, out_ref, onehot, spread, first, second, table
-):
+        for f, out_ref in enumerate(out_refs):
+            freq = part * len(out_refs) + f
+            one, two, three = tails[freq * per_freq : (freq + 1) * per_freq]
+            out_ref[part, pl.ds(base, 8), :] = jnp.where(low, one, two)
+            folded = jnp.where(low, three, pltpu.roll(three, 4, 0))
+            out_ref[part, pl.ds(base + 8, 8), :] = jnp.concatenate([folded[:4], speed_ref[freq]], axis=0)
+        out_refs[0][part, pl.ds(base + 16, shared.shape[0]), :] = shared
+
+
+UNROLL = 8
+
+
+def slab_kernel(parts, tile_rows, full, *refs):
+    recv_ref, shared_ref, out_ref = refs[0], refs[-9], refs[-8]
+    onehot, spread, first, second, table, faces_x, faces_r = refs[-7:]
     slab_rows = parts * tile_rows
-    freqs = 2
-    width = freqs * DIR
     half = LANES // 2
-    base = full * width + DIR
+    base = full * DIR
+    shared_base = base + 16
     highs = slab_rows // 2
-    depth = onehot.shape[1] // 2
     low_lane = lax.broadcasted_iota(jnp.int32, (1, LANES), 1) < half
-    low_lane_wide = lax.broadcasted_iota(jnp.int32, (DIR, LANES), 1) < half
-    cell_iota = lax.broadcasted_iota(jnp.int32, (2 * LANES, LANES), 0)
+    low_lanes = lax.broadcasted_iota(jnp.int32, (8, LANES), 1) < half
+    top_rows = lax.broadcasted_iota(jnp.int32, (8, LANES), 0) < 4
+    cell_iota = lax.broadcasted_iota(jnp.int32, (2 * LANES, LANES), 0).astype(jnp.float32).astype(jnp.bfloat16)
 
     def cells_of(owner, chunk):
-        return recv_ref[owner, pl.ds(base + 6 * tile_rows + chunk, 1), :].astype(jnp.int32)
-
-    def place(chunk_index, cells, values):
+        return shared_ref[owner, pl.ds(shared_base + 4 * tile_rows + chunk, 1), :].astype(jnp.int32)
+
+    def place(index, cells, values):
+        span = pl.ds(index * LANES, LANES)
         high = cells // (2 * LANES)
-        low = cells - high * (2 * LANES)
-        hot = (cell_iota == low).astype(jnp.float32).astype(jnp.bfloat16)
-        onehot[:, pl.ds(chunk_index * LANES, LANES)] = hot
-        onehot[:, pl.ds(depth + chunk_index * LANES, LANES)] = hot
-        head = values.astype(jnp.bfloat16)
-        rest = (values - head.astype(jnp.float32)).astype(jnp.bfloat16)
+        low = (cells - high * (2 * LANES)).astype(jnp.float32)
+        low = jnp.broadcast_to(low, (2 * LANES, LANES)).astype(jnp.bfloat16)
+        onehot[:, span] = jnp.where(cell_iota == low, 1.0, 0.0).astype(jnp.bfloat16)
+        head = values.astype(jnp.bfloat16).astype(jnp.float32)
+        both = jnp.concatenate([head, values - head], axis=0).astype(jnp.bfloat16)
         for h in range(highs):
-            pick = jnp.broadcast_to((high == h).astype(jnp.float32), (width, LANES)).astype(jnp.bfloat16)
-            spread[pl.ds(h * width, width), pl.ds(chunk_index * LANES, LANES)] = head * pick
-            spread[pl.ds(h * width, width), pl.ds(depth + chunk_index * LANES, LANES)] = rest * pick
+            pick = jnp.broadcast_to((high == h).astype(jnp.float32), (2 * DIR, LANES)).astype(jnp.bfloat16)
+            spread[pl.ds(h * 2 * DIR, 2 * DIR), span] = both * pick
 
     per_pair = 2 * full + 1
     for pair in range(parts // 2):
         even, odd = 2 * pair, 2 * pair + 1
         for side, owner in enumerate((even, odd)):
             for chunk in range(full):
-                values = recv_ref[owner, pl.ds(chunk * width, width), :]
+                values = recv_ref[owner, pl.ds(chunk * DIR, DIR), :]
                 place(pair * per_pair + side * full + chunk, cells_of(owner, chunk), values)
-        tail_even = recv_ref[even, pl.ds(full * width, DIR), :]
-        tail_odd = recv_ref[odd, pl.ds(full * width, DIR), :]
-        swapped_even = pltpu.roll(tail_even, half, 1)
-        swapped_odd = pltpu.roll(tail_odd, half, 1)
-        values = jnp.concatenate(
-            [
-                jnp.where(low_lane_wide, tail_even, swapped_odd),
-                jnp.where(low_lane_wide, swapped_even, tail_odd),
-            ],
-            axis=0,
-        )
-        cells_even, cells_odd = cells_of(even, full), cells_of(odd, full)
-        cells = jnp.where(low_lane, cells_even, pltpu.roll(cells_odd, half, 1))
+
+        def merged(offset):
+            own, other = recv_ref[even, pl.ds(offset, 8), :], recv_ref[odd, pl.ds(offset, 8), :]
+            return (
+                jnp.where(low_lanes, own, pltpu.roll(other, half, 1)),
+                jnp.where(low_lanes, pltpu.roll(own, half, 1), other),
+            )
+
+        one, two = merged(base)
+        three, four = merged(base + 8)
+        values = jnp.concatenate([one, two, jnp.where(top_rows, three, pltpu.roll(four, 4, 0))], axis=0)
+        cells = jnp.where(low_lane, cells_of(even, full), pltpu.roll(cells_of(odd, full), half, 1))
         place(pair * per_pair + 2 * full, cells, values)
 
     scattered = lax.dot_general(
@@ -257,23 +258,19 @@
     )
     nothing = jnp.zeros((DIR, LANES), jnp.float32)
     for field in (first, second):
-        for f in range(freqs):
-            for edge in (0, 1, slab_rows + 2, slab_rows + 3):
-                field[f, edge] = nothing
+        for edge in (0, 1, slab_rows + 2, slab_rows + 3):
+            field[edge] = nothing
     for h in range(highs):
-        for f in range(freqs):
-            span = scattered[h * width + f * DIR : h * width + (f + 1) * DIR]
-            first[f, 2 * h + 2] = span[:, :LANES]
-            first[f, 2 * h + 3] = span[:, LANES:]
+        at = h * 2 * DIR
+        total = scattered[at : at + DIR] + scattered[at + DIR : at + 2 * DIR]
+        first[2 * h + 2] = total[:, :LANES]
+        first[2 * h + 3] = total[:, LANES:]
 
     lane = lax.broadcasted_iota(jnp.int32, (slab_rows, LANES), 1)
     zero_rows = jnp.zeros((8, LANES), jnp.float32)
 
-    def gather(read):
-        return jnp.concatenate([read(owner) for owner in range(parts)], axis=0)
-
-    def small(kind):
-        return gather(lambda owner: recv_ref[owner, pl.ds(base + kind * tile_rows, tile_rows), :])
+    def gather(ref, offset):
+        return jnp.concatenate([ref[owner, pl.ds(offset, tile_rows), :] for owner in range(parts)], axis=0)
 
     gain = 0.5 * courant / 8.0
     slots = iter(range(table.shape[0]))
@@ -297,12 +294,12 @@
         before = jnp.where(lane > 0, pltpu.roll(rows, 1, 1), 0.0)
         return keep(gain * (rows + after)), keep(gain * (rows + before))
 
-    speeds = [small(f) for f in range(freqs)]
-    current_x, current_y, turning, land = (small(freqs + kind) for kind in range(4))
-    current_x_face = face_x(current_x)
-    current_y_faces = face_y(current_y)
-    speed_x_face = [face_x(s) for s in speeds]
-    speed_y_faces = [face_y(s) for s in speeds]
+    speed = gather(recv_ref, base + 12)
+    current_x, current_y, turning, land = (
+        gather(shared_ref, shared_base + kind * tile_rows) for kind in range(4)
+    )
+    current_x_face, speed_x_face = face_x(current_x), face_x(speed)
+    current_y_faces, speed_y_faces = face_y(current_y), face_y(speed)
     land_slot = keep(land)
     ahead = jnp.maximum(turning, 0.0) * 0.125
     back = jnp.minimum(turning, 0.0) * 0.125
@@ -325,90 +322,113 @@
     def row(slot, x):
         return table[slot, pl.ds(8 + x, 1), :]
 
-    def flux(speed, behind, centre, onward, beyond):
-        shared = 3.0 * (centre + onward)
-        return jnp.maximum(speed, 0.0) * (shared + 3.0 * centre - behind) + jnp.minimum(speed, 0.0) * (
-            shared + 3.0 * onward - beyond
-        )
-
-    def flux_x(field, f, x):
-        speed = row(speed_x_face[f], x) * cosine + row(current_x_face, x)
-        return flux(speed, field[f, x + 1], field[f, x + 2], field[f, x + 3], field[f, x + 4])
-
-    def advance(field, f, x, entering):
-        leaving = flux_x(field, f, x)
-        centre = field[f, x + 2]
-        up1 = jnp.where(lane_wide < LANES - 1, pltpu.roll(centre, LANES - 1, 1), 0.0)
-        up2 = jnp.where(lane_wide < LANES - 2, pltpu.roll(centre, LANES - 2, 1), 0.0)
-        down1 = jnp.where(lane_wide > 0, pltpu.roll(centre, 1, 1), 0.0)
-        down2 = jnp.where(lane_wide > 1, pltpu.roll(centre, 2, 1), 0.0)
-        right = flux(
-            row(speed_y_faces[f][0], x) * sine + row(current_y_faces[0], x), down1, centre, up1, up2
-        )
-        left = flux(
-            row(speed_y_faces[f][1], x) * sine + row(current_y_faces[1], x), down2, down1, centre, up1
-        )
-        moved = (centre - (leaving - entering) - (right - left)) * row(land_slot, x)
-        return moved, leaving
-
-    def sweep(field, finish):
-        def body(x, carry):
-            out = []
-            for f in range(freqs):
-                moved, leaving = advance(field, f, x, carry[f])
-                finish(f, x, moved)
-                out.append(leaving)
-            return tuple(out)
-
-        lax.fori_loop(0, slab_rows, body, tuple(flux_x(field, f, -1) for f in range(freqs)))
-
-    def store(f, x, moved):
-        second[f, x + 2] = moved
-
-    def refract(f, x, moved):
+    def flux(speeds, behind, centre, centre3, onward3, beyond):
+        both = centre3 + onward3
+        return speeds[0] * (both + centre3 - behind) + speeds[1] * (both + onward3 - beyond)
+
+    def split(speed):
+        return jnp.maximum(speed, 0.0), jnp.minimum(speed, 0.0)
+
+    def flux_x(field, x, speeds, centre3, onward3):
+        return flux(speeds, field[x + 1], None, centre3, onward3, field[x + 4])
+
+    def sweep(field, fresh, finish):
+        def speeds_x(x):
+            if fresh:
+                speeds = split(row(speed_x_face, x) * cosine + row(current_x_face, x))
+                faces_x[0, x + 1], faces_x[1, x + 1] = speeds
+                return speeds
+            return faces_x[0, x + 1], faces_x[1, x + 1]
+
+        def speeds_y(side, x):
+            if fresh:
+                speeds = split(row(speed_y_faces[side], x) * sine + row(current_y_faces[side], x))
+                faces_r[2 * side, x], faces_r[2 * side + 1, x] = speeds
+                return speeds
+            return faces_r[2 * side, x], faces_r[2 * side + 1, x]
+
+        def body(step, carry):
+            entering, centre3 = carry
+            for i in range(UNROLL):
+                x = step * UNROLL + i
+                centre = field[x + 2]
+                onward3 = 3.0 * field[x + 3]
+                leaving = flux_x(field, x, speeds_x(x), centre3, onward3)
+                up1 = jnp.where(lane_wide < LANES - 1, pltpu.roll(centre, LANES - 1, 1), 0.0)
+                up2 = jnp.where(lane_wide < LANES - 2, pltpu.roll(centre, LANES - 2, 1), 0.0)
+                down1 = jnp.where(lane_wide > 0, pltpu.roll(centre, 1, 1), 0.0)
+                down2 = jnp.where(lane_wide > 1, pltpu.roll(centre, 2, 1), 0.0)
+                right = flux(speeds_y(0, x), down1, centre, centre3, 3.0 * up1, up2)
+                left = flux(speeds_y(1, x), down2, down1, 3.0 * down1, centre3, up1)
+                finish(x, (centre - (leaving - entering) - (right - left)) * row(land_slot, x))
+                entering, centre3 = leaving, onward3
+            return entering, centre3
+
+        start3 = 3.0 * field[2]
+        entering = flux_x(field, -1, speeds_x(-1), nothing, start3)
+        lax.fori_loop(0, slab_rows // UNROLL, body, (entering, start3))
+
+    def store(x, moved):
+        second[x + 2] = moved
+
+    def refract(x, moved):
         bent = row(bend_slots[2], x) * moved
         for slot, shift in zip(bend_slots, (2, 1, 0, DIR - 1, DIR - 2)):
             if shift:
                 bent = bent + row(slot, x) * jnp.roll(moved, shift, axis=0)
         for g in range(DIR // 8):
-            out_ref[pl.ds((f * DIR + g * 8) * slab_rows + x, 8, stride=slab_rows), :] = bent[g * 8 : g * 8 + 8]
-
-    sweep(first, store)
-    sweep(second, refract)
+            out_ref[pl.ds(g * 8 * slab_rows + x, 8, stride=slab_rows), :] = bent[g * 8 : g * 8 + 8]
+
+    sweep(first, True, store)
+    sweep(second, False, refract)
 
 
 def slab_plan(spectra, wind, growth, damping, row_cell, land_mask, group_speed, current, turning):
     parts = lax.axis_size(GROUP)
     rows, comps = spectra.shape
     tile_rows = land_mask.shape[0]
-    width = comps // parts
+    freqs = comps // parts // DIR
     full = rows // LANES
     slab_rows = parts * tile_rows
-    shared_rows = 6 * tile_rows + full + 1
-    block_rows = -(-(full * width + DIR + shared_rows) // 8) * 8
-    vmem = pltpu.CompilerParams(vmem_limit_bytes=56 * 1024 * 1024)
+    depth = parts * rows
+    block_rows = full * DIR + 16
+    shared_rows = -(-(4 * tile_rows + full + 1) // 8) * 8
+    blocks = [block_rows + shared_rows * (f == 0) for f in range(freqs)]
+    params = pltpu.CompilerParams(vmem_limit_bytes=56 * 1024 * 1024)
     packed = pl.pallas_call(
         functools.partial(pack_kernel, parts),
-        out_shape=jax.ShapeDtypeStruct((parts, block_rows, LANES), jnp.float32),
-        compiler_params=vmem,
+        out_shape=[jax.ShapeDtypeStruct((parts, block, LANES), jnp.float32) for block in blocks],
+        compiler_params=params,
         name="pack",
     )(spectra, wind, growth, damping, row_cell, land_mask, group_speed, current, turning)
-    recv = lax.all_to_all(packed, GROUP, split_axis=0, concat_axis=0, tiled=True)
-    depth = parts * rows
-    out = pl.pallas_call(
-        functools.partial(slab_kernel, parts, tile_rows, full),
-        out_shape=jax.ShapeDtypeStruct((width * slab_rows, LANES), jnp.float32),
-        scratch_shapes=[
-            pltpu.VMEM((2 * LANES, 2 * depth), jnp.bfloat16),
-            pltpu.VMEM((slab_rows // 2 * width, 2 * depth), jnp.bfloat16),
-            pltpu.VMEM((2, slab_rows + 4, DIR, LANES), jnp.float32),
-            pltpu.VMEM((2, slab_rows + 4, DIR, LANES), jnp.float32),
-            pltpu.VMEM((15, slab_rows + 16, LANES), jnp.float32),
-        ],
-        compiler_params=vmem,
-        name="slab",
-    )(recv)
-    return out.reshape(1, width, slab_rows, LANES)
+    arrived = [lax.all_to_all(p, GROUP, split_axis=0, concat_axis=0, tiled=True) for p in packed]
+    whole = pl.BlockSpec(memory_space=pltpu.VMEM)
+    field = None
+    for f in range(freqs):
+        operands = [arrived[f]] if f == 0 else [arrived[f], field, arrived[0]]
+        field = pl.pallas_call(
+            functools.partial(slab_kernel, parts, tile_rows, full),
+            grid=(1,),
+            out_shape=jax.ShapeDtypeStruct((freqs * DIR * slab_rows, LANES), jnp.float32),
+            in_specs=[whole] if f == 0 else [whole, pl.BlockSpec(memory_space=pl.ANY), whole],
+            out_specs=pl.BlockSpec((DIR * slab_rows, LANES), functools.partial(lambda f, i: (f, 0), f)),
+            scratch_shapes=[
+                pltpu.VMEM((2 * LANES, depth), jnp.bfloat16),
+                pltpu.VMEM((slab_rows * DIR, depth), jnp.bfloat16),
+                pltpu.VMEM((slab_rows + 4, DIR, LANES), jnp.float32),
+                pltpu.VMEM((slab_rows + 4, DIR, LANES), jnp.float32),
+                pltpu.VMEM((12, slab_rows + 16, LANES), jnp.float32),
+                pltpu.VMEM((2, slab_rows + 1, DIR, LANES), jnp.float32),
+                pltpu.VMEM((4, slab_rows, DIR, LANES), jnp.float32),
+            ],
+            input_output_aliases={} if f == 0 else {1: 0},
+            cost_estimate=pl.CostEstimate(
+                flops=100 * slab_rows * DIR * LANES * 10, bytes_accessed=1 << 20, transcendentals=0
+            ),
+            compiler_params=params,
+            name="slab",
+        )(*operands)
+    return field.reshape(1, freqs * DIR, slab_rows, LANES)
 
 
 def shards(*arrays):

time: 38.9 us -> 39.9 us (1.026)
  blocking collectives: 24.5 us -> 18.9 us
  starting transfers between devices: 0 us -> 3.41 us
  waiting for transfers between devices: 0 us -> 2.65 us
  local copies, waits for them, and re-layouts: 0 us -> 0.7 us
    all_to_all x1, blocking collectives: 24.5 us -> 18.9 us  [slab_plan(): lax.all_to_all(p, GROUP, split_axis=0, concat_axis=0, tiled=True)]
    all_to_all x0 -> x1, starting transfers between devices: none -> 3.41 us  [slab_plan(): lax.all_to_all(p, GROUP, split_axis=0, concat_axis=0, tiled=True)]
    all_to_all x0 -> x1, waiting for transfers between devices: none -> 2.65 us  [slab_plan(): lax.all_to_all(p, GROUP, split_axis=0, concat_axis=0, tiled=True)]
    unnamed x0 -> x2, local copies, waits for them, and re-layouts: none -> 0.7 us
    pallas_call x2 -> x3, Pallas kernels: 14.2 us -> 13.9 us  [the longest x2 11.7 us: slab_plan(): pl.pallas_call(functools.partial(slab_kernel, parts, tile_rows, full), gr...]
  transfers between devices with their start and end apart: 0 -> 1, of which waited for: 0 -> 1; matrix products, arithmetic and copies ran while one was open for 0% -> 0% of each run, Pallas kernels for 0% -> 15%
where the time goes in v3:
time: 39.9 us; the launch traced here: 39.5 us
  blocking collectives  18.9 us (47%)
  Pallas kernels  13.9 us (35%)
  starting transfers between devices  3.41 us (9%)
  waiting for transfers between devices  2.65 us (7%)
  local copies, waits for them, and re-layouts  0.7 us (2%)
    all_to_all x1, blocking collectives, slab_plan(): lax.all_to_all(p, GROUP, split_axis=0, concat_axis=0, tiled=True)  18.9 us
    pallas_call x2, Pallas kernels, slab_plan(): pl.pallas_call(functools.partial(slab_kernel, parts, tile_rows, full), gr...  11.7 us
    all_to_all x1, starting transfers between devices, slab_plan(): lax.all_to_all(p, GROUP, split_axis=0, concat_axis=0, tiled=True)  3.41 us
    all_to_all x1, waiting for transfers between devices, slab_plan(): lax.all_to_all(p, GROUP, split_axis=0, concat_axis=0, tiled=True)  2.65 us
    pallas_call x1, Pallas kernels, slab_plan(): pl.pallas_call(functools.partial(pack_kernel, parts), out_shape=[jax.Shap...  2.23 us
  transfers between devices with their start and end apart: 1, of which 1 were waited for; matrix products, arithmetic and copies ran while one was open for 0% of the time, Pallas kernels for 15%

profile of v3, /device:TPU:0, one launch (start us, length us, event | category | flops | bytes accessed | tf_op | source)
XLA Modules:
  0.0 39.5 jit_solution(10755329473876915768)
XLA Ops:
  0.0 2.2 %pack.1 = (f32[8,88,128]{2,1,0:T(8,128)}, f32[8,64,128]{2,1,0:T(8,128)}) custom-call(f32[320,384]{1,0:T(8,128)} %spectra_ref.1, f32[320]{0:T(512)} %wind_ref.1, f32[384]{0:T(512)} %growth_ref.1, f32[384]{0:T(512)} %damping_ref.1, s32[320]{0:T(512)} %cell_ref.1, s32[4,128]{1,0:T(4,128)} %land_ref.1, f32[16,4,128]{2,1,0:T(4,128)} %speed_ref.1, ...), custom_call_target="tpu_custom_call" | custom-call | tf_op jit(solution)/shard_map/pack/pallas_call | solution.py:398
  2.2 18.9 %all_to_all.10.refs_0_.refs_2_ = f32[8,88,128]{2,1,0:T(8,128)} all-to-all(f32[8,88,128]{2,1,0:T(8,128)} %get-tuple-element.8), channel_id=1, replica_groups=mesh['groups'=2,'pts'=4,'comp'=2,'sub'=2] {'pts','comp'}, dimensions={0} | all-to-all | bytes 720896 | tf_op jit(solution)/shard_map/all_to_all | solution.py:404
  21.1 3.4 %all-to-all-start = ((f32[8,64,128]{2,1,0:T(8,128)}), f32[8,64,128]{2,1,0:T(8,128)S(1)}, u32[]{:S(2)}, u32[]{:S(2)}) async-start(f32[8,64,128]{2,1,0:T(8,128)} %get-tuple-element.7), calls=%async_computation | async-start | bytes 524288 | tf_op jit(solution)/shard_map/all_to_all | solution.py:404
  24.5 5.8 %slab.2.refs_1_ = f32[1536,128]{1,0:T(8,128)} custom-call(f32[8,88,128]{2,1,0:T(8,128)} %all_to_all.10.refs_0_.refs_2_), custom_call_target="tpu_custom_call" | custom-call | flops 98304000 | bytes 1048576 | tf_op jit(solution)/shard_map/slab/pallas_call | solution.py:409
  30.3 2.6 %all-to-all-done.refs_0_ = f32[8,64,128]{2,1,0:T(8,128)S(1)} async-done(((f32[8,64,128]{2,1,0:T(8,128)}), f32[8,64,128]{2,1,0:T(8,128)S(1)}, u32[]{:S(2)}, u32[]{:S(2)}) %all-to-all-start) | async-done | bytes 262176 | tf_op jit(solution)/shard_map/all_to_all | solution.py:404
  33.0 0.0 copy-start
  33.0 0.7 %copy-done = f32[8,64,128]{2,1,0:T(8,128)} copy-done((f32[8,64,128]{2,1,0:T(8,128)}, f32[8,64,128]{2,1,0:T(8,128)S(1)}, u32[]{:S(2)}) %copy-start) | copy-done | bytes 262168
  33.7 5.9 %slab.3 = f32[1536,128]{1,0:T(8,128)} custom-call(f32[8,64,128]{2,1,0:T(8,128)} %copy-done, f32[1536,128]{1,0:T(8,128)} %slab.2.refs_1_, f32[8,88,128]{2,1,0:T(8,128)} %all_to_all.10.refs_0_.refs_2_), custom_call_target="tpu_custom_call", output_to_operand_aliasing={{}: (1, {})} | custom-call | flops 98304000 | bytes 1048576 | tf_op jit(solution)/shard_map/slab/pallas_call | solution.py:409
Async XLA Ops:
  21.1 11.9 %all-to-all-start = ((f32[8,64,128]{2,1,0:T(8,128)}), f32[8,64,128]{2,1,0:T(8,128)S(1)}, u32[]{:S(2)}, u32[]{:S(2)}) async-start(f32[8,64,128]{2,1,0:T(8,128)} %get-tuple-element.7), calls=%async_computation | async-start | bytes 524288 | tf_op jit(solution)/shard_map/all_to_all | solution.py:404
  33.0 0.7 %copy-start = (f32[8,64,128]{2,1,0:T(8,128)}, f32[8,64,128]{2,1,0:T(8,128)S(1)}, u32[]{:S(2)}) copy-start(f32[8,64,128]{2,1,0:T(8,128)S(1)} %all-to-all-done.refs_0_) | copy-start | bytes 786436

commit v4 on v3

--- a/solution.py
+++ b/solution.py
@@ -143,19 +143,18 @@
 
 def pack_kernel(
     parts,
+    freqs,
     spectra_ref,
     wind_ref,
     growth_ref,
     damping_ref,
     cell_ref,
-    land_ref,
     speed_ref,
     current_ref,
     turning_ref,
-    *out_refs,
+    out_ref,
 ):
     rows, comps = spectra_ref.shape
-    tile_rows = land_ref.shape[0]
     half = LANES // 2
     full = rows // LANES
     spare = jnp.zeros((1, half), jnp.float32)
@@ -163,6 +162,7 @@
     wind_cols = jnp.broadcast_to(wind_row, (LANES, rows + half)).T
     low = lax.broadcasted_iota(jnp.int32, (8, LANES), 1) < half
     per_freq = DIR // 8
+    span_rows = full * DIR + 16
     tails = []
     for block in range(comps // LANES):
         lanes = pl.ds(block * LANES, LANES)
@@ -179,46 +179,64 @@
             turned = source(chunk * LANES, LANES).T
             for g in range(LANES // 8):
                 freq, within = divmod(block * (LANES // 8) + g, per_freq)
-                part, f = divmod(freq, len(out_refs))
-                out_refs[f][part, pl.ds(chunk * DIR + within * 8, 8), :] = turned[g * 8 : g * 8 + 8]
+                part, f = divmod(freq, freqs)
+                at = f * span_rows + chunk * DIR + within * 8
+                out_ref[part, pl.ds(at, 8), :] = turned[g * 8 : g * 8 + 8]
         tail = source(full * LANES, half)
         turned = jnp.concatenate([tail, tail], axis=0).T
         tails += [turned[g * 8 : g * 8 + 8] for g in range(LANES // 8)]
     cell_row = jnp.concatenate([cell_ref[...].astype(jnp.float32)[None], spare], axis=1)
     shared = jnp.concatenate(
-        [current_ref[0], current_ref[1], turning_ref[...], land_ref[...].astype(jnp.float32)]
+        [current_ref[0], current_ref[1], turning_ref[...]]
         + [cell_row[:, c * LANES : (c + 1) * LANES] for c in range(full + 1)],
         axis=0,
     )
-    base = full * DIR
     for part in range(parts):
-        for f, out_ref in enumerate(out_refs):
-            freq = part * len(out_refs) + f
+        for f in range(freqs):
+            freq = part * freqs + f
             one, two, three = tails[freq * per_freq : (freq + 1) * per_freq]
-            out_ref[part, pl.ds(base, 8), :] = jnp.where(low, one, two)
+            at = f * span_rows + full * DIR
+            out_ref[part, pl.ds(at, 8), :] = jnp.where(low, one, two)
             folded = jnp.where(low, three, pltpu.roll(three, 4, 0))
-            out_ref[part, pl.ds(base + 8, 8), :] = jnp.concatenate([folded[:4], speed_ref[freq]], axis=0)
-        out_refs[0][part, pl.ds(base + 16, shared.shape[0]), :] = shared
-
-
-UNROLL = 8
-
-
-def slab_kernel(parts, tile_rows, full, *refs):
-    recv_ref, shared_ref, out_ref = refs[0], refs[-9], refs[-8]
-    onehot, spread, first, second, table, faces_x, faces_r = refs[-7:]
+            out_ref[part, pl.ds(at + 8, 8), :] = jnp.concatenate([folded[:4], speed_ref[freq]], axis=0)
+        out_ref[part, pl.ds(freqs * span_rows, shared.shape[0]), :] = shared
+
+
+BLOCK = 8
+
+
+def slab_kernel(
+    parts,
+    tile_rows,
+    full,
+    freqs,
+    recv_ref,
+    out_ref,
+    onehot,
+    spread,
+    first,
+    second,
+    table,
+    faces_x,
+    faces_y,
+    moved_ref,
+    done_ref,
+    sems,
+):
     slab_rows = parts * tile_rows
     half = LANES // 2
-    base = full * DIR
-    shared_base = base + 16
+    span_rows = full * DIR + 16
+    shared_base = freqs * span_rows
     highs = slab_rows // 2
+    width = freqs * 2 * DIR
     low_lane = lax.broadcasted_iota(jnp.int32, (1, LANES), 1) < half
     low_lanes = lax.broadcasted_iota(jnp.int32, (8, LANES), 1) < half
     top_rows = lax.broadcasted_iota(jnp.int32, (8, LANES), 0) < 4
     cell_iota = lax.broadcasted_iota(jnp.int32, (2 * LANES, LANES), 0).astype(jnp.float32).astype(jnp.bfloat16)
+    high_iota = lax.broadcasted_iota(jnp.int32, (highs, LANES), 0)
 
     def cells_of(owner, chunk):
-        return shared_ref[owner, pl.ds(shared_base + 4 * tile_rows + chunk, 1), :].astype(jnp.int32)
+        return recv_ref[owner, pl.ds(shared_base + 3 * tile_rows + chunk, 1), :].astype(jnp.int32)
 
     def place(index, cells, values):
         span = pl.ds(index * LANES, LANES)
@@ -226,18 +244,26 @@
         low = (cells - high * (2 * LANES)).astype(jnp.float32)
         low = jnp.broadcast_to(low, (2 * LANES, LANES)).astype(jnp.bfloat16)
         onehot[:, span] = jnp.where(cell_iota == low, 1.0, 0.0).astype(jnp.bfloat16)
-        head = values.astype(jnp.bfloat16).astype(jnp.float32)
-        both = jnp.concatenate([head, values - head], axis=0).astype(jnp.bfloat16)
+        pieces = []
+        for value in values:
+            head = value.astype(jnp.bfloat16).astype(jnp.float32)
+            pieces += [head, value - head]
+        both = jnp.concatenate(pieces, axis=0).astype(jnp.bfloat16)
         for h in range(highs):
-            pick = jnp.broadcast_to((high == h).astype(jnp.float32), (2 * DIR, LANES)).astype(jnp.bfloat16)
-            spread[pl.ds(h * 2 * DIR, 2 * DIR), span] = both * pick
+            pick = jnp.broadcast_to((high == h).astype(jnp.float32), (width, LANES)).astype(jnp.bfloat16)
+            spread[pl.ds(h * width, width), span] = both * pick
+        spread[pl.ds(highs * width, highs), span] = (
+            (high_iota == high).astype(jnp.float32).astype(jnp.bfloat16)
+        )
 
     per_pair = 2 * full + 1
     for pair in range(parts // 2):
         even, odd = 2 * pair, 2 * pair + 1
         for side, owner in enumerate((even, odd)):
             for chunk in range(full):
-                values = recv_ref[owner, pl.ds(chunk * DIR, DIR), :]
+                values = [
+                    recv_ref[owner, pl.ds(f * span_rows + chunk * DIR, DIR), :] for f in range(freqs)
+                ]
                 place(pair * per_pair + side * full + chunk, cells_of(owner, chunk), values)
 
         def merged(offset):
@@ -247,9 +273,13 @@
                 jnp.where(low_lanes, pltpu.roll(own, half, 1), other),
             )
 
-        one, two = merged(base)
-        three, four = merged(base + 8)
-        values = jnp.concatenate([one, two, jnp.where(top_rows, three, pltpu.roll(four, 4, 0))], axis=0)
+        values = []
+        for f in range(freqs):
+            one, two = merged(f * span_rows + full * DIR)
+            three, four = merged(f * span_rows + full * DIR + 8)
+            values.append(
+                jnp.concatenate([one, two, jnp.where(top_rows, three, pltpu.roll(four, 4, 0))], axis=0)
+            )
         cells = jnp.where(low_lane, cells_of(even, full), pltpu.roll(cells_of(odd, full), half, 1))
         place(pair * per_pair + 2 * full, cells, values)
 
@@ -257,27 +287,30 @@
         spread[...], onehot[...], (((1,), (1,)), ((), ())), preferred_element_type=jnp.float32
     )
     nothing = jnp.zeros((DIR, LANES), jnp.float32)
-    for field in (first, second):
-        for edge in (0, 1, slab_rows + 2, slab_rows + 3):
-            field[edge] = nothing
-    for h in range(highs):
-        at = h * 2 * DIR
-        total = scattered[at : at + DIR] + scattered[at + DIR : at + 2 * DIR]
-        first[2 * h + 2] = total[:, :LANES]
-        first[2 * h + 3] = total[:, LANES:]
+    for f in range(freqs):
+        for field in (first, second):
+            for edge in (0, 1, slab_rows + 2, slab_rows + 3):
+                field[f, edge] = nothing
+        for h in range(highs):
+            at = h * width + f * 2 * DIR
+            total = scattered[at : at + DIR] + scattered[at + DIR : at + 2 * DIR]
+            first[f, 2 * h + 2] = total[:, :LANES]
+            first[f, 2 * h + 3] = total[:, LANES:]
 
     lane = lax.broadcasted_iota(jnp.int32, (slab_rows, LANES), 1)
     zero_rows = jnp.zeros((8, LANES), jnp.float32)
 
-    def gather(ref, offset):
-        return jnp.concatenate([ref[owner, pl.ds(offset, tile_rows), :] for owner in range(parts)], axis=0)
+    def gather(offset):
+        return jnp.concatenate(
+            [recv_ref[owner, pl.ds(offset, tile_rows), :] for owner in range(parts)], axis=0
+        )
 
     gain = 0.5 * courant / 8.0
     slots = iter(range(table.shape[0]))
 
     def keep(rows):
         slot = next(slots)
-        table[slot, pl.ds(8, slab_rows), :] = rows
+        table[slot, pl.ds(8, rows.shape[0]), :] = rows
         return slot
 
     def face_x(rows):
@@ -294,13 +327,12 @@
         before = jnp.where(lane > 0, pltpu.roll(rows, 1, 1), 0.0)
         return keep(gain * (rows + after)), keep(gain * (rows + before))
 
-    speed = gather(recv_ref, base + 12)
-    current_x, current_y, turning, land = (
-        gather(shared_ref, shared_base + kind * tile_rows) for kind in range(4)
-    )
-    current_x_face, speed_x_face = face_x(current_x), face_x(speed)
-    current_y_faces, speed_y_faces = face_y(current_y), face_y(speed)
-    land_slot = keep(land)
+    speeds = [gather(f * span_rows + full * DIR + 12) for f in range(freqs)]
+    current_x, current_y, turning = (gather(shared_base + kind * tile_rows) for kind in range(3))
+    current_x_face, speed_x_face = face_x(current_x), [face_x(s) for s in speeds]
+    current_y_faces, speed_y_faces = face_y(current_y), [face_y(s) for s in speeds]
+    named = scattered[highs * width : highs * width + highs]
+    land_slots = keep(named[:, :LANES]), keep(named[:, LANES:])
     ahead = jnp.maximum(turning, 0.0) * 0.125
     back = jnp.minimum(turning, 0.0) * 0.125
     bend_slots = [
@@ -322,113 +354,122 @@
     def row(slot, x):
         return table[slot, pl.ds(8 + x, 1), :]
 
-    def flux(speeds, behind, centre, centre3, onward3, beyond):
-        both = centre3 + onward3
-        return speeds[0] * (both + centre3 - behind) + speeds[1] * (both + onward3 - beyond)
-
-    def split(speed):
-        return jnp.maximum(speed, 0.0), jnp.minimum(speed, 0.0)
-
-    def flux_x(field, x, speeds, centre3, onward3):
-        return flux(speeds, field[x + 1], None, centre3, onward3, field[x + 4])
-
-    def sweep(field, fresh, finish):
-        def speeds_x(x):
+    def flux(speed, behind, centre3, onward3, beyond):
+        positive = speed > 0.0
+        near = jnp.where(positive, centre3, onward3)
+        far = jnp.where(positive, behind, beyond)
+        return speed * ((centre3 + onward3) + (near - far))
+
+    def advance(field, fresh, step, carry, finish):
+        def speed_x(f, x):
             if fresh:
-                speeds = split(row(speed_x_face, x) * cosine + row(current_x_face, x))
-                faces_x[0, x + 1], faces_x[1, x + 1] = speeds
-                return speeds
-            return faces_x[0, x + 1], faces_x[1, x + 1]
-
-        def speeds_y(side, x):
+                faces_x[f, x + 1] = row(speed_x_face[f], x) * cosine + row(current_x_face, x)
+            return faces_x[f, x + 1]
+
+        def speed_y(f, side, x):
             if fresh:
-                speeds = split(row(speed_y_faces[side], x) * sine + row(current_y_faces[side], x))
-                faces_r[2 * side, x], faces_r[2 * side + 1, x] = speeds
-                return speeds
-            return faces_r[2 * side, x], faces_r[2 * side + 1, x]
-
-        def body(step, carry):
-            entering, centre3 = carry
-            for i in range(UNROLL):
-                x = step * UNROLL + i
-                centre = field[x + 2]
-                onward3 = 3.0 * field[x + 3]
-                leaving = flux_x(field, x, speeds_x(x), centre3, onward3)
+                faces_y[f, side, x] = row(speed_y_faces[f][side], x) * sine + row(current_y_faces[side], x)
+            return faces_y[f, side, x]
+
+        carry = list(carry)
+        for i in range(BLOCK):
+            x = step * BLOCK + i
+            sea = row(land_slots[i % 2], step * (BLOCK // 2) + i // 2)
+            for f in range(freqs):
+                entering, centre3 = carry[f]
+                centre = field[f, x + 2]
+                onward3 = 3.0 * field[f, x + 3]
+                leaving = flux(speed_x(f, x), field[f, x + 1], centre3, onward3, field[f, x + 4])
                 up1 = jnp.where(lane_wide < LANES - 1, pltpu.roll(centre, LANES - 1, 1), 0.0)
                 up2 = jnp.where(lane_wide < LANES - 2, pltpu.roll(centre, LANES - 2, 1), 0.0)
                 down1 = jnp.where(lane_wide > 0, pltpu.roll(centre, 1, 1), 0.0)
                 down2 = jnp.where(lane_wide > 1, pltpu.roll(centre, 2, 1), 0.0)
-                right = flux(speeds_y(0, x), down1, centre, centre3, 3.0 * up1, up2)
-                left = flux(speeds_y(1, x), down2, down1, 3.0 * down1, centre3, up1)
-                finish(x, (centre - (leaving - entering) - (right - left)) * row(land_slot, x))
-                entering, centre3 = leaving, onward3
-            return entering, centre3
-
-        start3 = 3.0 * field[2]
-        entering = flux_x(field, -1, speeds_x(-1), nothing, start3)
-        lax.fori_loop(0, slab_rows // UNROLL, body, (entering, start3))
-
-    def store(x, moved):
-        second[x + 2] = moved
-
-    def refract(x, moved):
-        bent = row(bend_slots[2], x) * moved
-        for slot, shift in zip(bend_slots, (2, 1, 0, DIR - 1, DIR - 2)):
-            if shift:
-                bent = bent + row(slot, x) * jnp.roll(moved, shift, axis=0)
+                right = flux(speed_y(f, 0, x), down1, centre3, 3.0 * up1, up2)
+                left = flux(speed_y(f, 1, x), down2, 3.0 * down1, centre3, up1)
+                finish(f, x, (centre - (leaving - entering) - (right - left)) * sea)
+                carry[f] = leaving, onward3
+        return tuple(carry)
+
+    def enter(field, fresh):
+        carry = []
+        for f in range(freqs):
+            if fresh:
+                faces_x[f, 0] = row(speed_x_face[f], -1) * cosine + row(current_x_face, -1)
+            start3 = 3.0 * field[f, 2]
+            carry.append((flux(faces_x[f, 0], nothing, nothing, start3, field[f, 3]), start3))
+        return tuple(carry)
+
+    def store(f, x, moved):
+        second[f, x + 2] = moved
+
+    def turn(f, x, moved):
         for g in range(DIR // 8):
-            out_ref[pl.ds(g * 8 * slab_rows + x, 8, stride=slab_rows), :] = bent[g * 8 : g * 8 + 8]
-
-    sweep(first, True, store)
-    sweep(second, False, refract)
-
-
-def slab_plan(spectra, wind, growth, damping, row_cell, land_mask, group_speed, current, turning):
+            at = (f * DIR + g * 8) * slab_rows + x
+            moved_ref[pl.ds(at, 8, stride=slab_rows), :] = moved[g * 8 : g * 8 + 8]
+
+    def copy_out(step):
+        part = pl.ds(pl.multiple_of(step * BLOCK, BLOCK), BLOCK)
+        return pltpu.make_async_copy(done_ref.at[:, part, :], out_ref.at[:, part, :], sems.at[step])
+
+    def final(step, carry):
+        carry = advance(second, False, step, carry, turn)
+        at = pl.multiple_of(step * BLOCK, BLOCK)
+        weights = [table[slot, pl.ds(8 + at, BLOCK), :] for slot in bend_slots]
+        for f in range(freqs):
+            ring = [moved_ref[pl.ds((f * DIR + d) * slab_rows + at, BLOCK), :] for d in range(DIR)]
+            for d in range(DIR):
+                bent = weights[2] * ring[d]
+                for k in (0, 1, 3, 4):
+                    bent = bent + weights[k] * ring[(d + k - 2) % DIR]
+                done_ref[f * DIR + d, pl.ds(at, BLOCK), :] = bent
+        copy_out(step).start()
+        return carry
+
+    steps = slab_rows // BLOCK
+    lax.fori_loop(0, steps, lambda step, carry: advance(first, True, step, carry, store), enter(first, True))
+    lax.fori_loop(0, steps, final, enter(second, False))
+    for step in range(steps):
+        copy_out(step).wait()
+
+
+def slab_plan(spectra, wind, growth, damping, row_cell, group_speed, current, turning):
     parts = lax.axis_size(GROUP)
     rows, comps = spectra.shape
-    tile_rows = land_mask.shape[0]
+    tile_rows = turning.shape[0]
     freqs = comps // parts // DIR
     full = rows // LANES
     slab_rows = parts * tile_rows
     depth = parts * rows
-    block_rows = full * DIR + 16
-    shared_rows = -(-(4 * tile_rows + full + 1) // 8) * 8
-    blocks = [block_rows + shared_rows * (f == 0) for f in range(freqs)]
-    params = pltpu.CompilerParams(vmem_limit_bytes=56 * 1024 * 1024)
+    highs = slab_rows // 2
+    block_rows = -(-(freqs * (full * DIR + 16) + 3 * tile_rows + full + 1) // 8) * 8
     packed = pl.pallas_call(
-        functools.partial(pack_kernel, parts),
-        out_shape=[jax.ShapeDtypeStruct((parts, block, LANES), jnp.float32) for block in blocks],
-        compiler_params=params,
+        functools.partial(pack_kernel, parts, freqs),
+        out_shape=jax.ShapeDtypeStruct((parts, block_rows, LANES), jnp.float32),
+        compiler_params=pltpu.CompilerParams(vmem_limit_bytes=56 * 1024 * 1024),
         name="pack",
-    )(spectra, wind, growth, damping, row_cell, land_mask, group_speed, current, turning)
-    arrived = [lax.all_to_all(p, GROUP, split_axis=0, concat_axis=0, tiled=True) for p in packed]
-    whole = pl.BlockSpec(memory_space=pltpu.VMEM)
-    field = None
-    for f in range(freqs):
-        operands = [arrived[f]] if f == 0 else [arrived[f], field, arrived[0]]
-        field = pl.pallas_call(
-            functools.partial(slab_kernel, parts, tile_rows, full),
-            grid=(1,),
-            out_shape=jax.ShapeDtypeStruct((freqs * DIR * slab_rows, LANES), jnp.float32),
-            in_specs=[whole] if f == 0 else [whole, pl.BlockSpec(memory_space=pl.ANY), whole],
-            out_specs=pl.BlockSpec((DIR * slab_rows, LANES), functools.partial(lambda f, i: (f, 0), f)),
-            scratch_shapes=[
-                pltpu.VMEM((2 * LANES, depth), jnp.bfloat16),
-                pltpu.VMEM((slab_rows * DIR, depth), jnp.bfloat16),
-                pltpu.VMEM((slab_rows + 4, DIR, LANES), jnp.float32),
-                pltpu.VMEM((slab_rows + 4, DIR, LANES), jnp.float32),
-                pltpu.VMEM((12, slab_rows + 16, LANES), jnp.float32),
-                pltpu.VMEM((2, slab_rows + 1, DIR, LANES), jnp.float32),
-                pltpu.VMEM((4, slab_rows, DIR, LANES), jnp.float32),
-            ],
-            input_output_aliases={} if f == 0 else {1: 0},
-            cost_estimate=pl.CostEstimate(
-                flops=100 * slab_rows * DIR * LANES * 10, bytes_accessed=1 << 20, transcendentals=0
-            ),
-            compiler_params=params,
-            name="slab",
-        )(*operands)
-    return field.reshape(1, freqs * DIR, slab_rows, LANES)
+    )(spectra, wind, growth, damping, row_cell, group_speed, current, turning)
+    arrived = lax.all_to_all(packed, GROUP, split_axis=0, concat_axis=0, tiled=True)
+    out = pl.pallas_call(
+        functools.partial(slab_kernel, parts, tile_rows, full, freqs),
+        out_shape=jax.ShapeDtypeStruct((freqs * DIR, slab_rows, LANES), jnp.float32),
+        in_specs=[pl.BlockSpec(memory_space=pltpu.VMEM)],
+        out_specs=pl.BlockSpec(memory_space=pl.ANY),
+        scratch_shapes=[
+            pltpu.VMEM((2 * LANES, depth), jnp.bfloat16),
+            pltpu.VMEM((highs * (freqs * 2 * DIR + 1), depth), jnp.bfloat16),
+            pltpu.VMEM((freqs, slab_rows + 4, DIR, LANES), jnp.float32),
+            pltpu.VMEM((freqs, slab_rows + 4, DIR, LANES), jnp.float32),
+            pltpu.VMEM((10 + 3 * freqs, slab_rows + 16, LANES), jnp.float32),
+            pltpu.VMEM((freqs, slab_rows + 1, DIR, LANES), jnp.float32),
+            pltpu.VMEM((freqs, 2, slab_rows, DIR, LANES), jnp.float32),
+            pltpu.VMEM((freqs * DIR * slab_rows, LANES), jnp.float32),
+            pltpu.VMEM((freqs * DIR, slab_rows, LANES), jnp.float32),
+            pltpu.SemaphoreType.DMA((slab_rows // BLOCK,)),
+        ],
+        compiler_params=pltpu.CompilerParams(vmem_limit_bytes=32 * 1024 * 1024),
+        name="slab",
+    )(arrived)
+    return out.reshape(1, freqs * DIR, slab_rows, LANES)
 
 
 def shards(*arrays):
@@ -438,7 +479,7 @@
     whole_frequencies = comps == parts * 2 * DIR
     fits = rows % LANES == LANES // 2 and land_mask.shape == (4, LANES) and parts % 2 == 0
     if whole_frequencies and fits:
-        return slab_plan(*arrays)
+        return slab_plan(*arrays[:5], *arrays[6:])
     return tile_plan(*arrays)
 
 

time: 39.9 us -> 33.1 us (0.83)
  blocking collectives: 18.9 us -> 23.8 us
  Pallas kernels: 13.9 us -> 9.11 us
  starting transfers between devices: 3.41 us -> 0 us
  waiting for transfers between devices: 2.65 us -> 0 us
  local copies, waits for them, and re-layouts: 0.7 us -> 0 us
    all_to_all x1, blocking collectives: 18.9 us -> 23.8 us  [slab_plan(): lax.all_to_all(packed, GROUP, split_axis=0, concat_axis=0, tiled=True)]
    pallas_call x3 -> x2, Pallas kernels: 13.9 us -> 9.11 us  [the longest x1 6.9 us: slab_plan(): pl.pallas_call(functools.partial(slab_kernel, parts, tile_rows, full, fre...]
    all_to_all x1 -> x0, starting transfers between devices: 3.41 us -> none  [slab_plan(): lax.all_to_all(p, GROUP, split_axis=0, concat_axis=0, tiled=True)]
    all_to_all x1 -> x0, waiting for transfers between devices: 2.65 us -> none  [slab_plan(): lax.all_to_all(p, GROUP, split_axis=0, concat_axis=0, tiled=True)]
    unnamed x2 -> x0, local copies, waits for them, and re-layouts: 0.7 us -> none
  transfers between devices with their start and end apart: 1 -> 0, of which waited for: 1 -> 0; matrix products, arithmetic and copies ran while one was open for 0% -> 0% of each run, Pallas kernels for 15% -> 0%
where the time goes in v4:
time: 33.1 us; the launch traced here: 32.9 us
  blocking collectives  23.8 us (72%)
  Pallas kernels  9.11 us (28%)
    all_to_all x1, blocking collectives, slab_plan(): lax.all_to_all(packed, GROUP, split_axis=0, concat_axis=0, tiled=True)  23.8 us
    pallas_call x1, Pallas kernels, slab_plan(): pl.pallas_call(functools.partial(slab_kernel, parts, tile_rows, full, fre...  6.9 us
    pallas_call x1, Pallas kernels, slab_plan(): pl.pallas_call(functools.partial(pack_kernel, parts, freqs), out_shape=ja...  2.22 us

profile of v4, /device:TPU:0, one launch (start us, length us, event | category | flops | bytes accessed | tf_op | source)
XLA Modules:
  0.0 32.9 jit_solution(14157128792210591839)
XLA Ops:
  0.0 2.2 %pack.1 = f32[8,144,128]{2,1,0:T(8,128)} custom-call(f32[320,384]{1,0:T(8,128)} %spectra_ref.1, f32[320]{0:T(512)} %wind_ref.1, f32[384]{0:T(512)} %growth_ref.1, f32[384]{0:T(512)} %damping_ref.1, s32[320]{0:T(512)} %cell_ref.1, f32[16,4,128]{2,1,0:T(4,128)} %speed_ref.1, f32[2,4,128]{2,1,0:T(4,128)} %current_ref.1, f32[4,128]{1,0:T(4,128)} %turning_ref.1), custom_call_target="tpu_custom_call" | custom-call | tf_op jit(solution)/shard_map/pack/pallas_call | solution.py:445
  2.2 23.8 %all_to_all.5.recv_ref = f32[8,144,128]{2,1,0:T(8,128)S(1)} all-to-all(f32[8,144,128]{2,1,0:T(8,128)} %pack.1), channel_id=1, replica_groups=mesh['groups'=2,'pts'=4,'comp'=2,'sub'=2] {'pts','comp'}, dimensions={0} | all-to-all | bytes 1179648 | tf_op jit(solution)/shard_map/all_to_all | solution.py:451
  26.0 6.9 %slab.1 = f32[48,32,128]{2,1,0:T(8,128)} custom-call(f32[8,144,128]{2,1,0:T(8,128)S(1)} %all_to_all.5.recv_ref), custom_call_target="tpu_custom_call" | custom-call | tf_op jit(solution)/shard_map/slab/pallas_call | solution.py:452

commit v5 on v4

--- a/solution.py
+++ b/solution.py
@@ -203,6 +203,7 @@
 
 
 BLOCK = 8
+SPAN = 4
 
 
 def slab_kernel(
@@ -213,6 +214,7 @@
     recv_ref,
     out_ref,
     onehot,
+    masses,
     spread,
     first,
     second,
@@ -227,34 +229,40 @@
     half = LANES // 2
     span_rows = full * DIR + 16
     shared_base = freqs * span_rows
-    highs = slab_rows // 2
+    highs = slab_rows // SPAN
     width = freqs * 2 * DIR
+    half_rows = highs // 2 * width
+    depth = onehot.shape[1]
+    named_rows = spread.shape[0] - highs * width
     low_lane = lax.broadcasted_iota(jnp.int32, (1, LANES), 1) < half
     low_lanes = lax.broadcasted_iota(jnp.int32, (8, LANES), 1) < half
     top_rows = lax.broadcasted_iota(jnp.int32, (8, LANES), 0) < 4
-    cell_iota = lax.broadcasted_iota(jnp.int32, (2 * LANES, LANES), 0).astype(jnp.float32).astype(jnp.bfloat16)
-    high_iota = lax.broadcasted_iota(jnp.int32, (highs, LANES), 0)
+    cell_iota = (
+        lax.broadcasted_iota(jnp.int32, (2 * LANES, LANES), 0).astype(jnp.float32).astype(jnp.bfloat16)
+    )
+    high_iota = lax.broadcasted_iota(jnp.int32, (named_rows, LANES), 0)
+    high_parts = []
 
     def cells_of(owner, chunk):
         return recv_ref[owner, pl.ds(shared_base + 3 * tile_rows + chunk, 1), :].astype(jnp.int32)
 
     def place(index, cells, values):
         span = pl.ds(index * LANES, LANES)
-        high = cells // (2 * LANES)
-        low = (cells - high * (2 * LANES)).astype(jnp.float32)
-        low = jnp.broadcast_to(low, (2 * LANES, LANES)).astype(jnp.bfloat16)
-        onehot[:, span] = jnp.where(cell_iota == low, 1.0, 0.0).astype(jnp.bfloat16)
+        high = cells // (SPAN * LANES)
+        low = cells - high * (SPAN * LANES)
+        for k in range(0, SPAN, 2):
+            near = jnp.broadcast_to((low - k * LANES).astype(jnp.float32), (2 * LANES, LANES))
+            hit = cell_iota == near.astype(jnp.bfloat16)
+            onehot[pl.ds(k * LANES, 2 * LANES), span] = jnp.where(hit, 1.0, 0.0).astype(jnp.bfloat16)
         pieces = []
         for value in values:
             head = value.astype(jnp.bfloat16).astype(jnp.float32)
             pieces += [head, value - head]
-        both = jnp.concatenate(pieces, axis=0).astype(jnp.bfloat16)
-        for h in range(highs):
-            pick = jnp.broadcast_to((high == h).astype(jnp.float32), (width, LANES)).astype(jnp.bfloat16)
-            spread[pl.ds(h * width, width), span] = both * pick
-        spread[pl.ds(highs * width, highs), span] = (
+        masses[:, span] = jnp.concatenate(pieces, axis=0).astype(jnp.bfloat16)
+        spread[pl.ds(highs * width, named_rows), span] = (
             (high_iota == high).astype(jnp.float32).astype(jnp.bfloat16)
         )
+        high_parts.append(high)
 
     per_pair = 2 * full + 1
     for pair in range(parts // 2):
@@ -283,19 +291,37 @@
         cells = jnp.where(low_lane, cells_of(even, full), pltpu.roll(cells_of(odd, full), half, 1))
         place(pair * per_pair + 2 * full, cells, values)
 
-    scattered = lax.dot_general(
-        spread[...], onehot[...], (((1,), (1,)), ((), ())), preferred_element_type=jnp.float32
-    )
+    def product(first_row, count):
+        return lax.dot_general(
+            spread[pl.ds(first_row, count), :],
+            onehot[...],
+            (((1,), (1,)), ((), ())),
+            preferred_element_type=jnp.float32,
+        )
+
+    def build(h):
+        for index, high in enumerate(high_parts):
+            span = pl.ds(index * LANES, LANES)
+            pick = jnp.broadcast_to((high == h).astype(jnp.float32), (width, LANES)).astype(jnp.bfloat16)
+            spread[pl.ds(h * width, width), span] = masses[:, span] * pick
+
     nothing = jnp.zeros((DIR, LANES), jnp.float32)
     for f in range(freqs):
         for field in (first, second):
             for edge in (0, 1, slab_rows + 2, slab_rows + 3):
                 field[f, edge] = nothing
-        for h in range(highs):
-            at = h * width + f * 2 * DIR
-            total = scattered[at : at + DIR] + scattered[at + DIR : at + 2 * DIR]
-            first[f, 2 * h + 2] = total[:, :LANES]
-            first[f, 2 * h + 3] = total[:, LANES:]
+    named = product(highs * width, named_rows)
+    for part in range(2):
+        some = range(part * highs // 2, (part + 1) * highs // 2)
+        for h in some:
+            build(h)
+        scattered = product(part * half_rows, half_rows)
+        for h in some:
+            for f in range(freqs):
+                at = (h - some[0]) * width + f * 2 * DIR
+                total = scattered[at : at + DIR] + scattered[at + DIR : at + 2 * DIR]
+                for k in range(SPAN):
+                    first[f, SPAN * h + 2 + k] = total[:, k * LANES : (k + 1) * LANES]
 
     lane = lax.broadcasted_iota(jnp.int32, (slab_rows, LANES), 1)
     zero_rows = jnp.zeros((8, LANES), jnp.float32)
@@ -331,8 +357,7 @@
     current_x, current_y, turning = (gather(shared_base + kind * tile_rows) for kind in range(3))
     current_x_face, speed_x_face = face_x(current_x), [face_x(s) for s in speeds]
     current_y_faces, speed_y_faces = face_y(current_y), [face_y(s) for s in speeds]
-    named = scattered[highs * width : highs * width + highs]
-    land_slots = keep(named[:, :LANES]), keep(named[:, LANES:])
+    land_slots = [keep(named[:highs, k * LANES : (k + 1) * LANES]) for k in range(SPAN)]
     ahead = jnp.maximum(turning, 0.0) * 0.125
     back = jnp.minimum(turning, 0.0) * 0.125
     bend_slots = [
@@ -374,7 +399,7 @@
         carry = list(carry)
         for i in range(BLOCK):
             x = step * BLOCK + i
-            sea = row(land_slots[i % 2], step * (BLOCK // 2) + i // 2)
+            sea = row(land_slots[i % SPAN], step * (BLOCK // SPAN) + i // SPAN)
             for f in range(freqs):
                 entering, centre3 = carry[f]
                 centre = field[f, x + 2]
@@ -440,11 +465,11 @@
     full = rows // LANES
     slab_rows = parts * tile_rows
     depth = parts * rows
-    highs = slab_rows // 2
+    highs = slab_rows // SPAN
     block_rows = -(-(freqs * (full * DIR + 16) + 3 * tile_rows + full + 1) // 8) * 8
     packed = pl.pallas_call(
         functools.partial(pack_kernel, parts, freqs),
-        out_shape=jax.ShapeDtypeStruct((parts, block_rows, LANES), jnp.float32),
+        out_shape=pltpu.VMEM((parts, block_rows, LANES), jnp.float32),
         compiler_params=pltpu.CompilerParams(vmem_limit_bytes=56 * 1024 * 1024),
         name="pack",
     )(spectra, wind, growth, damping, row_cell, group_speed, current, turning)
@@ -455,11 +480,12 @@
         in_specs=[pl.BlockSpec(memory_space=pltpu.VMEM)],
         out_specs=pl.BlockSpec(memory_space=pl.ANY),
         scratch_shapes=[
-            pltpu.VMEM((2 * LANES, depth), jnp.bfloat16),
-            pltpu.VMEM((highs * (freqs * 2 * DIR + 1), depth), jnp.bfloat16),
+            pltpu.VMEM((SPAN * LANES, depth), jnp.bfloat16),
+            pltpu.VMEM((freqs * 2 * DIR, depth), jnp.bfloat16),
+            pltpu.VMEM((highs * freqs * 2 * DIR + -(-highs // 16) * 16, depth), jnp.bfloat16),
             pltpu.VMEM((freqs, slab_rows + 4, DIR, LANES), jnp.float32),
             pltpu.VMEM((freqs, slab_rows + 4, DIR, LANES), jnp.float32),
-            pltpu.VMEM((10 + 3 * freqs, slab_rows + 16, LANES), jnp.float32),
+            pltpu.VMEM((8 + SPAN + 3 * freqs, slab_rows + 16, LANES), jnp.float32),
             pltpu.VMEM((freqs, slab_rows + 1, DIR, LANES), jnp.float32),
             pltpu.VMEM((freqs, 2, slab_rows, DIR, LANES), jnp.float32),
             pltpu.VMEM((freqs * DIR * slab_rows, LANES), jnp.float32),

time: 33.1 us -> 33.4 us (level)
  Pallas kernels: 9.11 us -> 9.64 us
    pallas_call x1, Pallas kernels: 6.9 us -> 8.24 us  [slab_plan(): pl.pallas_call(functools.partial(slab_kernel, parts, tile_rows, full, fre...]
    pallas_call x1, Pallas kernels: 2.22 us -> 1.4 us  [slab_plan(): pl.pallas_call(functools.partial(pack_kernel, parts, freqs), out_shape=pl...]
where the time goes in v5:
time: 33.4 us; the launch traced here: 33.3 us
  blocking collectives  23.6 us (71%)
  Pallas kernels  9.64 us (29%)
    all_to_all x1, blocking collectives, slab_plan(): lax.all_to_all(packed, GROUP, split_axis=0, concat_axis=0, tiled=True)  23.6 us
    pallas_call x1, Pallas kernels, slab_plan(): pl.pallas_call(functools.partial(slab_kernel, parts, tile_rows, full, fre...  8.24 us
    pallas_call x1, Pallas kernels, slab_plan(): pl.pallas_call(functools.partial(pack_kernel, parts, freqs), out_shape=pl...  1.4 us

profile of v5, /device:TPU:0, one launch (start us, length us, event | category | flops | bytes accessed | tf_op | source)
XLA Modules:
  0.0 33.3 jit_solution(6754732755627603574)
XLA Ops:
  0.0 1.4 %pack.1 = f32[8,144,128]{2,1,0:T(8,128)S(1)} custom-call(f32[320,384]{1,0:T(8,128)} %spectra_ref.1, f32[320]{0:T(512)} %wind_ref.1, f32[384]{0:T(512)} %growth_ref.1, f32[384]{0:T(512)} %damping_ref.1, s32[320]{0:T(512)} %cell_ref.1, f32[16,4,128]{2,1,0:T(4,128)} %speed_ref.1, f32[2,4,128]{2,1,0:T(4,128)} %current_ref.1, f32[4,128]{1,0:T(4,128)} %turning_ref.1), custom_call_target="tpu_custom_call" | custom-call | tf_op jit(solution)/shard_map/pack/pallas_call | solution.py:470
  1.4 23.6 %all_to_all.5.recv_ref = f32[8,144,128]{2,1,0:T(8,128)S(1)} all-to-all(f32[8,144,128]{2,1,0:T(8,128)S(1)} %pack.1), channel_id=1, replica_groups=mesh['groups'=2,'pts'=4,'comp'=2,'sub'=2] {'pts','comp'}, dimensions={0} | all-to-all | bytes 1179648 | tf_op jit(solution)/shard_map/all_to_all | solution.py:476
  25.0 8.2 %slab.1 = f32[48,32,128]{2,1,0:T(8,128)} custom-call(f32[8,144,128]{2,1,0:T(8,128)S(1)} %all_to_all.5.recv_ref), custom_call_target="tpu_custom_call" | custom-call | tf_op jit(solution)/shard_map/slab/pallas_call | solution.py:477

commit v6 on v4

--- a/solution.py
+++ b/solution.py
@@ -203,6 +203,7 @@
 
 
 BLOCK = 8
+PER_STEP = 2
 
 
 def slab_kernel(
@@ -411,9 +412,9 @@
         part = pl.ds(pl.multiple_of(step * BLOCK, BLOCK), BLOCK)
         return pltpu.make_async_copy(done_ref.at[:, part, :], out_ref.at[:, part, :], sems.at[step])
 
-    def final(step, carry):
-        carry = advance(second, False, step, carry, turn)
-        at = pl.multiple_of(step * BLOCK, BLOCK)
+    def final(block, carry):
+        carry = advance(second, False, block, carry, turn)
+        at = pl.multiple_of(block * BLOCK, BLOCK)
         weights = [table[slot, pl.ds(8 + at, BLOCK), :] for slot in bend_slots]
         for f in range(freqs):
             ring = [moved_ref[pl.ds((f * DIR + d) * slab_rows + at, BLOCK), :] for d in range(DIR)]
@@ -422,14 +423,21 @@
                 for k in (0, 1, 3, 4):
                     bent = bent + weights[k] * ring[(d + k - 2) % DIR]
                 done_ref[f * DIR + d, pl.ds(at, BLOCK), :] = bent
-        copy_out(step).start()
+        copy_out(block).start()
         return carry
 
-    steps = slab_rows // BLOCK
-    lax.fori_loop(0, steps, lambda step, carry: advance(first, True, step, carry, store), enter(first, True))
-    lax.fori_loop(0, steps, final, enter(second, False))
-    for step in range(steps):
-        copy_out(step).wait()
+    def sweep(one_block, carry):
+        def body(step, carry):
+            for i in range(PER_STEP):
+                carry = one_block(step * PER_STEP + i, carry)
+            return carry
+
+        lax.fori_loop(0, slab_rows // BLOCK // PER_STEP, body, carry)
+
+    sweep(lambda block, carry: advance(first, True, block, carry, store), enter(first, True))
+    sweep(final, enter(second, False))
+    for block in range(slab_rows // BLOCK):
+        copy_out(block).wait()
 
 
 def slab_plan(spectra, wind, growth, damping, row_cell, group_speed, current, turning):
@@ -444,7 +452,7 @@
     block_rows = -(-(freqs * (full * DIR + 16) + 3 * tile_rows + full + 1) // 8) * 8
     packed = pl.pallas_call(
         functools.partial(pack_kernel, parts, freqs),
-        out_shape=jax.ShapeDtypeStruct((parts, block_rows, LANES), jnp.float32),
+        out_shape=pltpu.VMEM((parts, block_rows, LANES), jnp.float32),
         compiler_params=pltpu.CompilerParams(vmem_limit_bytes=56 * 1024 * 1024),
         name="pack",
     )(spectra, wind, growth, damping, row_cell, group_speed, current, turning)

time: 33.1 us -> 31.8 us (0.961)
  Pallas kernels: 9.11 us -> 8.02 us
    pallas_call x1, Pallas kernels: 2.22 us -> 1.4 us  [slab_plan(): pl.pallas_call(functools.partial(pack_kernel, parts, freqs), out_shape=pl...]
where the time goes in v6:
time: 31.8 us; the launch traced here: 31.6 us
  blocking collectives  23.6 us (74%)
  Pallas kernels  8.02 us (25%)
    all_to_all x1, blocking collectives, slab_plan(): lax.all_to_all(packed, GROUP, split_axis=0, concat_axis=0, tiled=True)  23.6 us
    pallas_call x1, Pallas kernels, slab_plan(): pl.pallas_call(functools.partial(slab_kernel, parts, tile_rows, full, fre...  6.62 us
    pallas_call x1, Pallas kernels, slab_plan(): pl.pallas_call(functools.partial(pack_kernel, parts, freqs), out_shape=pl...  1.4 us

profile of v6, /device:TPU:0, one launch (start us, length us, event | category | flops | bytes accessed | tf_op | source)
XLA Modules:
  0.0 31.6 jit_solution(11009793271143416090)
XLA Ops:
  0.0 1.4 %pack.1 = f32[8,144,128]{2,1,0:T(8,128)S(1)} custom-call(f32[320,384]{1,0:T(8,128)} %spectra_ref.1, f32[320]{0:T(512)} %wind_ref.1, f32[384]{0:T(512)} %growth_ref.1, f32[384]{0:T(512)} %damping_ref.1, s32[320]{0:T(512)} %cell_ref.1, f32[16,4,128]{2,1,0:T(4,128)} %speed_ref.1, f32[2,4,128]{2,1,0:T(4,128)} %current_ref.1, f32[4,128]{1,0:T(4,128)} %turning_ref.1), custom_call_target="tpu_custom_call" | custom-call | tf_op jit(solution)/shard_map/pack/pallas_call | solution.py:453
  1.4 23.6 %all_to_all.5.recv_ref = f32[8,144,128]{2,1,0:T(8,128)S(1)} all-to-all(f32[8,144,128]{2,1,0:T(8,128)S(1)} %pack.1), channel_id=1, replica_groups=mesh['groups'=2,'pts'=4,'comp'=2,'sub'=2] {'pts','comp'}, dimensions={0} | all-to-all | bytes 1179648 | tf_op jit(solution)/shard_map/all_to_all | solution.py:459
  25.0 6.6 %slab.1 = f32[48,32,128]{2,1,0:T(8,128)} custom-call(f32[8,144,128]{2,1,0:T(8,128)S(1)} %all_to_all.5.recv_ref), custom_call_target="tpu_custom_call" | custom-call | tf_op jit(solution)/shard_map/slab/pallas_call | solution.py:460

commit v7 on v0

--- a/solution.py
+++ b/solution.py
@@ -1,10 +1,16 @@
+import functools
+import math
 import jax
 import jax.numpy as jnp
 from jax import lax
+from jax.experimental import pallas as pl
+from jax.experimental.pallas import tpu as pltpu
 from jax.sharding import PartitionSpec as P
 
 DIR = 24
 SUBSTEPS = 2
+LANES = 128
+GROUP = ("pts", "comp")
 
 
 courant = 0.35
@@ -80,13 +86,13 @@
 
 def deliver(bulk_rows, small_rows):
     return (
-        lax.all_to_all(bulk_rows, ("pts", "comp"), split_axis=0, concat_axis=0, tiled=True),
-        lax.all_to_all(small_rows, ("pts", "comp"), split_axis=0, concat_axis=0, tiled=True),
-    )
-
-
-def shards(spectra, wind, growth, damping, row_cell, land_mask, group_speed, current, turning):
-    tile_count = lax.axis_size(("pts", "comp"))
+        lax.all_to_all(bulk_rows, GROUP, split_axis=0, concat_axis=0, tiled=True),
+        lax.all_to_all(small_rows, GROUP, split_axis=0, concat_axis=0, tiled=True),
+    )
+
+
+def tile_plan(spectra, wind, growth, damping, row_cell, land_mask, group_speed, current, turning):
+    tile_count = lax.axis_size(GROUP)
     comp_width = spectra.shape[1]
     tile_rows, tile_cols = land_mask.shape
     cell_count = tile_rows * tile_cols
@@ -116,7 +122,7 @@
     freq_count = comp_width // DIR
     reach = 2 * SUBSTEPS
     stacked = jnp.concatenate([group_speed, current, land_mask.astype(jnp.float32)[None]], axis=0)
-    rimmed = with_halo(stacked, ((("pts", "comp"), 1),), 2 * SUBSTEPS)
+    rimmed = with_halo(stacked, ((GROUP, 1),), 2 * SUBSTEPS)
     speed_x, speed_y = velocities(rimmed, freq_count)
     sea_rim = rimmed[freq_count + 2 :]
 
@@ -124,15 +130,409 @@
         return lax.slice_in_dim(values, reach - margin, reach + tile_rows + margin, axis=1)
 
     for repeat in range(SUBSTEPS):
-        extended = with_halo(spectrum, ((("pts", "comp"), 1),), 2)
+        extended = with_halo(spectrum, ((GROUP, 1),), 2)
         spectrum = substep(extended, window(speed_x, 2), window(speed_y, 0), window(sea_rim, 0)[0])
     blocks = spectrum.reshape(freq_count, DIR, tile_rows, tile_cols)
     wrapped = jnp.concatenate([blocks[:, -2:], blocks, blocks[:, :2]], axis=1)
     turning_full = jnp.broadcast_to(turning[None, None], wrapped.shape)
     blocks = blocks - upwind_divergence(wrapped, turning_full, 1)
     spectrum = blocks.reshape(comp_width, tile_rows, tile_cols)
-    shipped = lax.all_to_all(spectrum, ("pts", "comp"), split_axis=0, concat_axis=1, tiled=True)
+    shipped = lax.all_to_all(spectrum, GROUP, split_axis=0, concat_axis=1, tiled=True)
     return shipped[None]
+
+
+def pack_kernel(
+    parts,
+    freqs,
+    spectra_ref,
+    wind_ref,
+    growth_ref,
+    damping_ref,
+    cell_ref,
+    land_ref,
+    speed_ref,
+    current_ref,
+    turning_ref,
+    rows_ref,
+    small_ref,
+):
+    rows, comps = spectra_ref.shape
+    half = LANES // 2
+    full = rows // LANES
+    width = freqs * DIR
+    spare = jnp.zeros((1, half), jnp.float32)
+    wind_row = jnp.concatenate([wind_ref[...][None], spare], axis=1)
+    wind_cols = jnp.broadcast_to(wind_row, (LANES, rows + half)).T
+    low = lax.broadcasted_iota(jnp.int32, (8, LANES), 1) < half
+    tails = []
+    for block in range(comps // LANES):
+        lanes = pl.ds(block * LANES, LANES)
+        growth = growth_ref[lanes][None]
+        damping = damping_ref[lanes][None]
+
+        def source(first, count):
+            span = pl.ds(first, count)
+            return spectra_ref[span, lanes] * jnp.exp(
+                wind_cols[first : first + count] * growth - damping
+            )
+
+        for chunk in range(full):
+            turned = source(chunk * LANES, LANES).T
+            for g in range(LANES // 8):
+                part, within = divmod(block * LANES + g * 8, width)
+                rows_ref[part, pl.ds(chunk * width + within, 8), :] = turned[g * 8 : g * 8 + 8]
+        tail = source(full * LANES, half)
+        turned = jnp.concatenate([tail, tail], axis=0).T
+        tails += [turned[g * 8 : g * 8 + 8] for g in range(LANES // 8)]
+    for part in range(parts):
+        for g in range(DIR // 8):
+            one = tails[part * width // 8 + g]
+            two = tails[(part * width + DIR) // 8 + g]
+            rows_ref[part, pl.ds(full * width + g * 8, 8), :] = jnp.where(low, one, two)
+    cell_row = jnp.concatenate([cell_ref[...].astype(jnp.float32)[None], spare], axis=1)
+    small = jnp.concatenate(
+        [speed_ref[f] for f in range(speed_ref.shape[0])]
+        + [current_ref[0], current_ref[1], turning_ref[...], land_ref[...].astype(jnp.float32)]
+        + [cell_row[:, c * LANES : (c + 1) * LANES] for c in range(full + 1)],
+        axis=0,
+    )
+    spare_rows = jnp.zeros((small_ref.shape[0] - small.shape[0], LANES), jnp.float32)
+    small_ref[...] = jnp.concatenate([small, spare_rows], axis=0)
+
+
+def prepare_kernel(
+    parts,
+    tile_rows,
+    full,
+    freqs,
+    me_ref,
+    small_ref,
+    onehot_ref,
+    pick_ref,
+    weight_ref,
+    bend_ref,
+    table,
+):
+    slab_rows = parts * tile_rows
+    small_rows = small_ref.shape[0] // parts
+    base = small_rows - 8 * -(-(4 * tile_rows + full + 1) // 8)
+    half = LANES // 2
+    highs = slab_rows // 2
+    low_lane = lax.broadcasted_iota(jnp.int32, (1, LANES), 1) < half
+    cell_iota = (
+        lax.broadcasted_iota(jnp.int32, (2 * LANES, LANES), 0).astype(jnp.float32).astype(jnp.bfloat16)
+    )
+
+    def cells_of(owner, chunk):
+        return small_ref[pl.ds(owner * small_rows + base + 4 * tile_rows + chunk, 1), :].astype(jnp.int32)
+
+    def place(index, cells):
+        span = pl.ds(index * LANES, LANES)
+        high = cells // (2 * LANES)
+        low = jnp.broadcast_to((cells - high * (2 * LANES)).astype(jnp.float32), (2 * LANES, LANES))
+        hit = cell_iota == low.astype(jnp.bfloat16)
+        onehot_ref[:, span] = jnp.where(hit, 1.0, 0.0).astype(jnp.bfloat16)
+        for h in range(highs):
+            pick = jnp.broadcast_to((high == h).astype(jnp.float32), (16, LANES))
+            pick_ref[h, :, span] = pick.astype(jnp.bfloat16)
+
+    per_pair = 2 * full + 1
+    for pair in range(parts // 2):
+        for side in range(2):
+            for chunk in range(full):
+                place(pair * per_pair + side * full + chunk, cells_of(2 * pair + side, chunk))
+        even, odd = cells_of(2 * pair, full), cells_of(2 * pair + 1, full)
+        place(pair * per_pair + 2 * full, jnp.where(low_lane, even, pltpu.roll(odd, half, 1)))
+
+    lane = lax.broadcasted_iota(jnp.int32, (slab_rows, LANES), 1)
+    zero_rows = jnp.zeros((8, LANES), jnp.float32)
+    slots = iter(range(table.shape[0]))
+    gain = 0.5 * courant / 8.0
+
+    def keep(rows):
+        slot = next(slots)
+        table[slot, pl.ds(8, slab_rows), :] = rows
+        return slot
+
+    def face_x(rows):
+        slot = next(slots)
+        table[slot, pl.ds(0, 8), :] = zero_rows
+        table[slot, pl.ds(8 + slab_rows, 8), :] = zero_rows
+        table[slot, pl.ds(8, slab_rows), :] = rows
+        faces = gain * (table[slot, pl.ds(7, slab_rows + 8), :] + table[slot, pl.ds(8, slab_rows + 8), :])
+        table[slot, pl.ds(7, slab_rows + 8), :] = faces
+        return slot
+
+    def face_y(rows):
+        after = jnp.where(lane < LANES - 1, pltpu.roll(rows, LANES - 1, 1), 0.0)
+        before = jnp.where(lane > 0, pltpu.roll(rows, 1, 1), 0.0)
+        return keep(gain * (rows + after)), keep(gain * (rows + before))
+
+    def small(kind):
+        return jnp.concatenate(
+            [
+                small_ref[pl.ds(owner * small_rows + base + kind * tile_rows, tile_rows), :]
+                for owner in range(parts)
+            ],
+            axis=0,
+        )
+
+    mine = [
+        small_ref[pl.ds(pl.multiple_of(owner * small_rows + me_ref[0] * 8, 8), 8), :] for owner in range(parts)
+    ]
+    speeds = [
+        jnp.concatenate([m[f * tile_rows : (f + 1) * tile_rows] for m in mine], axis=0) for f in range(freqs)
+    ]
+    current_x, current_y, turning, land = (small(kind) for kind in range(4))
+    current_x_face, speed_x_face = face_x(current_x), [face_x(s) for s in speeds]
+    current_y_faces, speed_y_faces = face_y(current_y), [face_y(s) for s in speeds]
+    land_slots = [
+        keep(rows)
+        for rows in (
+            jnp.where(lane > 1, land, 0.0),
+            jnp.where(lane > 0, land, 0.0),
+            jnp.where(lane < LANES - 1, land, 0.0),
+            jnp.where(lane < LANES - 2, land, 0.0),
+            land,
+        )
+    ]
+    ahead = jnp.maximum(turning, 0.0) * 0.125
+    back = jnp.minimum(turning, 0.0) * 0.125
+    bend_ref[0] = -ahead
+    bend_ref[1] = 7.0 * ahead + 3.0 * back
+    bend_ref[2] = 1.0 - 3.0 * (ahead - back)
+    bend_ref[3] = -3.0 * ahead - 7.0 * back
+    bend_ref[4] = back
+
+    angles = lax.broadcasted_iota(jnp.int32, (DIR, LANES), 0).astype(jnp.float32) * (2.0 * math.pi / DIR)
+    cosine = jnp.cos(angles)
+    sine = jnp.sin(angles)
+
+    def row(slot, x):
+        return table[slot, pl.ds(8 + x, 1), :]
+
+    def face(speed):
+        plus, minus = jnp.maximum(speed, 0.0), jnp.minimum(speed, 0.0)
+        return plus, minus, 6.0 * plus + 3.0 * minus, 3.0 * plus + 6.0 * minus
+
+    def weights(right, left):
+        plus, minus, centre, onward = right
+        plus_l, minus_l, centre_l, onward_l = left
+        return -plus_l, plus + centre_l, -onward - minus_l, minus, onward_l - centre
+
+    def body(x, carry):
+        seas = [row(slot, x) for slot in land_slots]
+        leaving = []
+        for f in range(freqs):
+            right = face(row(speed_x_face[f], x) * cosine + row(current_x_face, x))
+            along_x = weights(right, carry[f])
+            along_y = weights(
+                *(
+                    face(row(speed_y_faces[f][side], x) * sine + row(current_y_faces[side], x))
+                    for side in range(2)
+                )
+            )
+            for k in range(4):
+                weight_ref[k, f, x] = along_x[k] * seas[4]
+                weight_ref[4 + k, f, x] = along_y[k] * seas[k]
+            weight_ref[8, f, x] = (1.0 + along_x[4] + along_y[4]) * seas[4]
+            leaving.append(right)
+        return tuple(leaving)
+
+    entering = tuple(
+        face(row(speed_x_face[f], -1) * cosine + row(current_x_face, -1)) for f in range(freqs)
+    )
+    lax.fori_loop(0, slab_rows, body, entering)
+
+
+BLOCK = 8
+PER_STEP = 2
+
+
+def slab_kernel(
+    parts,
+    tile_rows,
+    full,
+    freqs,
+    recv_ref,
+    onehot_ref,
+    pick_ref,
+    weight_ref,
+    bend_ref,
+    out_ref,
+    spread,
+    first,
+    second,
+    moved_ref,
+    done_ref,
+    sems,
+):
+    slab_rows = parts * tile_rows
+    half = LANES // 2
+    highs = slab_rows // 2
+    width = freqs * DIR
+    low_lanes = lax.broadcasted_iota(jnp.int32, (DIR, LANES), 1) < half
+
+    def place(index, values):
+        span = pl.ds(index * LANES, LANES)
+        pieces = []
+        for value in values:
+            head = value.astype(jnp.bfloat16).astype(jnp.float32)
+            pieces += [head, value - head]
+        both = jnp.concatenate(pieces, axis=0).astype(jnp.bfloat16)
+        for h in range(highs):
+            pick = jnp.concatenate([pick_ref[h, :, span]] * (2 * width // 16), axis=0)
+            spread[pl.ds(h * 2 * width, 2 * width), span] = both * pick
+
+    per_pair = 2 * full + 1
+    for pair in range(parts // 2):
+        even, odd = 2 * pair, 2 * pair + 1
+        for side, owner in enumerate((even, odd)):
+            for chunk in range(full):
+                values = [
+                    recv_ref[owner, pl.ds(chunk * width + f * DIR, DIR), :] for f in range(freqs)
+                ]
+                place(pair * per_pair + side * full + chunk, values)
+        own = recv_ref[even, pl.ds(full * width, DIR), :]
+        other = recv_ref[odd, pl.ds(full * width, DIR), :]
+        values = [
+            jnp.where(low_lanes, own, pltpu.roll(other, half, 1)),
+            jnp.where(low_lanes, pltpu.roll(own, half, 1), other),
+        ]
+        place(pair * per_pair + 2 * full, values)
+
+    scattered = lax.dot_general(
+        spread[...], onehot_ref[...], (((1,), (1,)), ((), ())), preferred_element_type=jnp.float32
+    )
+    nothing = jnp.zeros((DIR, LANES), jnp.float32)
+    for f in range(freqs):
+        for field in (first, second):
+            for edge in (0, 1, slab_rows + 2, slab_rows + 3):
+                field[f, edge] = nothing
+        for h in range(highs):
+            at = (h * freqs + f) * 2 * DIR
+            total = scattered[at : at + DIR] + scattered[at + DIR : at + 2 * DIR]
+            first[f, 2 * h + 2] = total[:, :LANES]
+            first[f, 2 * h + 3] = total[:, LANES:]
+
+    def advance(field, block, finish):
+        for i in range(BLOCK):
+            x = block * BLOCK + i
+            for f in range(freqs):
+                centre = field[f, x + 2]
+                moved = weight_ref[8, f, x] * centre
+                for k, there in enumerate((x, x + 1, x + 3, x + 4)):
+                    moved = moved + weight_ref[k, f, x] * field[f, there]
+                for k, shift in enumerate((2, 1, LANES - 1, LANES - 2)):
+                    moved = moved + weight_ref[4 + k, f, x] * pltpu.roll(centre, shift, 1)
+                finish(f, x, moved)
+
+    def store(f, x, moved):
+        second[f, x + 2] = moved
+
+    def turn(f, x, moved):
+        for g in range(DIR // 8):
+            at = (f * DIR + g * 8) * slab_rows + x
+            moved_ref[pl.ds(at, 8, stride=slab_rows), :] = moved[g * 8 : g * 8 + 8]
+
+    def copy_out(block):
+        part = pl.ds(pl.multiple_of(block * BLOCK, BLOCK), BLOCK)
+        return pltpu.make_async_copy(done_ref.at[:, part, :], out_ref.at[:, part, :], sems.at[block])
+
+    def final(block):
+        advance(second, block, turn)
+        at = pl.multiple_of(block * BLOCK, BLOCK)
+        bends = [bend_ref[k, pl.ds(at, BLOCK), :] for k in range(5)]
+        for f in range(freqs):
+            ring = [moved_ref[pl.ds((f * DIR + d) * slab_rows + at, BLOCK), :] for d in range(DIR)]
+            for d in range(DIR):
+                bent = bends[2] * ring[d]
+                for k in (0, 1, 3, 4):
+                    bent = bent + bends[k] * ring[(d + k - 2) % DIR]
+                done_ref[f * DIR + d, pl.ds(at, BLOCK), :] = bent
+        copy_out(block).start()
+
+    def sweep(one_block):
+        def body(step, carry):
+            for i in range(PER_STEP):
+                one_block(step * PER_STEP + i)
+            return carry
+
+        lax.fori_loop(0, slab_rows // BLOCK // PER_STEP, body, 0)
+
+    sweep(lambda block: advance(first, block, store))
+    sweep(final)
+    for block in range(slab_rows // BLOCK):
+        copy_out(block).wait()
+
+
+def slab_plan(spectra, wind, growth, damping, row_cell, land_mask, group_speed, current, turning):
+    parts = lax.axis_size(GROUP)
+    rows, comps = spectra.shape
+    tile_rows = turning.shape[0]
+    freqs = comps // parts // DIR
+    width = freqs * DIR
+    full = rows // LANES
+    slab_rows = parts * tile_rows
+    depth = parts * rows
+    highs = slab_rows // 2
+    small_rows = group_speed.shape[0] * tile_rows + 8 * -(-(4 * tile_rows + full + 1) // 8)
+    megabyte = 1024 * 1024
+    vmem = pl.BlockSpec(memory_space=pltpu.VMEM)
+    packed, small = pl.pallas_call(
+        functools.partial(pack_kernel, parts, freqs),
+        out_shape=[
+            pltpu.VMEM((parts, full * width + DIR, LANES), jnp.float32),
+            jax.ShapeDtypeStruct((small_rows, LANES), jnp.float32),
+        ],
+        compiler_params=pltpu.CompilerParams(vmem_limit_bytes=56 * megabyte),
+        name="pack",
+    )(spectra, wind, growth, damping, row_cell, land_mask, group_speed, current, turning)
+    gathered = lax.all_gather(small, GROUP, axis=0, tiled=True)
+    arrived = lax.all_to_all(packed, GROUP, split_axis=0, concat_axis=0, tiled=True)
+    me = lax.axis_index(GROUP).astype(jnp.int32)[None]
+    prepared = pl.pallas_call(
+        functools.partial(prepare_kernel, parts, tile_rows, full, freqs),
+        out_shape=[
+            pltpu.VMEM((2 * LANES, depth), jnp.bfloat16),
+            pltpu.VMEM((highs, 16, depth), jnp.bfloat16),
+            pltpu.VMEM((9, freqs, slab_rows, DIR, LANES), jnp.float32),
+            pltpu.VMEM((5, slab_rows, LANES), jnp.float32),
+        ],
+        in_specs=[pl.BlockSpec(memory_space=pltpu.SMEM), vmem],
+        scratch_shapes=[pltpu.VMEM((8 + 3 * freqs, slab_rows + 16, LANES), jnp.float32)],
+        cost_estimate=pl.CostEstimate(flops=60 * 1000 * 1000, bytes_accessed=8 * megabyte, transcendentals=0),
+        compiler_params=pltpu.CompilerParams(vmem_limit_bytes=16 * megabyte),
+        name="prepare",
+    )(me, gathered)
+    out = pl.pallas_call(
+        functools.partial(slab_kernel, parts, tile_rows, full, freqs),
+        out_shape=jax.ShapeDtypeStruct((width, slab_rows, LANES), jnp.float32),
+        in_specs=[vmem] * 5,
+        out_specs=pl.BlockSpec(memory_space=pl.ANY),
+        scratch_shapes=[
+            pltpu.VMEM((highs * 2 * width, depth), jnp.bfloat16),
+            pltpu.VMEM((freqs, slab_rows + 4, DIR, LANES), jnp.float32),
+            pltpu.VMEM((freqs, slab_rows + 4, DIR, LANES), jnp.float32),
+            pltpu.VMEM((width * slab_rows, LANES), jnp.float32),
+            pltpu.VMEM((width, slab_rows, LANES), jnp.float32),
+            pltpu.SemaphoreType.DMA((slab_rows // BLOCK,)),
+        ],
+        compiler_params=pltpu.CompilerParams(vmem_limit_bytes=32 * megabyte),
+        name="slab",
+    )(arrived, *prepared)
+    return out.reshape(1, width, slab_rows, LANES)
+
+
+def shards(*arrays):
+    spectra, land_mask = arrays[0], arrays[5]
+    parts = lax.axis_size(GROUP)
+    rows, comps = spectra.shape
+    whole_frequencies = comps == parts * 2 * DIR
+    fits = rows % LANES == LANES // 2 and land_mask.shape == (4, LANES) and parts % 2 == 0
+    if whole_frequencies and fits:
+        return slab_plan(*arrays)
+    return tile_plan(*arrays)
 
 
 def solution(mesh):

time: 207 us -> 61.6 us (0.30); the launches traced: 205 us -> 61.3 us
  local copies, waits for them, and re-layouts: 98 us -> 5.92 us
  waiting for transfers between devices: 37.7 us -> 0.01 us
  starting transfers between devices: 31.8 us -> 7.25 us
  Pallas kernels: 0 us -> 10.6 us
  blocking collectives: 27.7 us -> 37.5 us
  other arithmetic: 8.99 us -> 0 us
    scatter x3 -> x0, local copies, waits for them, and re-layouts: 90.7 us -> none  [the longest x2 87.7 us: bucket(): jnp.full(shape_out, filler, jnp.float32).at[target, bucket_slot].set(values)]
    all_gather x0 -> x1, blocking collectives: none -> 37.5 us  [slab_plan(): gathered = lax.all_gather(small, GROUP, axis=0, tiled=True)]
    ppermute x6 -> x0, waiting for transfers between devices: 29.9 us -> none  [the longest x3 18.2 us: with_halo(): lax.ppermute(tail, axis, [(i, (i + 1) % count) for i in range(ends)])]
    all_to_all x1 -> x0, blocking collectives: 27.7 us -> none  [shards(): lax.all_to_all(spectrum, ('pts', 'comp'), split_axis=0, concat_axis=1, ti...]
    ppermute x6 -> x0, starting transfers between devices: 18 us -> none  [the longest x3 14.2 us: with_halo(): lax.ppermute(tail, axis, [(i, (i + 1) % count) for i in range(ends)])]
    pallas_call x0 -> x3, Pallas kernels: none -> 10.6 us  [the longest x1 5.54 us: slab_plan(): pl.pallas_call(functools.partial(slab_kernel, parts, tile_rows, full, fre...]
    all_to_all x2 -> x1, waiting for transfers between devices: 7.78 us -> 0.01 us  [slab_plan(): lax.all_to_all(packed, GROUP, split_axis=0, concat_axis=0, tiled=True)]
    all_to_all x2 -> x1, starting transfers between devices: 13.8 us -> 7.25 us  [slab_plan(): lax.all_to_all(packed, GROUP, split_axis=0, concat_axis=0, tiled=True)]
  transfers between devices with their start and end apart: 8 -> 1, of which waited for: 6 -> 0; matrix products, arithmetic and copies ran while one was open for 23% -> 0% of each run, Pallas kernels for 0% -> 5%
where the time goes in v7:
time: 61.6 us; the launch traced here: 61.3 us
  blocking collectives  37.5 us (61%)
  Pallas kernels  10.6 us (17%)
  starting transfers between devices  7.25 us (12%)
  local copies, waits for them, and re-layouts  5.92 us (10%)
    all_gather x1, blocking collectives, slab_plan(): gathered = lax.all_gather(small, GROUP, axis=0, tiled=True)  37.5 us
    all_to_all x1, starting transfers between devices, slab_plan(): lax.all_to_all(packed, GROUP, split_axis=0, concat_axis=0, tiled=True)  7.25 us
    unnamed x4, local copies, waits for them, and re-layouts  5.92 us
    pallas_call x1, Pallas kernels, slab_plan(): pl.pallas_call(functools.partial(slab_kernel, parts, tile_rows, full, fre...  5.54 us
    pallas_call x1, Pallas kernels, slab_plan(): pl.pallas_call(functools.partial(prepare_kernel, parts, tile_rows, full,...  2.83 us
    pallas_call x1, Pallas kernels, slab_plan(): pl.pallas_call(functools.partial(pack_kernel, parts, freqs), out_shape=[p...  2.2 us
  transfers between devices with their start and end apart: 1, of which 0 were waited for; matrix products, arithmetic and copies ran while one was open for 0% of the time, Pallas kernels for 5%

profile of v7, /device:TPU:0, one launch (start us, length us, event | category | flops | bytes accessed | tf_op | source)
XLA Modules:
  0.0 61.3 jit_solution(15599477354749433449)
XLA Ops:
  0.0 2.2 %pack.1 = (f32[8,120,128]{2,1,0:T(8,128)}, f32[88,128]{1,0:T(8,128)}) custom-call(f32[320,384]{1,0:T(8,128)} %spectra_ref.1, f32[320]{0:T(512)} %wind_ref.1, f32[384]{0:T(512)} %growth_ref.1, f32[384]{0:T(512)} %damping_ref.1, s32[320]{0:T(512)} %cell_ref.1, s32[4,128]{1,0:T(4,128)} %land_ref.1, f32[16,4,128]{2,1,0:T(4,128)} %speed_ref.1, ...), custom_call_target="tpu_custom_call" | custom-call | tf_op jit(solution)/shard_map/pack/pallas_call | solution.py:482
  2.2 7.3 %all-to-all-start = ((f32[8,120,128]{2,1,0:T(8,128)}), f32[8,120,128]{2,1,0:T(8,128)S(1)}, u32[]{:S(2)}, u32[]{:S(2)}) async-start(f32[8,120,128]{2,1,0:T(8,128)} %get-tuple-element.11), calls=%async_computation | async-start | bytes 983040 | tf_op jit(solution)/shard_map/all_to_all | solution.py:492
  9.5 37.5 %all_gather.3.small_ref = f32[704,128]{1,0:T(8,128)S(1)} all-gather(f32[88,128]{1,0:T(8,128)} %get-tuple-element.12), channel_id=1, replica_groups=mesh['groups'=2,'pts'=4,'comp'=2,'sub'=2] {'pts','comp'}, dimensions={0}, use_global_device_ids=true | all-gather | bytes 405504 | tf_op jit(solution)/shard_map/all_gather | solution.py:491
  47.0 2.8 %prepare.1 = (bf16[256,2560]{1,0:T(8,128)(2,1)S(1)}, bf16[16,16,2560]{2,1,0:T(8,128)(2,1)S(1)}, f32[9,2,32,24,128]{4,3,2,1,0:T(8,128)S(1)}, f32[5,32,128]{2,1,0:T(8,128)S(1)}) custom-call(s32[1]{0:T(128)} %bitcast.me_ref, f32[704,128]{1,0:T(8,128)S(1)} %all_gather.3.small_ref), custom_call_target="tpu_custom_call" | custom-call | flops 60000000 | bytes 8388608 | tf_op jit(solution)/shard_map/prepare/pallas_call | solution.py:494
  49.8 0.0 copy-start
  49.8 2.9 %copy-done = f32[9,2,32,24,128]{4,3,2,1,0:T(8,128)} copy-done((f32[9,2,32,24,128]{4,3,2,1,0:T(8,128)}, f32[9,2,32,24,128]{4,3,2,1,0:T(8,128)S(1)}, u32[]{:S(2)}) %copy-start) | copy-done | bytes 7077912
  52.8 0.0 all-to-all-done.recv_ref
  52.8 0.0 copy-start.1
  52.8 3.0 %copy-done.1 = f32[9,2,32,24,128]{4,3,2,1,0:T(8,128)S(1)} copy-done((f32[9,2,32,24,128]{4,3,2,1,0:T(8,128)S(1)}, f32[9,2,32,24,128]{4,3,2,1,0:T(8,128)}, u32[]{:S(2)}) %copy-start.1) | copy-done | bytes 7077912
  55.8 5.5 %slab.1 = f32[48,32,128]{2,1,0:T(8,128)} custom-call(f32[8,120,128]{2,1,0:T(8,128)S(1)} %all-to-all-done.recv_ref, bf16[256,2560]{1,0:T(8,128)(2,1)S(1)} %get-tuple-element.13.onehot_ref, bf16[16,16,2560]{2,1,0:T(8,128)(2,1)S(1)} %get-tuple-element.14.pick_ref, f32[9,2,32,24,128]{4,3,2,1,0:T(8,128)S(1)} %copy-done.1, ...), custom_call_target="tpu_custom_call" | custom-call | tf_op jit(solution)/shard_map/slab/pallas_call | solution.py:508
Async XLA Ops:
  2.2 50.6 %all-to-all-start = ((f32[8,120,128]{2,1,0:T(8,128)}), f32[8,120,128]{2,1,0:T(8,128)S(1)}, u32[]{:S(2)}, u32[]{:S(2)}) async-start(f32[8,120,128]{2,1,0:T(8,128)} %get-tuple-element.11), calls=%async_computation | async-start | bytes 983040 | tf_op jit(solution)/shard_map/all_to_all | solution.py:492
  49.8 2.9 %copy-start = (f32[9,2,32,24,128]{4,3,2,1,0:T(8,128)}, f32[9,2,32,24,128]{4,3,2,1,0:T(8,128)S(1)}, u32[]{:S(2)}) copy-start(f32[9,2,32,24,128]{4,3,2,1,0:T(8,128)S(1)} %get-tuple-element.15.weight_ref) | copy-start | bytes 21233668
  52.8 3.0 %copy-start.1 = (f32[9,2,32,24,128]{4,3,2,1,0:T(8,128)S(1)}, f32[9,2,32,24,128]{4,3,2,1,0:T(8,128)}, u32[]{:S(2)}) copy-start(f32[9,2,32,24,128]{4,3,2,1,0:T(8,128)} %copy-done) | copy-start | bytes 21233668

commit v8 on v6

--- a/solution.py
+++ b/solution.py
@@ -214,7 +214,6 @@
     recv_ref,
     out_ref,
     onehot,
-    spread,
     first,
     second,
     table,
@@ -239,6 +238,8 @@
     def cells_of(owner, chunk):
         return recv_ref[owner, pl.ds(shared_base + 3 * tile_rows + chunk, 1), :].astype(jnp.int32)
 
+    columns = []
+
     def place(index, cells, values):
         span = pl.ds(index * LANES, LANES)
         high = cells // (2 * LANES)
@@ -250,12 +251,12 @@
             head = value.astype(jnp.bfloat16).astype(jnp.float32)
             pieces += [head, value - head]
         both = jnp.concatenate(pieces, axis=0).astype(jnp.bfloat16)
+        column = []
         for h in range(highs):
             pick = jnp.broadcast_to((high == h).astype(jnp.float32), (width, LANES)).astype(jnp.bfloat16)
-            spread[pl.ds(h * width, width), span] = both * pick
-        spread[pl.ds(highs * width, highs), span] = (
-            (high_iota == high).astype(jnp.float32).astype(jnp.bfloat16)
-        )
+            column.append(both * pick)
+        column.append((high_iota == high).astype(jnp.float32).astype(jnp.bfloat16))
+        columns.append(jnp.concatenate(column, axis=0))
 
     per_pair = 2 * full + 1
     for pair in range(parts // 2):
@@ -285,7 +286,10 @@
         place(pair * per_pair + 2 * full, cells, values)
 
     scattered = lax.dot_general(
-        spread[...], onehot[...], (((1,), (1,)), ((), ())), preferred_element_type=jnp.float32
+        jnp.concatenate(columns, axis=1),
+        onehot[...],
+        (((1,), (1,)), ((), ())),
+        preferred_element_type=jnp.float32,
     )
     nothing = jnp.zeros((DIR, LANES), jnp.float32)
     for f in range(freqs):
@@ -464,7 +468,6 @@
         out_specs=pl.BlockSpec(memory_space=pl.ANY),
         scratch_shapes=[
             pltpu.VMEM((2 * LANES, depth), jnp.bfloat16),
-            pltpu.VMEM((highs * (freqs * 2 * DIR + 1), depth), jnp.bfloat16),
             pltpu.VMEM((freqs, slab_rows + 4, DIR, LANES), jnp.float32),
             pltpu.VMEM((freqs, slab_rows + 4, DIR, LANES), jnp.float32),
             pltpu.VMEM((10 + 3 * freqs, slab_rows + 16, LANES), jnp.float32),

time: 31.8 us -> 31.6 us (level)
  no operation moved by 1% of the time
where the time goes in v8:
time: 31.6 us; the launch traced here: 31.4 us
  blocking collectives  23.6 us (75%)
  Pallas kernels  7.8 us (25%)
    all_to_all x1, blocking collectives, slab_plan(): lax.all_to_all(packed, GROUP, split_axis=0, concat_axis=0, tiled=True)  23.6 us
    pallas_call x1, Pallas kernels, slab_plan(): pl.pallas_call(functools.partial(slab_kernel, parts, tile_rows, full, fre...  6.4 us
    pallas_call x1, Pallas kernels, slab_plan(): pl.pallas_call(functools.partial(pack_kernel, parts, freqs), out_shape=pl...  1.4 us

profile of v8, /device:TPU:0, one launch (start us, length us, event | category | flops | bytes accessed | tf_op | source)
XLA Modules:
  0.0 31.4 jit_solution(4025788936671228397)
XLA Ops:
  0.0 1.4 %pack.1 = f32[8,144,128]{2,1,0:T(8,128)S(1)} custom-call(f32[320,384]{1,0:T(8,128)} %spectra_ref.1, f32[320]{0:T(512)} %wind_ref.1, f32[384]{0:T(512)} %growth_ref.1, f32[384]{0:T(512)} %damping_ref.1, s32[320]{0:T(512)} %cell_ref.1, f32[16,4,128]{2,1,0:T(4,128)} %speed_ref.1, f32[2,4,128]{2,1,0:T(4,128)} %current_ref.1, f32[4,128]{1,0:T(4,128)} %turning_ref.1), custom_call_target="tpu_custom_call" | custom-call | tf_op jit(solution)/shard_map/pack/pallas_call | solution.py:457
  1.4 23.6 %all_to_all.5.recv_ref = f32[8,144,128]{2,1,0:T(8,128)S(1)} all-to-all(f32[8,144,128]{2,1,0:T(8,128)S(1)} %pack.1), channel_id=1, replica_groups=mesh['groups'=2,'pts'=4,'comp'=2,'sub'=2] {'pts','comp'}, dimensions={0} | all-to-all | bytes 1179648 | tf_op jit(solution)/shard_map/all_to_all | solution.py:463
  25.0 6.4 %slab.1 = f32[48,32,128]{2,1,0:T(8,128)} custom-call(f32[8,144,128]{2,1,0:T(8,128)S(1)} %all_to_all.5.recv_ref), custom_call_target="tpu_custom_call" | custom-call | tf_op jit(solution)/shard_map/slab/pallas_call | solution.py:464

commit v9 on v8

--- a/solution.py
+++ b/solution.py
@@ -157,13 +157,35 @@
     rows, comps = spectra_ref.shape
     half = LANES // 2
     full = rows // LANES
-    spare = jnp.zeros((1, half), jnp.float32)
-    wind_row = jnp.concatenate([wind_ref[...][None], spare], axis=1)
-    wind_cols = jnp.broadcast_to(wind_row, (LANES, rows + half)).T
+    padded = (full + 1) * LANES
     low = lax.broadcasted_iota(jnp.int32, (8, LANES), 1) < half
     per_freq = DIR // 8
     span_rows = full * DIR + 16
-    tails = []
+
+    def extended(row, filler):
+        return jnp.concatenate([row[None], jnp.full((1, half), filler, jnp.float32)], axis=1)
+
+    def as_columns(row):
+        return jnp.broadcast_to(row, (LANES, padded)).T
+
+    cells = cell_ref[...].astype(jnp.float32)
+    keys = extended(cells, 1e9)
+    key_cols = as_columns(keys)
+    ranks = jnp.concatenate(
+        [
+            jnp.sum(
+                jnp.where(key_cols < keys[:, c * LANES : (c + 1) * LANES], 1.0, 0.0), axis=0, keepdims=True
+            )
+            for c in range(full + 1)
+        ],
+        axis=1,
+    )
+    place = lax.broadcasted_iota(jnp.int32, (padded, padded), 0)
+    place = jnp.where(place < rows, place, place - half).astype(jnp.float32)
+    order = jnp.where(place == ranks, 1.0, 0.0).astype(jnp.bfloat16)
+
+    wind_cols = as_columns(extended(wind_ref[...], 0.0))
+    turned = []
     for block in range(comps // LANES):
         lanes = pl.ds(block * LANES, LANES)
         growth = growth_ref[lanes][None]
@@ -175,27 +197,36 @@
                 wind_cols[first : first + count] * growth - damping
             )
 
-        for chunk in range(full):
-            turned = source(chunk * LANES, LANES).T
-            for g in range(LANES // 8):
-                freq, within = divmod(block * (LANES // 8) + g, per_freq)
-                part, f = divmod(freq, freqs)
-                at = f * span_rows + chunk * DIR + within * 8
-                out_ref[part, pl.ds(at, 8), :] = turned[g * 8 : g * 8 + 8]
-        tail = source(full * LANES, half)
-        turned = jnp.concatenate([tail, tail], axis=0).T
-        tails += [turned[g * 8 : g * 8 + 8] for g in range(LANES // 8)]
-    cell_row = jnp.concatenate([cell_ref[...].astype(jnp.float32)[None], spare], axis=1)
+        pieces = [source(c * LANES, LANES).T for c in range(full)]
+        last = jnp.concatenate([source(full * LANES, half), jnp.zeros((half, LANES), jnp.float32)], axis=0)
+        turned.append(jnp.concatenate(pieces + [last.T], axis=1))
+    turned.append(jnp.broadcast_to(extended(cells, 0.0), (16, padded)))
+    values = jnp.concatenate(turned, axis=0)
+    head = values.astype(jnp.bfloat16)
+    rest = (values - head.astype(jnp.float32)).astype(jnp.bfloat16)
+    both = lax.dot_general(
+        jnp.concatenate([head, rest], axis=0),
+        order,
+        (((1,), (1,)), ((), ())),
+        preferred_element_type=jnp.float32,
+    )
+
+    def piece(first, count, chunk):
+        lanes = slice(chunk * LANES, (chunk + 1) * LANES)
+        return both[first : first + count, lanes] + both[comps + 16 + first : comps + 16 + first + count, lanes]
+
     shared = jnp.concatenate(
-        [current_ref[0], current_ref[1], turning_ref[...]]
-        + [cell_row[:, c * LANES : (c + 1) * LANES] for c in range(full + 1)],
+        [current_ref[0], current_ref[1], turning_ref[...]] + [piece(comps, 1, c) for c in range(full + 1)],
         axis=0,
     )
     for part in range(parts):
         for f in range(freqs):
             freq = part * freqs + f
-            one, two, three = tails[freq * per_freq : (freq + 1) * per_freq]
-            at = f * span_rows + full * DIR
+            at = f * span_rows
+            for chunk in range(full):
+                out_ref[part, pl.ds(at + chunk * DIR, DIR), :] = piece(freq * DIR, DIR, chunk)
+            at += full * DIR
+            one, two, three = (piece(freq * DIR + g * 8, 8, full) for g in range(per_freq))
             out_ref[part, pl.ds(at, 8), :] = jnp.where(low, one, two)
             folded = jnp.where(low, three, pltpu.roll(three, 4, 0))
             out_ref[part, pl.ds(at + 8, 8), :] = jnp.concatenate([folded[:4], speed_ref[freq]], axis=0)
@@ -238,10 +269,22 @@
     def cells_of(owner, chunk):
         return recv_ref[owner, pl.ds(shared_base + 3 * tile_rows + chunk, 1), :].astype(jnp.int32)
 
-    columns = []
-
-    def place(index, cells, values):
-        span = pl.ds(index * LANES, LANES)
+    owner_rows = full * LANES + half
+    capacity = tile_rows * LANES // parts
+    spans = []
+    for chunk in range(full + 1):
+        begin, end = chunk * LANES, min((chunk + 1) * LANES, owner_rows)
+        tiles = [
+            t
+            for t in range(parts)
+            if owner_rows - capacity * (parts - t) < end and capacity * (t + 1) > begin
+        ]
+        spans.append(range(tiles[0] * tile_rows // 2, (tiles[-1] + 1) * tile_rows // 2))
+    offsets = [parts * LANES * chunk for chunk in range(full + 1)]
+    columns = [[] for _ in spans]
+
+    def place(chunk, cells, values):
+        span = pl.ds(offsets[chunk] + len(columns[chunk]) * LANES, LANES)
         high = cells // (2 * LANES)
         low = (cells - high * (2 * LANES)).astype(jnp.float32)
         low = jnp.broadcast_to(low, (2 * LANES, LANES)).astype(jnp.bfloat16)
@@ -252,21 +295,20 @@
             pieces += [head, value - head]
         both = jnp.concatenate(pieces, axis=0).astype(jnp.bfloat16)
         column = []
-        for h in range(highs):
+        for h in spans[chunk]:
             pick = jnp.broadcast_to((high == h).astype(jnp.float32), (width, LANES)).astype(jnp.bfloat16)
             column.append(both * pick)
         column.append((high_iota == high).astype(jnp.float32).astype(jnp.bfloat16))
-        columns.append(jnp.concatenate(column, axis=0))
-
-    per_pair = 2 * full + 1
+        columns[chunk].append(jnp.concatenate(column, axis=0))
+
     for pair in range(parts // 2):
         even, odd = 2 * pair, 2 * pair + 1
-        for side, owner in enumerate((even, odd)):
+        for owner in (even, odd):
             for chunk in range(full):
                 values = [
                     recv_ref[owner, pl.ds(f * span_rows + chunk * DIR, DIR), :] for f in range(freqs)
                 ]
-                place(pair * per_pair + side * full + chunk, cells_of(owner, chunk), values)
+                place(chunk, cells_of(owner, chunk), values)
 
         def merged(offset):
             own, other = recv_ref[even, pl.ds(offset, 8), :], recv_ref[odd, pl.ds(offset, 8), :]
@@ -282,25 +324,32 @@
             values.append(
                 jnp.concatenate([one, two, jnp.where(top_rows, three, pltpu.roll(four, 4, 0))], axis=0)
             )
-        cells = jnp.where(low_lane, cells_of(even, full), pltpu.roll(cells_of(odd, full), half, 1))
-        place(pair * per_pair + 2 * full, cells, values)
-
-    scattered = lax.dot_general(
-        jnp.concatenate(columns, axis=1),
-        onehot[...],
-        (((1,), (1,)), ((), ())),
-        preferred_element_type=jnp.float32,
-    )
+        place(full, jnp.where(low_lane, cells_of(even, full), cells_of(odd, full)), values)
+
+    scattered = [
+        lax.dot_general(
+            jnp.concatenate(column, axis=1),
+            onehot[:, pl.ds(offset, len(column) * LANES)],
+            (((1,), (1,)), ((), ())),
+            preferred_element_type=jnp.float32,
+        )
+        for offset, column in zip(offsets, columns)
+    ]
     nothing = jnp.zeros((DIR, LANES), jnp.float32)
     for f in range(freqs):
         for field in (first, second):
             for edge in (0, 1, slab_rows + 2, slab_rows + 3):
                 field[f, edge] = nothing
         for h in range(highs):
-            at = h * width + f * 2 * DIR
-            total = scattered[at : at + DIR] + scattered[at + DIR : at + 2 * DIR]
+            terms = []
+            for span, product in zip(spans, scattered):
+                if h in span:
+                    at = (h - span[0]) * width + f * 2 * DIR
+                    terms += [product[at : at + DIR], product[at + DIR : at + 2 * DIR]]
+            total = sum(terms[1:], terms[0])
             first[f, 2 * h + 2] = total[:, :LANES]
             first[f, 2 * h + 3] = total[:, LANES:]
+    named = sum(product[len(span) * width :] for span, product in zip(spans, scattered))
 
     lane = lax.broadcasted_iota(jnp.int32, (slab_rows, LANES), 1)
     zero_rows = jnp.zeros((8, LANES), jnp.float32)
@@ -336,7 +385,6 @@
     current_x, current_y, turning = (gather(shared_base + kind * tile_rows) for kind in range(3))
     current_x_face, speed_x_face = face_x(current_x), [face_x(s) for s in speeds]
     current_y_faces, speed_y_faces = face_y(current_y), [face_y(s) for s in speeds]
-    named = scattered[highs * width : highs * width + highs]
     land_slots = keep(named[:, :LANES]), keep(named[:, LANES:])
     ahead = jnp.maximum(turning, 0.0) * 0.125
     back = jnp.minimum(turning, 0.0) * 0.125

time: 31.6 us -> 31.1 us (0.984)
  Pallas kernels: 7.8 us -> 7.31 us
    pallas_call x1, Pallas kernels: 6.4 us -> 5.5 us  [slab_plan(): pl.pallas_call(functools.partial(slab_kernel, parts, tile_rows, full, fre...]
    pallas_call x1, Pallas kernels: 1.4 us -> 1.81 us  [slab_plan(): pl.pallas_call(functools.partial(pack_kernel, parts, freqs), out_shape=pl...]
where the time goes in v9:
time: 31.1 us; the launch traced here: 30.9 us
  blocking collectives  23.6 us (76%)
  Pallas kernels  7.31 us (24%)
    all_to_all x1, blocking collectives, slab_plan(): lax.all_to_all(packed, GROUP, split_axis=0, concat_axis=0, tiled=True)  23.6 us
    pallas_call x1, Pallas kernels, slab_plan(): pl.pallas_call(functools.partial(slab_kernel, parts, tile_rows, full, fre...  5.5 us
    pallas_call x1, Pallas kernels, slab_plan(): pl.pallas_call(functools.partial(pack_kernel, parts, freqs), out_shape=pl...  1.81 us

profile of v9, /device:TPU:0, one launch (start us, length us, event | category | flops | bytes accessed | tf_op | source)
XLA Modules:
  0.0 30.9 jit_solution(6390387604163882270)
XLA Ops:
  0.0 1.8 %pack.1 = f32[8,144,128]{2,1,0:T(8,128)S(1)} custom-call(f32[320,384]{1,0:T(8,128)} %spectra_ref.1, f32[320]{0:T(512)} %wind_ref.1, f32[384]{0:T(512)} %growth_ref.1, f32[384]{0:T(512)} %damping_ref.1, s32[320]{0:T(512)} %cell_ref.1, f32[16,4,128]{2,1,0:T(4,128)} %speed_ref.1, f32[2,4,128]{2,1,0:T(4,128)} %current_ref.1, f32[4,128]{1,0:T(4,128)} %turning_ref.1), custom_call_target="tpu_custom_call" | custom-call | tf_op jit(solution)/shard_map/pack/pallas_call | solution.py:505
  1.8 23.6 %all_to_all.5.recv_ref = f32[8,144,128]{2,1,0:T(8,128)S(1)} all-to-all(f32[8,144,128]{2,1,0:T(8,128)S(1)} %pack.1), channel_id=1, replica_groups=mesh['groups'=2,'pts'=4,'comp'=2,'sub'=2] {'pts','comp'}, dimensions={0} | all-to-all | bytes 1179648 | tf_op jit(solution)/shard_map/all_to_all | solution.py:511
  25.4 5.5 %slab.1 = f32[48,32,128]{2,1,0:T(8,128)} custom-call(f32[8,144,128]{2,1,0:T(8,128)S(1)} %all_to_all.5.recv_ref), custom_call_target="tpu_custom_call" | custom-call | tf_op jit(solution)/shard_map/slab/pallas_call | solution.py:512

commit v10 on v9

--- a/solution.py
+++ b/solution.py
@@ -181,6 +181,9 @@
         axis=1,
     )
     place = lax.broadcasted_iota(jnp.int32, (padded, padded), 0)
+    odd = lax.axis_index(GROUP) % 2 == 1
+    swapped = jnp.where(place % LANES < half, place + half, place - half)
+    place = jnp.where((place < full * LANES) & odd, swapped, place)
     place = jnp.where(place < rows, place, place - half).astype(jnp.float32)
     order = jnp.where(place == ranks, 1.0, 0.0).astype(jnp.bfloat16)
 
@@ -262,6 +265,7 @@
     width = freqs * 2 * DIR
     low_lane = lax.broadcasted_iota(jnp.int32, (1, LANES), 1) < half
     low_lanes = lax.broadcasted_iota(jnp.int32, (8, LANES), 1) < half
+    low_wide = lax.broadcasted_iota(jnp.int32, (DIR, LANES), 1) < half
     top_rows = lax.broadcasted_iota(jnp.int32, (8, LANES), 0) < 4
     cell_iota = lax.broadcasted_iota(jnp.int32, (2 * LANES, LANES), 0).astype(jnp.float32).astype(jnp.bfloat16)
     high_iota = lax.broadcasted_iota(jnp.int32, (highs, LANES), 0)
@@ -272,15 +276,14 @@
     owner_rows = full * LANES + half
     capacity = tile_rows * LANES // parts
     spans = []
-    for chunk in range(full + 1):
-        begin, end = chunk * LANES, min((chunk + 1) * LANES, owner_rows)
+    for begin in range(0, owner_rows, half):
         tiles = [
             t
             for t in range(parts)
-            if owner_rows - capacity * (parts - t) < end and capacity * (t + 1) > begin
+            if owner_rows - capacity * (parts - t) < begin + half and capacity * (t + 1) > begin
         ]
         spans.append(range(tiles[0] * tile_rows // 2, (tiles[-1] + 1) * tile_rows // 2))
-    offsets = [parts * LANES * chunk for chunk in range(full + 1)]
+    offsets = [parts // 2 * LANES * chunk for chunk in range(len(spans))]
     columns = [[] for _ in spans]
 
     def place(chunk, cells, values):
@@ -303,12 +306,19 @@
 
     for pair in range(parts // 2):
         even, odd = 2 * pair, 2 * pair + 1
-        for owner in (even, odd):
-            for chunk in range(full):
-                values = [
-                    recv_ref[owner, pl.ds(f * span_rows + chunk * DIR, DIR), :] for f in range(freqs)
-                ]
-                place(chunk, cells_of(owner, chunk), values)
+        for chunk in range(full):
+            here, there = (
+                [recv_ref[owner, pl.ds(f * span_rows + chunk * DIR, DIR), :] for f in range(freqs)]
+                for owner in (even, odd)
+            )
+            cells, cells_there = cells_of(even, chunk), cells_of(odd, chunk)
+            for side in range(2):
+                place(
+                    2 * chunk + side,
+                    jnp.where(low_lane, cells, cells_there),
+                    [jnp.where(low_wide, a, b) for a, b in zip(here, there)],
+                )
+                here, there, cells, cells_there = there, here, cells_there, cells
 
         def merged(offset):
             own, other = recv_ref[even, pl.ds(offset, 8), :], recv_ref[odd, pl.ds(offset, 8), :]
@@ -324,7 +334,62 @@
             values.append(
                 jnp.concatenate([one, two, jnp.where(top_rows, three, pltpu.roll(four, 4, 0))], axis=0)
             )
-        place(full, jnp.where(low_lane, cells_of(even, full), cells_of(odd, full)), values)
+        place(2 * full, jnp.where(low_lane, cells_of(even, full), cells_of(odd, full)), values)
+
+    lane = lax.broadcasted_iota(jnp.int32, (slab_rows, LANES), 1)
+    zero_rows = jnp.zeros((8, LANES), jnp.float32)
+
+    def gather(offset):
+        return jnp.concatenate(
+            [recv_ref[owner, pl.ds(offset, tile_rows), :] for owner in range(parts)], axis=0
+        )
+
+    gain = 0.5 * courant / 8.0
+    slots = iter(range(table.shape[0]))
+
+    def keep(rows):
+        slot = next(slots)
+        table[slot, pl.ds(8, rows.shape[0]), :] = rows
+        return slot
+
+    def face_x(rows):
+        slot = next(slots)
+        table[slot, pl.ds(0, 8), :] = zero_rows
+        table[slot, pl.ds(8 + slab_rows, 8), :] = zero_rows
+        table[slot, pl.ds(8, slab_rows), :] = rows
+        faces = gain * (table[slot, pl.ds(7, slab_rows + 8), :] + table[slot, pl.ds(8, slab_rows + 8), :])
+        table[slot, pl.ds(7, slab_rows + 8), :] = faces
+        return slot
+
+    def face_y(rows):
+        after = jnp.where(lane < LANES - 1, pltpu.roll(rows, LANES - 1, 1), 0.0)
+        before = jnp.where(lane > 0, pltpu.roll(rows, 1, 1), 0.0)
+        return keep(gain * (rows + after)), keep(gain * (rows + before))
+
+    speeds = [gather(f * span_rows + full * DIR + 12) for f in range(freqs)]
+    current_x, current_y, turning = (gather(shared_base + kind * tile_rows) for kind in range(3))
+    current_x_face, speed_x_face = face_x(current_x), [face_x(s) for s in speeds]
+    current_y_faces, speed_y_faces = face_y(current_y), [face_y(s) for s in speeds]
+    step_angle = 2.0 * math.pi / DIR
+    sublane = lax.broadcasted_iota(jnp.int32, (8, LANES), 0)
+    cosine0 = jnp.ones((8, LANES), jnp.float32)
+    sine0 = jnp.zeros((8, LANES), jnp.float32)
+    for d in range(1, 8):
+        cosine0 = jnp.where(sublane == d, math.cos(d * step_angle), cosine0)
+        sine0 = jnp.where(sublane == d, math.sin(d * step_angle), sine0)
+    turns = [(math.cos(g * 8 * step_angle), math.sin(g * 8 * step_angle)) for g in range(DIR // 8)]
+    cosine = jnp.concatenate([c * cosine0 - t * sine0 for c, t in turns], axis=0)
+    sine = jnp.concatenate([c * sine0 + t * cosine0 for c, t in turns], axis=0)
+
+    def row(slot, x):
+        return table[slot, pl.ds(8 + x, 1), :]
+
+    for f in range(freqs):
+        for x in range(-1, slab_rows):
+            faces_x[f, x + 1] = row(speed_x_face[f], x) * cosine + row(current_x_face, x)
+        for x in range(slab_rows):
+            for side in range(2):
+                faces_y[f, side, x] = row(speed_y_faces[f][side], x) * sine + row(current_y_faces[side], x)
 
     scattered = [
         lax.dot_general(
@@ -351,40 +416,6 @@
             first[f, 2 * h + 3] = total[:, LANES:]
     named = sum(product[len(span) * width :] for span, product in zip(spans, scattered))
 
-    lane = lax.broadcasted_iota(jnp.int32, (slab_rows, LANES), 1)
-    zero_rows = jnp.zeros((8, LANES), jnp.float32)
-
-    def gather(offset):
-        return jnp.concatenate(
-            [recv_ref[owner, pl.ds(offset, tile_rows), :] for owner in range(parts)], axis=0
-        )
-
-    gain = 0.5 * courant / 8.0
-    slots = iter(range(table.shape[0]))
-
-    def keep(rows):
-        slot = next(slots)
-        table[slot, pl.ds(8, rows.shape[0]), :] = rows
-        return slot
-
-    def face_x(rows):
-        slot = next(slots)
-        table[slot, pl.ds(0, 8), :] = zero_rows
-        table[slot, pl.ds(8 + slab_rows, 8), :] = zero_rows
-        table[slot, pl.ds(8, slab_rows), :] = rows
-        faces = gain * (table[slot, pl.ds(7, slab_rows + 8), :] + table[slot, pl.ds(8, slab_rows + 8), :])
-        table[slot, pl.ds(7, slab_rows + 8), :] = faces
-        return slot
-
-    def face_y(rows):
-        after = jnp.where(lane < LANES - 1, pltpu.roll(rows, LANES - 1, 1), 0.0)
-        before = jnp.where(lane > 0, pltpu.roll(rows, 1, 1), 0.0)
-        return keep(gain * (rows + after)), keep(gain * (rows + before))
-
-    speeds = [gather(f * span_rows + full * DIR + 12) for f in range(freqs)]
-    current_x, current_y, turning = (gather(shared_base + kind * tile_rows) for kind in range(3))
-    current_x_face, speed_x_face = face_x(current_x), [face_x(s) for s in speeds]
-    current_y_faces, speed_y_faces = face_y(current_y), [face_y(s) for s in speeds]
     land_slots = keep(named[:, :LANES]), keep(named[:, LANES:])
     ahead = jnp.maximum(turning, 0.0) * 0.125
     back = jnp.minimum(turning, 0.0) * 0.125
@@ -399,13 +430,7 @@
         )
     ]
 
-    angles = lax.broadcasted_iota(jnp.int32, (DIR, LANES), 0).astype(jnp.float32) * (2.0 * math.pi / DIR)
-    cosine = jnp.cos(angles)
-    sine = jnp.sin(angles)
     lane_wide = lax.broadcasted_iota(jnp.int32, (DIR, LANES), 1)
-
-    def row(slot, x):
-        return table[slot, pl.ds(8 + x, 1), :]
 
     def flux(speed, behind, centre3, onward3, beyond):
         positive = speed > 0.0
@@ -413,17 +438,7 @@
         far = jnp.where(positive, behind, beyond)
         return speed * ((centre3 + onward3) + (near - far))
 
-    def advance(field, fresh, step, carry, finish):
-        def speed_x(f, x):
-            if fresh:
-                faces_x[f, x + 1] = row(speed_x_face[f], x) * cosine + row(current_x_face, x)
-            return faces_x[f, x + 1]
-
-        def speed_y(f, side, x):
-            if fresh:
-                faces_y[f, side, x] = row(speed_y_faces[f][side], x) * sine + row(current_y_faces[side], x)
-            return faces_y[f, side, x]
-
+    def advance(field, step, carry, finish):
         carry = list(carry)
         for i in range(BLOCK):
             x = step * BLOCK + i
@@ -432,22 +447,20 @@
                 entering, centre3 = carry[f]
                 centre = field[f, x + 2]
                 onward3 = 3.0 * field[f, x + 3]
-                leaving = flux(speed_x(f, x), field[f, x + 1], centre3, onward3, field[f, x + 4])
+                leaving = flux(faces_x[f, x + 1], field[f, x + 1], centre3, onward3, field[f, x + 4])
                 up1 = jnp.where(lane_wide < LANES - 1, pltpu.roll(centre, LANES - 1, 1), 0.0)
                 up2 = jnp.where(lane_wide < LANES - 2, pltpu.roll(centre, LANES - 2, 1), 0.0)
                 down1 = jnp.where(lane_wide > 0, pltpu.roll(centre, 1, 1), 0.0)
                 down2 = jnp.where(lane_wide > 1, pltpu.roll(centre, 2, 1), 0.0)
-                right = flux(speed_y(f, 0, x), down1, centre3, 3.0 * up1, up2)
-                left = flux(speed_y(f, 1, x), down2, 3.0 * down1, centre3, up1)
+                right = flux(faces_y[f, 0, x], down1, centre3, 3.0 * up1, up2)
+                left = flux(faces_y[f, 1, x], down2, 3.0 * down1, centre3, up1)
                 finish(f, x, (centre - (leaving - entering) - (right - left)) * sea)
                 carry[f] = leaving, onward3
         return tuple(carry)
 
-    def enter(field, fresh):
+    def enter(field):
         carry = []
         for f in range(freqs):
-            if fresh:
-                faces_x[f, 0] = row(speed_x_face[f], -1) * cosine + row(current_x_face, -1)
             start3 = 3.0 * field[f, 2]
             carry.append((flux(faces_x[f, 0], nothing, nothing, start3, field[f, 3]), start3))
         return tuple(carry)
@@ -465,7 +478,7 @@
         return pltpu.make_async_copy(done_ref.at[:, part, :], out_ref.at[:, part, :], sems.at[step])
 
     def final(block, carry):
-        carry = advance(second, False, block, carry, turn)
+        carry = advance(second, block, carry, turn)
         at = pl.multiple_of(block * BLOCK, BLOCK)
         weights = [table[slot, pl.ds(8 + at, BLOCK), :] for slot in bend_slots]
         for f in range(freqs):
@@ -486,8 +499,8 @@
 
         lax.fori_loop(0, slab_rows // BLOCK // PER_STEP, body, carry)
 
-    sweep(lambda block, carry: advance(first, True, block, carry, store), enter(first, True))
-    sweep(final, enter(second, False))
+    sweep(lambda block, carry: advance(first, block, carry, store), enter(first))
+    sweep(final, enter(second))
     for block in range(slab_rows // BLOCK):
         copy_out(block).wait()
 

time: 31.1 us -> 31.3 us (level)
  no operation moved by 1% of the time
where the time goes in v10:
time: 31.3 us; the launch traced here: 31.1 us
  blocking collectives  23.6 us (75%)
  Pallas kernels  7.43 us (24%)
    all_to_all x1, blocking collectives, slab_plan(): lax.all_to_all(packed, GROUP, split_axis=0, concat_axis=0, tiled=True)  23.6 us
    pallas_call x1, Pallas kernels, slab_plan(): pl.pallas_call(functools.partial(slab_kernel, parts, tile_rows, full, fre...  5.59 us
    pallas_call x1, Pallas kernels, slab_plan(): pl.pallas_call(functools.partial(pack_kernel, parts, freqs), out_shape=pl...  1.84 us

profile of v10, /device:TPU:0, one launch (start us, length us, event | category | flops | bytes accessed | tf_op | source)
XLA Modules:
  0.0 31.1 jit_solution(18240828252970050591)
XLA Ops:
  0.0 1.8 %pack.1 = f32[8,144,128]{2,1,0:T(8,128)S(1)} custom-call(f32[320,384]{1,0:T(8,128)} %spectra_ref.1, f32[320]{0:T(512)} %wind_ref.1, f32[384]{0:T(512)} %growth_ref.1, f32[384]{0:T(512)} %damping_ref.1, s32[320]{0:T(512)} %cell_ref.1, f32[16,4,128]{2,1,0:T(4,128)} %speed_ref.1, f32[2,4,128]{2,1,0:T(4,128)} %current_ref.1, f32[4,128]{1,0:T(4,128)} %turning_ref.1), custom_call_target="tpu_custom_call" | custom-call | tf_op jit(solution)/shard_map/pack/pallas_call | solution.py:518
  1.8 23.6 %all_to_all.5.recv_ref = f32[8,144,128]{2,1,0:T(8,128)S(1)} all-to-all(f32[8,144,128]{2,1,0:T(8,128)S(1)} %pack.1), channel_id=1, replica_groups=mesh['groups'=2,'pts'=4,'comp'=2,'sub'=2] {'pts','comp'}, dimensions={0} | all-to-all | bytes 1179648 | tf_op jit(solution)/shard_map/all_to_all | solution.py:524
  25.5 5.6 %slab.1 = f32[48,32,128]{2,1,0:T(8,128)} custom-call(f32[8,144,128]{2,1,0:T(8,128)S(1)} %all_to_all.5.recv_ref), custom_call_target="tpu_custom_call" | custom-call | tf_op jit(solution)/shard_map/slab/pallas_call | solution.py:525

commit v11 on v10

--- a/solution.py
+++ b/solution.py
@@ -237,7 +237,7 @@
 
 
 BLOCK = 8
-PER_STEP = 2
+PER_STEP = 4
 
 
 def slab_kernel(

time: 31.3 us -> 30.9 us (0.987)
  no operation moved by 1% of the time
where the time goes in v11:
time: 30.9 us; the launch traced here: 30.8 us
  blocking collectives  23.6 us (76%)
  Pallas kernels  7.12 us (23%)
    all_to_all x1, blocking collectives, slab_plan(): lax.all_to_all(packed, GROUP, split_axis=0, concat_axis=0, tiled=True)  23.6 us
    pallas_call x1, Pallas kernels, slab_plan(): pl.pallas_call(functools.partial(slab_kernel, parts, tile_rows, full, fre...  5.28 us
    pallas_call x1, Pallas kernels, slab_plan(): pl.pallas_call(functools.partial(pack_kernel, parts, freqs), out_shape=pl...  1.84 us

profile of v11, /device:TPU:0, one launch (start us, length us, event | category | flops | bytes accessed | tf_op | source)
XLA Modules:
  0.0 30.8 jit_solution(12833368083969003664)
XLA Ops:
  0.0 1.8 %pack.1 = f32[8,144,128]{2,1,0:T(8,128)S(1)} custom-call(f32[320,384]{1,0:T(8,128)} %spectra_ref.1, f32[320]{0:T(512)} %wind_ref.1, f32[384]{0:T(512)} %growth_ref.1, f32[384]{0:T(512)} %damping_ref.1, s32[320]{0:T(512)} %cell_ref.1, f32[16,4,128]{2,1,0:T(4,128)} %speed_ref.1, f32[2,4,128]{2,1,0:T(4,128)} %current_ref.1, f32[4,128]{1,0:T(4,128)} %turning_ref.1), custom_call_target="tpu_custom_call" | custom-call | tf_op jit(solution)/shard_map/pack/pallas_call | solution.py:518
  1.8 23.6 %all_to_all.5.recv_ref = f32[8,144,128]{2,1,0:T(8,128)S(1)} all-to-all(f32[8,144,128]{2,1,0:T(8,128)S(1)} %pack.1), channel_id=1, replica_groups=mesh['groups'=2,'pts'=4,'comp'=2,'sub'=2] {'pts','comp'}, dimensions={0} | all-to-all | bytes 1179648 | tf_op jit(solution)/shard_map/all_to_all | solution.py:524
  25.5 5.3 %slab.1 = f32[48,32,128]{2,1,0:T(8,128)} custom-call(f32[8,144,128]{2,1,0:T(8,128)S(1)} %all_to_all.5.recv_ref), custom_call_target="tpu_custom_call" | custom-call | tf_op jit(solution)/shard_map/slab/pallas_call | solution.py:525

commit v12 on v11

--- a/solution.py
+++ b/solution.py
@@ -237,7 +237,6 @@
 
 
 BLOCK = 8
-PER_STEP = 4
 
 
 def slab_kernel(
@@ -391,32 +390,6 @@
             for side in range(2):
                 faces_y[f, side, x] = row(speed_y_faces[f][side], x) * sine + row(current_y_faces[side], x)
 
-    scattered = [
-        lax.dot_general(
-            jnp.concatenate(column, axis=1),
-            onehot[:, pl.ds(offset, len(column) * LANES)],
-            (((1,), (1,)), ((), ())),
-            preferred_element_type=jnp.float32,
-        )
-        for offset, column in zip(offsets, columns)
-    ]
-    nothing = jnp.zeros((DIR, LANES), jnp.float32)
-    for f in range(freqs):
-        for field in (first, second):
-            for edge in (0, 1, slab_rows + 2, slab_rows + 3):
-                field[f, edge] = nothing
-        for h in range(highs):
-            terms = []
-            for span, product in zip(spans, scattered):
-                if h in span:
-                    at = (h - span[0]) * width + f * 2 * DIR
-                    terms += [product[at : at + DIR], product[at + DIR : at + 2 * DIR]]
-            total = sum(terms[1:], terms[0])
-            first[f, 2 * h + 2] = total[:, :LANES]
-            first[f, 2 * h + 3] = total[:, LANES:]
-    named = sum(product[len(span) * width :] for span, product in zip(spans, scattered))
-
-    land_slots = keep(named[:, :LANES]), keep(named[:, LANES:])
     ahead = jnp.maximum(turning, 0.0) * 0.125
     back = jnp.minimum(turning, 0.0) * 0.125
     bend_slots = [
@@ -429,7 +402,12 @@
             back,
         )
     ]
-
+    land_slots = next(slots), next(slots)
+    nothing = jnp.zeros((DIR, LANES), jnp.float32)
+    for f in range(freqs):
+        for field in (first, second):
+            for edge in (0, 1, slab_rows + 2, slab_rows + 3):
+                field[f, edge] = nothing
     lane_wide = lax.broadcasted_iota(jnp.int32, (DIR, LANES), 1)
 
     def flux(speed, behind, centre3, onward3, beyond):
@@ -438,32 +416,24 @@
         far = jnp.where(positive, behind, beyond)
         return speed * ((centre3 + onward3) + (near - far))
 
-    def advance(field, step, carry, finish):
-        carry = list(carry)
-        for i in range(BLOCK):
-            x = step * BLOCK + i
-            sea = row(land_slots[i % 2], step * (BLOCK // 2) + i // 2)
-            for f in range(freqs):
-                entering, centre3 = carry[f]
-                centre = field[f, x + 2]
-                onward3 = 3.0 * field[f, x + 3]
-                leaving = flux(faces_x[f, x + 1], field[f, x + 1], centre3, onward3, field[f, x + 4])
-                up1 = jnp.where(lane_wide < LANES - 1, pltpu.roll(centre, LANES - 1, 1), 0.0)
-                up2 = jnp.where(lane_wide < LANES - 2, pltpu.roll(centre, LANES - 2, 1), 0.0)
-                down1 = jnp.where(lane_wide > 0, pltpu.roll(centre, 1, 1), 0.0)
-                down2 = jnp.where(lane_wide > 1, pltpu.roll(centre, 2, 1), 0.0)
-                right = flux(faces_y[f, 0, x], down1, centre3, 3.0 * up1, up2)
-                left = flux(faces_y[f, 1, x], down2, 3.0 * down1, centre3, up1)
-                finish(f, x, (centre - (leaving - entering) - (right - left)) * sea)
-                carry[f] = leaving, onward3
-        return tuple(carry)
-
-    def enter(field):
-        carry = []
+    def advance(field, x, carry, finish):
+        sea = row(land_slots[x % 2], x // 2)
         for f in range(freqs):
-            start3 = 3.0 * field[f, 2]
-            carry.append((flux(faces_x[f, 0], nothing, nothing, start3, field[f, 3]), start3))
-        return tuple(carry)
+            if x == 0:
+                start3 = 3.0 * field[f, 2]
+                carry[f] = flux(faces_x[f, 0], nothing, nothing, start3, field[f, 3]), start3
+            entering, centre3 = carry[f]
+            centre = field[f, x + 2]
+            onward3 = 3.0 * field[f, x + 3]
+            leaving = flux(faces_x[f, x + 1], field[f, x + 1], centre3, onward3, field[f, x + 4])
+            up1 = jnp.where(lane_wide < LANES - 1, pltpu.roll(centre, LANES - 1, 1), 0.0)
+            up2 = jnp.where(lane_wide < LANES - 2, pltpu.roll(centre, LANES - 2, 1), 0.0)
+            down1 = jnp.where(lane_wide > 0, pltpu.roll(centre, 1, 1), 0.0)
+            down2 = jnp.where(lane_wide > 1, pltpu.roll(centre, 2, 1), 0.0)
+            right = flux(faces_y[f, 0, x], down1, centre3, 3.0 * up1, up2)
+            left = flux(faces_y[f, 1, x], down2, 3.0 * down1, centre3, up1)
+            finish(f, x, (centre - (leaving - entering) - (right - left)) * sea)
+            carry[f] = leaving, onward3
 
     def store(f, x, moved):
         second[f, x + 2] = moved
@@ -473,13 +443,12 @@
             at = (f * DIR + g * 8) * slab_rows + x
             moved_ref[pl.ds(at, 8, stride=slab_rows), :] = moved[g * 8 : g * 8 + 8]
 
-    def copy_out(step):
-        part = pl.ds(pl.multiple_of(step * BLOCK, BLOCK), BLOCK)
-        return pltpu.make_async_copy(done_ref.at[:, part, :], out_ref.at[:, part, :], sems.at[step])
-
-    def final(block, carry):
-        carry = advance(second, block, carry, turn)
-        at = pl.multiple_of(block * BLOCK, BLOCK)
+    def copy_out(block):
+        part = pl.ds(block * BLOCK, BLOCK)
+        return pltpu.make_async_copy(done_ref.at[:, part, :], out_ref.at[:, part, :], sems.at[block])
+
+    def refract(block):
+        at = block * BLOCK
         weights = [table[slot, pl.ds(8 + at, BLOCK), :] for slot in bend_slots]
         for f in range(freqs):
             ring = [moved_ref[pl.ds((f * DIR + d) * slab_rows + at, BLOCK), :] for d in range(DIR)]
@@ -489,18 +458,48 @@
                     bent = bent + weights[k] * ring[(d + k - 2) % DIR]
                 done_ref[f * DIR + d, pl.ds(at, BLOCK), :] = bent
         copy_out(block).start()
-        return carry
-
-    def sweep(one_block, carry):
-        def body(step, carry):
-            for i in range(PER_STEP):
-                carry = one_block(step * PER_STEP + i, carry)
-            return carry
-
-        lax.fori_loop(0, slab_rows // BLOCK // PER_STEP, body, carry)
-
-    sweep(lambda block, carry: advance(first, block, carry, store), enter(first))
-    sweep(final, enter(second))
+
+    sums = [None] * highs
+    named = [None, None]
+    complete = 0
+    reached = [0, 0, 0]
+    carries = [[None] * freqs, [None] * freqs]
+    for part, (span, offset, column) in enumerate(zip(spans, offsets, columns)):
+        product = lax.dot_general(
+            jnp.concatenate(column, axis=1),
+            onehot[:, pl.ds(offset, len(column) * LANES)],
+            (((1,), (1,)), ((), ())),
+            preferred_element_type=jnp.float32,
+        )
+        for h in span:
+            at = (h - span[0]) * width
+            for f in range(freqs):
+                here = at + f * 2 * DIR
+                term = product[here : here + DIR] + product[here + DIR : here + 2 * DIR]
+                sums[h] = sums[h] or []
+                if len(sums[h]) > f:
+                    sums[h][f] = sums[h][f] + term
+                else:
+                    sums[h].append(term)
+        for side in range(2):
+            hit = product[len(span) * width :, side * LANES : (side + 1) * LANES]
+            named[side] = hit if part == 0 else named[side] + hit
+            table[land_slots[side], pl.ds(8, highs), :] = named[side]
+        until = highs if part + 1 == len(spans) else spans[part + 1][0]
+        for h in range(complete, until):
+            for f in range(freqs):
+                first[f, 2 * h + 2] = sums[h][f][:, :LANES]
+                first[f, 2 * h + 3] = sums[h][f][:, LANES:]
+        complete = until
+        ready = 2 * complete
+        for stage, (field, finish) in enumerate(((first, store), (second, turn))):
+            ready = slab_rows if ready == slab_rows else max(ready - 2, 0)
+            for x in range(reached[stage], ready):
+                advance(field, x, carries[stage], finish)
+            reached[stage] = ready
+        for block in range(reached[2], ready // BLOCK):
+            refract(block)
+        reached[2] = ready // BLOCK
     for block in range(slab_rows // BLOCK):
         copy_out(block).wait()
 

time: 30.9 us -> 30.9 us (level)
  no operation moved by 1% of the time
where the time goes in v12:
time: 30.9 us; the launch traced here: 30.8 us
  blocking collectives  23.6 us (76%)
  Pallas kernels  7.12 us (23%)
    all_to_all x1, blocking collectives, slab_plan(): lax.all_to_all(packed, GROUP, split_axis=0, concat_axis=0, tiled=True)  23.6 us
    pallas_call x1, Pallas kernels, slab_plan(): pl.pallas_call(functools.partial(slab_kernel, parts, tile_rows, full, fre...  5.28 us
    pallas_call x1, Pallas kernels, slab_plan(): pl.pallas_call(functools.partial(pack_kernel, parts, freqs), out_shape=pl...  1.84 us

profile of v12, /device:TPU:0, one launch (start us, length us, event | category | flops | bytes accessed | tf_op | source)
XLA Modules:
  0.0 30.8 jit_solution(14669696003715907646)
XLA Ops:
  0.0 1.8 %pack.1 = f32[8,144,128]{2,1,0:T(8,128)S(1)} custom-call(f32[320,384]{1,0:T(8,128)} %spectra_ref.1, f32[320]{0:T(512)} %wind_ref.1, f32[384]{0:T(512)} %growth_ref.1, f32[384]{0:T(512)} %damping_ref.1, s32[320]{0:T(512)} %cell_ref.1, f32[16,4,128]{2,1,0:T(4,128)} %speed_ref.1, f32[2,4,128]{2,1,0:T(4,128)} %current_ref.1, f32[4,128]{1,0:T(4,128)} %turning_ref.1), custom_call_target="tpu_custom_call" | custom-call | tf_op jit(solution)/shard_map/pack/pallas_call | solution.py:517
  1.8 23.6 %all_to_all.5.recv_ref = f32[8,144,128]{2,1,0:T(8,128)S(1)} all-to-all(f32[8,144,128]{2,1,0:T(8,128)S(1)} %pack.1), channel_id=1, replica_groups=mesh['groups'=2,'pts'=4,'comp'=2,'sub'=2] {'pts','comp'}, dimensions={0} | all-to-all | bytes 1179648 | tf_op jit(solution)/shard_map/all_to_all | solution.py:523
  25.5 5.3 %slab.1 = f32[48,32,128]{2,1,0:T(8,128)} custom-call(f32[8,144,128]{2,1,0:T(8,128)S(1)} %all_to_all.5.recv_ref), custom_call_target="tpu_custom_call" | custom-call | tf_op jit(solution)/shard_map/slab/pallas_call | solution.py:524

commit v13 on v11

--- a/solution.py
+++ b/solution.py
@@ -237,7 +237,6 @@
 
 
 BLOCK = 8
-PER_STEP = 4
 
 
 def slab_kernel(
@@ -430,7 +429,21 @@
         )
     ]
 
-    lane_wide = lax.broadcasted_iota(jnp.int32, (DIR, LANES), 1)
+    gap = lax.broadcasted_iota(jnp.int32, (LANES, LANES), 0) - lax.broadcasted_iota(
+        jnp.int32, (LANES, LANES), 1
+    )
+
+    def band(first_gap, values):
+        out = jnp.zeros((LANES, LANES), jnp.float32)
+        for i, value in enumerate(values):
+            out = jnp.where(gap == first_gap + i, value, out)
+        return out
+
+    left_values, right_values = (-1.0, 6.0, 3.0), (3.0, 6.0, -1.0)
+    bands = jnp.concatenate(
+        [band(-1, left_values), band(0, right_values), band(-2, left_values), band(-1, right_values)], axis=1
+    ).astype(jnp.bfloat16)
+    bands = jnp.concatenate([bands, bands], axis=0)
 
     def flux(speed, behind, centre3, onward3, beyond):
         positive = speed > 0.0
@@ -438,32 +451,41 @@
         far = jnp.where(positive, behind, beyond)
         return speed * ((centre3 + onward3) + (near - far))
 
-    def advance(field, step, carry, finish):
-        carry = list(carry)
-        for i in range(BLOCK):
-            x = step * BLOCK + i
-            sea = row(land_slots[i % 2], step * (BLOCK // 2) + i // 2)
-            for f in range(freqs):
-                entering, centre3 = carry[f]
-                centre = field[f, x + 2]
-                onward3 = 3.0 * field[f, x + 3]
-                leaving = flux(faces_x[f, x + 1], field[f, x + 1], centre3, onward3, field[f, x + 4])
-                up1 = jnp.where(lane_wide < LANES - 1, pltpu.roll(centre, LANES - 1, 1), 0.0)
-                up2 = jnp.where(lane_wide < LANES - 2, pltpu.roll(centre, LANES - 2, 1), 0.0)
-                down1 = jnp.where(lane_wide > 0, pltpu.roll(centre, 1, 1), 0.0)
-                down2 = jnp.where(lane_wide > 1, pltpu.roll(centre, 2, 1), 0.0)
-                right = flux(faces_y[f, 0, x], down1, centre3, 3.0 * up1, up2)
-                left = flux(faces_y[f, 1, x], down2, 3.0 * down1, centre3, up1)
-                finish(f, x, (centre - (leaving - entering) - (right - left)) * sea)
-                carry[f] = leaving, onward3
-        return tuple(carry)
-
-    def enter(field):
+    def along_y(field):
+        rows = jnp.concatenate(
+            [field[f, 2 : slab_rows + 2].reshape(slab_rows * DIR, LANES) for f in range(freqs)], axis=0
+        )
+        head = rows.astype(jnp.bfloat16)
+        rest = (rows - head.astype(jnp.float32)).astype(jnp.bfloat16)
+        return lax.dot_general(
+            jnp.concatenate([head, rest], axis=1),
+            bands,
+            (((1,), (0,)), ((), ())),
+            preferred_element_type=jnp.float32,
+        )
+
+    def upwind(speed, values):
+        return speed * jnp.where(speed > 0.0, values[:, :LANES], values[:, LANES:])
+
+    def advance(field, finish, after_block):
+        values = along_y(field)
         carry = []
         for f in range(freqs):
             start3 = 3.0 * field[f, 2]
             carry.append((flux(faces_x[f, 0], nothing, nothing, start3, field[f, 3]), start3))
-        return tuple(carry)
+        for x in range(slab_rows):
+            sea = row(land_slots[x % 2], x // 2)
+            for f in range(freqs):
+                entering, centre3 = carry[f]
+                onward3 = 3.0 * field[f, x + 3]
+                leaving = flux(faces_x[f, x + 1], field[f, x + 1], centre3, onward3, field[f, x + 4])
+                at = (f * slab_rows + x) * DIR
+                right = upwind(faces_y[f, 0, x], values[at : at + DIR, : 2 * LANES])
+                left = upwind(faces_y[f, 1, x], values[at : at + DIR, 2 * LANES :])
+                finish(f, x, (field[f, x + 2] - (leaving - entering) - (right - left)) * sea)
+                carry[f] = leaving, onward3
+            if (x + 1) % BLOCK == 0:
+                after_block(x // BLOCK)
 
     def store(f, x, moved):
         second[f, x + 2] = moved
@@ -477,9 +499,8 @@
         part = pl.ds(pl.multiple_of(step * BLOCK, BLOCK), BLOCK)
         return pltpu.make_async_copy(done_ref.at[:, part, :], out_ref.at[:, part, :], sems.at[step])
 
-    def final(block, carry):
-        carry = advance(second, block, carry, turn)
-        at = pl.multiple_of(block * BLOCK, BLOCK)
+    def refract(block):
+        at = block * BLOCK
         weights = [table[slot, pl.ds(8 + at, BLOCK), :] for slot in bend_slots]
         for f in range(freqs):
             ring = [moved_ref[pl.ds((f * DIR + d) * slab_rows + at, BLOCK), :] for d in range(DIR)]
@@ -489,18 +510,9 @@
                     bent = bent + weights[k] * ring[(d + k - 2) % DIR]
                 done_ref[f * DIR + d, pl.ds(at, BLOCK), :] = bent
         copy_out(block).start()
-        return carry
-
-    def sweep(one_block, carry):
-        def body(step, carry):
-            for i in range(PER_STEP):
-                carry = one_block(step * PER_STEP + i, carry)
-            return carry
-
-        lax.fori_loop(0, slab_rows // BLOCK // PER_STEP, body, carry)
-
-    sweep(lambda block, carry: advance(first, block, carry, store), enter(first))
-    sweep(final, enter(second))
+
+    advance(first, store, lambda block: None)
+    advance(second, turn, refract)
     for block in range(slab_rows // BLOCK):
         copy_out(block).wait()
 

time: 30.9 us -> 31.3 us (1.013)
  Pallas kernels: 7.12 us -> 7.45 us
    pallas_call x1, Pallas kernels: 5.28 us -> 5.61 us  [slab_plan(): pl.pallas_call(functools.partial(slab_kernel, parts, tile_rows, full, fre...]
where the time goes in v13:
time: 31.3 us; the launch traced here: 31.1 us
  blocking collectives  23.6 us (75%)
  Pallas kernels  7.45 us (24%)
    all_to_all x1, blocking collectives, slab_plan(): lax.all_to_all(packed, GROUP, split_axis=0, concat_axis=0, tiled=True)  23.6 us
    pallas_call x1, Pallas kernels, slab_plan(): pl.pallas_call(functools.partial(slab_kernel, parts, tile_rows, full, fre...  5.61 us
    pallas_call x1, Pallas kernels, slab_plan(): pl.pallas_call(functools.partial(pack_kernel, parts, freqs), out_shape=pl...  1.84 us

profile of v13, /device:TPU:0, one launch (start us, length us, event | category | flops | bytes accessed | tf_op | source)
XLA Modules:
  0.0 31.1 jit_solution(14603641464835031838)
XLA Ops:
  0.0 1.8 %pack.1 = f32[8,144,128]{2,1,0:T(8,128)S(1)} custom-call(f32[320,384]{1,0:T(8,128)} %spectra_ref.1, f32[320]{0:T(512)} %wind_ref.1, f32[384]{0:T(512)} %growth_ref.1, f32[384]{0:T(512)} %damping_ref.1, s32[320]{0:T(512)} %cell_ref.1, f32[16,4,128]{2,1,0:T(4,128)} %speed_ref.1, f32[2,4,128]{2,1,0:T(4,128)} %current_ref.1, f32[4,128]{1,0:T(4,128)} %turning_ref.1), custom_call_target="tpu_custom_call" | custom-call | tf_op jit(solution)/shard_map/pack/pallas_call | solution.py:530
  1.8 23.6 %all_to_all.5.recv_ref = f32[8,144,128]{2,1,0:T(8,128)S(1)} all-to-all(f32[8,144,128]{2,1,0:T(8,128)S(1)} %pack.1), channel_id=1, replica_groups=mesh['groups'=2,'pts'=4,'comp'=2,'sub'=2] {'pts','comp'}, dimensions={0} | all-to-all | bytes 1179648 | tf_op jit(solution)/shard_map/all_to_all | solution.py:536
  25.5 5.6 %slab.1 = f32[48,32,128]{2,1,0:T(8,128)} custom-call(f32[8,144,128]{2,1,0:T(8,128)S(1)} %all_to_all.5.recv_ref), custom_call_target="tpu_custom_call" | custom-call | tf_op jit(solution)/shard_map/slab/pallas_call | solution.py:537

commit v14 on v11

--- a/solution.py
+++ b/solution.py
@@ -247,7 +247,6 @@
     freqs,
     recv_ref,
     out_ref,
-    onehot,
     first,
     second,
     table,
@@ -283,15 +282,18 @@
             if owner_rows - capacity * (parts - t) < begin + half and capacity * (t + 1) > begin
         ]
         spans.append(range(tiles[0] * tile_rows // 2, (tiles[-1] + 1) * tile_rows // 2))
-    offsets = [parts // 2 * LANES * chunk for chunk in range(len(spans))]
     columns = [[] for _ in spans]
+    hots = [[] for _ in spans]
+
+    def repeated(line, count):
+        tile = jnp.broadcast_to(line, (16, LANES)).astype(jnp.bfloat16)
+        return jnp.concatenate([tile] * (count // 16), axis=0)
 
     def place(chunk, cells, values):
-        span = pl.ds(offsets[chunk] + len(columns[chunk]) * LANES, LANES)
         high = cells // (2 * LANES)
         low = (cells - high * (2 * LANES)).astype(jnp.float32)
-        low = jnp.broadcast_to(low, (2 * LANES, LANES)).astype(jnp.bfloat16)
-        onehot[:, span] = jnp.where(cell_iota == low, 1.0, 0.0).astype(jnp.bfloat16)
+        low = repeated(low, 2 * LANES)
+        hots[chunk].append(jnp.where(cell_iota == low, 1.0, 0.0).astype(jnp.bfloat16))
         pieces = []
         for value in values:
             head = value.astype(jnp.bfloat16).astype(jnp.float32)
@@ -299,8 +301,7 @@
         both = jnp.concatenate(pieces, axis=0).astype(jnp.bfloat16)
         column = []
         for h in spans[chunk]:
-            pick = jnp.broadcast_to((high == h).astype(jnp.float32), (width, LANES)).astype(jnp.bfloat16)
-            column.append(both * pick)
+            column.append(both * repeated((high == h).astype(jnp.float32), width))
         column.append((high_iota == high).astype(jnp.float32).astype(jnp.bfloat16))
         columns[chunk].append(jnp.concatenate(column, axis=0))
 
@@ -394,11 +395,11 @@
     scattered = [
         lax.dot_general(
             jnp.concatenate(column, axis=1),
-            onehot[:, pl.ds(offset, len(column) * LANES)],
+            jnp.concatenate(hot, axis=1),
             (((1,), (1,)), ((), ())),
             preferred_element_type=jnp.float32,
         )
-        for offset, column in zip(offsets, columns)
+        for hot, column in zip(hots, columns)
     ]
     nothing = jnp.zeros((DIR, LANES), jnp.float32)
     for f in range(freqs):
@@ -512,7 +513,6 @@
     freqs = comps // parts // DIR
     full = rows // LANES
     slab_rows = parts * tile_rows
-    depth = parts * rows
     highs = slab_rows // 2
     block_rows = -(-(freqs * (full * DIR + 16) + 3 * tile_rows + full + 1) // 8) * 8
     packed = pl.pallas_call(
@@ -528,7 +528,6 @@
         in_specs=[pl.BlockSpec(memory_space=pltpu.VMEM)],
         out_specs=pl.BlockSpec(memory_space=pl.ANY),
         scratch_shapes=[
-            pltpu.VMEM((2 * LANES, depth), jnp.bfloat16),
             pltpu.VMEM((freqs, slab_rows + 4, DIR, LANES), jnp.float32),
             pltpu.VMEM((freqs, slab_rows + 4, DIR, LANES), jnp.float32),
             pltpu.VMEM((10 + 3 * freqs, slab_rows + 16, LANES), jnp.float32),

time: 30.9 us -> 30.5 us (0.987)
  Pallas kernels: 7.12 us -> 6.7 us
    pallas_call x1, Pallas kernels: 5.28 us -> 4.87 us  [slab_plan(): pl.pallas_call(functools.partial(slab_kernel, parts, tile_rows, full, fre...]
where the time goes in v14:
time: 30.5 us; the launch traced here: 30.3 us
  blocking collectives  23.6 us (77%)
  Pallas kernels  6.7 us (22%)
    all_to_all x1, blocking collectives, slab_plan(): lax.all_to_all(packed, GROUP, split_axis=0, concat_axis=0, tiled=True)  23.6 us
    pallas_call x1, Pallas kernels, slab_plan(): pl.pallas_call(functools.partial(slab_kernel, parts, tile_rows, full, fre...  4.87 us
    pallas_call x1, Pallas kernels, slab_plan(): pl.pallas_call(functools.partial(pack_kernel, parts, freqs), out_shape=pl...  1.84 us

profile of v14, /device:TPU:0, one launch (start us, length us, event | category | flops | bytes accessed | tf_op | source)
XLA Modules:
  0.0 30.3 jit_solution(8806893105466919113)
XLA Ops:
  0.0 1.8 %pack.1 = f32[8,144,128]{2,1,0:T(8,128)S(1)} custom-call(f32[320,384]{1,0:T(8,128)} %spectra_ref.1, f32[320]{0:T(512)} %wind_ref.1, f32[384]{0:T(512)} %growth_ref.1, f32[384]{0:T(512)} %damping_ref.1, s32[320]{0:T(512)} %cell_ref.1, f32[16,4,128]{2,1,0:T(4,128)} %speed_ref.1, f32[2,4,128]{2,1,0:T(4,128)} %current_ref.1, f32[4,128]{1,0:T(4,128)} %turning_ref.1), custom_call_target="tpu_custom_call" | custom-call | tf_op jit(solution)/shard_map/pack/pallas_call | solution.py:518
  1.8 23.6 %all_to_all.5.recv_ref = f32[8,144,128]{2,1,0:T(8,128)S(1)} all-to-all(f32[8,144,128]{2,1,0:T(8,128)S(1)} %pack.1), channel_id=1, replica_groups=mesh['groups'=2,'pts'=4,'comp'=2,'sub'=2] {'pts','comp'}, dimensions={0} | all-to-all | bytes 1179648 | tf_op jit(solution)/shard_map/all_to_all | solution.py:524
  25.5 4.9 %slab.1 = f32[48,32,128]{2,1,0:T(8,128)} custom-call(f32[8,144,128]{2,1,0:T(8,128)S(1)} %all_to_all.5.recv_ref), custom_call_target="tpu_custom_call" | custom-call | tf_op jit(solution)/shard_map/slab/pallas_call | solution.py:525

commit v15 on v14

--- a/solution.py
+++ b/solution.py
@@ -469,10 +469,12 @@
     def store(f, x, moved):
         second[f, x + 2] = moved
 
+    pitch = slab_rows + 1
+
     def turn(f, x, moved):
         for g in range(DIR // 8):
-            at = (f * DIR + g * 8) * slab_rows + x
-            moved_ref[pl.ds(at, 8, stride=slab_rows), :] = moved[g * 8 : g * 8 + 8]
+            at = (f * DIR + g * 8) * pitch + x
+            moved_ref[pl.ds(at, 8, stride=pitch), :] = moved[g * 8 : g * 8 + 8]
 
     def copy_out(step):
         part = pl.ds(pl.multiple_of(step * BLOCK, BLOCK), BLOCK)
@@ -483,7 +485,7 @@
         at = pl.multiple_of(block * BLOCK, BLOCK)
         weights = [table[slot, pl.ds(8 + at, BLOCK), :] for slot in bend_slots]
         for f in range(freqs):
-            ring = [moved_ref[pl.ds((f * DIR + d) * slab_rows + at, BLOCK), :] for d in range(DIR)]
+            ring = [moved_ref[pl.ds((f * DIR + d) * pitch + at, BLOCK), :] for d in range(DIR)]
             for d in range(DIR):
                 bent = weights[2] * ring[d]
                 for k in (0, 1, 3, 4):
@@ -533,7 +535,7 @@
             pltpu.VMEM((10 + 3 * freqs, slab_rows + 16, LANES), jnp.float32),
             pltpu.VMEM((freqs, slab_rows + 1, DIR, LANES), jnp.float32),
             pltpu.VMEM((freqs, 2, slab_rows, DIR, LANES), jnp.float32),
-            pltpu.VMEM((freqs * DIR * slab_rows, LANES), jnp.float32),
+            pltpu.VMEM((freqs * DIR * (slab_rows + 1), LANES), jnp.float32),
             pltpu.VMEM((freqs * DIR, slab_rows, LANES), jnp.float32),
             pltpu.SemaphoreType.DMA((slab_rows // BLOCK,)),
         ],

time: 30.5 us -> 30.2 us (level)
  Pallas kernels: 6.7 us -> 6.33 us
    pallas_call x1, Pallas kernels: 4.87 us -> 4.5 us  [slab_plan(): pl.pallas_call(functools.partial(slab_kernel, parts, tile_rows, full, fre...]
where the time goes in v15:
time: 30.2 us; the launch traced here: 30 us
  blocking collectives  23.6 us (78%)
  Pallas kernels  6.33 us (21%)
    all_to_all x1, blocking collectives, slab_plan(): lax.all_to_all(packed, GROUP, split_axis=0, concat_axis=0, tiled=True)  23.6 us
    pallas_call x1, Pallas kernels, slab_plan(): pl.pallas_call(functools.partial(slab_kernel, parts, tile_rows, full, fre...  4.5 us
    pallas_call x1, Pallas kernels, slab_plan(): pl.pallas_call(functools.partial(pack_kernel, parts, freqs), out_shape=pl...  1.84 us

profile of v15, /device:TPU:0, one launch (start us, length us, event | category | flops | bytes accessed | tf_op | source)
XLA Modules:
  0.0 30.0 jit_solution(11490954902467494538)
XLA Ops:
  0.0 1.8 %pack.1 = f32[8,144,128]{2,1,0:T(8,128)S(1)} custom-call(f32[320,384]{1,0:T(8,128)} %spectra_ref.1, f32[320]{0:T(512)} %wind_ref.1, f32[384]{0:T(512)} %growth_ref.1, f32[384]{0:T(512)} %damping_ref.1, s32[320]{0:T(512)} %cell_ref.1, f32[16,4,128]{2,1,0:T(4,128)} %speed_ref.1, f32[2,4,128]{2,1,0:T(4,128)} %current_ref.1, f32[4,128]{1,0:T(4,128)} %turning_ref.1), custom_call_target="tpu_custom_call" | custom-call | tf_op jit(solution)/shard_map/pack/pallas_call | solution.py:520
  1.8 23.6 %all_to_all.5.recv_ref = f32[8,144,128]{2,1,0:T(8,128)S(1)} all-to-all(f32[8,144,128]{2,1,0:T(8,128)S(1)} %pack.1), channel_id=1, replica_groups=mesh['groups'=2,'pts'=4,'comp'=2,'sub'=2] {'pts','comp'}, dimensions={0} | all-to-all | bytes 1179648 | tf_op jit(solution)/shard_map/all_to_all | solution.py:526
  25.5 4.5 %slab.1 = f32[48,32,128]{2,1,0:T(8,128)} custom-call(f32[8,144,128]{2,1,0:T(8,128)S(1)} %all_to_all.5.recv_ref), custom_call_target="tpu_custom_call" | custom-call | tf_op jit(solution)/shard_map/slab/pallas_call | solution.py:527

commit v16 on v12

--- a/solution.py
+++ b/solution.py
@@ -246,7 +246,6 @@
     freqs,
     recv_ref,
     out_ref,
-    onehot,
     first,
     second,
     table,
@@ -282,15 +281,18 @@
             if owner_rows - capacity * (parts - t) < begin + half and capacity * (t + 1) > begin
         ]
         spans.append(range(tiles[0] * tile_rows // 2, (tiles[-1] + 1) * tile_rows // 2))
-    offsets = [parts // 2 * LANES * chunk for chunk in range(len(spans))]
     columns = [[] for _ in spans]
+    hots = [[] for _ in spans]
+
+    def repeated(line, count):
+        tile = jnp.broadcast_to(line, (16, LANES)).astype(jnp.bfloat16)
+        return jnp.concatenate([tile] * (count // 16), axis=0)
 
     def place(chunk, cells, values):
-        span = pl.ds(offsets[chunk] + len(columns[chunk]) * LANES, LANES)
         high = cells // (2 * LANES)
         low = (cells - high * (2 * LANES)).astype(jnp.float32)
-        low = jnp.broadcast_to(low, (2 * LANES, LANES)).astype(jnp.bfloat16)
-        onehot[:, span] = jnp.where(cell_iota == low, 1.0, 0.0).astype(jnp.bfloat16)
+        low = repeated(low, 2 * LANES)
+        hots[chunk].append(jnp.where(cell_iota == low, 1.0, 0.0).astype(jnp.bfloat16))
         pieces = []
         for value in values:
             head = value.astype(jnp.bfloat16).astype(jnp.float32)
@@ -298,8 +300,7 @@
         both = jnp.concatenate(pieces, axis=0).astype(jnp.bfloat16)
         column = []
         for h in spans[chunk]:
-            pick = jnp.broadcast_to((high == h).astype(jnp.float32), (width, LANES)).astype(jnp.bfloat16)
-            column.append(both * pick)
+            column.append(both * repeated((high == h).astype(jnp.float32), width))
         column.append((high_iota == high).astype(jnp.float32).astype(jnp.bfloat16))
         columns[chunk].append(jnp.concatenate(column, axis=0))
 
@@ -438,10 +439,12 @@
     def store(f, x, moved):
         second[f, x + 2] = moved
 
+    pitch = slab_rows + 1
+
     def turn(f, x, moved):
         for g in range(DIR // 8):
-            at = (f * DIR + g * 8) * slab_rows + x
-            moved_ref[pl.ds(at, 8, stride=slab_rows), :] = moved[g * 8 : g * 8 + 8]
+            at = (f * DIR + g * 8) * pitch + x
+            moved_ref[pl.ds(at, 8, stride=pitch), :] = moved[g * 8 : g * 8 + 8]
 
     def copy_out(block):
         part = pl.ds(block * BLOCK, BLOCK)
@@ -451,7 +454,7 @@
         at = block * BLOCK
         weights = [table[slot, pl.ds(8 + at, BLOCK), :] for slot in bend_slots]
         for f in range(freqs):
-            ring = [moved_ref[pl.ds((f * DIR + d) * slab_rows + at, BLOCK), :] for d in range(DIR)]
+            ring = [moved_ref[pl.ds((f * DIR + d) * pitch + at, BLOCK), :] for d in range(DIR)]
             for d in range(DIR):
                 bent = weights[2] * ring[d]
                 for k in (0, 1, 3, 4):
@@ -464,10 +467,10 @@
     complete = 0
     reached = [0, 0, 0]
     carries = [[None] * freqs, [None] * freqs]
-    for part, (span, offset, column) in enumerate(zip(spans, offsets, columns)):
+    for part, (span, hot, column) in enumerate(zip(spans, hots, columns)):
         product = lax.dot_general(
             jnp.concatenate(column, axis=1),
-            onehot[:, pl.ds(offset, len(column) * LANES)],
+            jnp.concatenate(hot, axis=1),
             (((1,), (1,)), ((), ())),
             preferred_element_type=jnp.float32,
         )
@@ -511,7 +514,6 @@
     freqs = comps // parts // DIR
     full = rows // LANES
     slab_rows = parts * tile_rows
-    depth = parts * rows
     highs = slab_rows // 2
     block_rows = -(-(freqs * (full * DIR + 16) + 3 * tile_rows + full + 1) // 8) * 8
     packed = pl.pallas_call(
@@ -527,13 +529,12 @@
         in_specs=[pl.BlockSpec(memory_space=pltpu.VMEM)],
         out_specs=pl.BlockSpec(memory_space=pl.ANY),
         scratch_shapes=[
-            pltpu.VMEM((2 * LANES, depth), jnp.bfloat16),
             pltpu.VMEM((freqs, slab_rows + 4, DIR, LANES), jnp.float32),
             pltpu.VMEM((freqs, slab_rows + 4, DIR, LANES), jnp.float32),
             pltpu.VMEM((10 + 3 * freqs, slab_rows + 16, LANES), jnp.float32),
             pltpu.VMEM((freqs, slab_rows + 1, DIR, LANES), jnp.float32),
             pltpu.VMEM((freqs, 2, slab_rows, DIR, LANES), jnp.float32),
-            pltpu.VMEM((freqs * DIR * slab_rows, LANES), jnp.float32),
+            pltpu.VMEM((freqs * DIR * (slab_rows + 1), LANES), jnp.float32),
             pltpu.VMEM((freqs * DIR, slab_rows, LANES), jnp.float32),
             pltpu.SemaphoreType.DMA((slab_rows // BLOCK,)),
         ],

time: 30.9 us -> 30.2 us (0.977)
  Pallas kernels: 7.12 us -> 6.35 us
    pallas_call x1, Pallas kernels: 5.28 us -> 4.52 us  [slab_plan(): pl.pallas_call(functools.partial(slab_kernel, parts, tile_rows, full, fre...]
where the time goes in v16:
time: 30.2 us; the launch traced here: 30 us
  blocking collectives  23.6 us (78%)
  Pallas kernels  6.35 us (21%)
    all_to_all x1, blocking collectives, slab_plan(): lax.all_to_all(packed, GROUP, split_axis=0, concat_axis=0, tiled=True)  23.6 us
    pallas_call x1, Pallas kernels, slab_plan(): pl.pallas_call(functools.partial(slab_kernel, parts, tile_rows, full, fre...  4.52 us
    pallas_call x1, Pallas kernels, slab_plan(): pl.pallas_call(functools.partial(pack_kernel, parts, freqs), out_shape=pl...  1.84 us

profile of v16, /device:TPU:0, one launch (start us, length us, event | category | flops | bytes accessed | tf_op | source)
XLA Modules:
  0.0 30.0 jit_solution(5850534019830998816)
XLA Ops:
  0.0 1.8 %pack.1 = f32[8,144,128]{2,1,0:T(8,128)S(1)} custom-call(f32[320,384]{1,0:T(8,128)} %spectra_ref.1, f32[320]{0:T(512)} %wind_ref.1, f32[384]{0:T(512)} %growth_ref.1, f32[384]{0:T(512)} %damping_ref.1, s32[320]{0:T(512)} %cell_ref.1, f32[16,4,128]{2,1,0:T(4,128)} %speed_ref.1, f32[2,4,128]{2,1,0:T(4,128)} %current_ref.1, f32[4,128]{1,0:T(4,128)} %turning_ref.1), custom_call_target="tpu_custom_call" | custom-call | tf_op jit(solution)/shard_map/pack/pallas_call | solution.py:519
  1.8 23.6 %all_to_all.5.recv_ref = f32[8,144,128]{2,1,0:T(8,128)S(1)} all-to-all(f32[8,144,128]{2,1,0:T(8,128)S(1)} %pack.1), channel_id=1, replica_groups=mesh['groups'=2,'pts'=4,'comp'=2,'sub'=2] {'pts','comp'}, dimensions={0} | all-to-all | bytes 1179648 | tf_op jit(solution)/shard_map/all_to_all | solution.py:525
  25.5 4.5 %slab.1 = f32[48,32,128]{2,1,0:T(8,128)} custom-call(f32[8,144,128]{2,1,0:T(8,128)S(1)} %all_to_all.5.recv_ref), custom_call_target="tpu_custom_call" | custom-call | tf_op jit(solution)/shard_map/slab/pallas_call | solution.py:526

commit v17 on v15

--- a/solution.py
+++ b/solution.py
@@ -433,11 +433,13 @@
 
     lane_wide = lax.broadcasted_iota(jnp.int32, (DIR, LANES), 1)
 
+    not_first, not_last = lane_wide > 0, lane_wide < LANES - 1
+
+    def upwind(speed, shared, from_left, from_right):
+        return speed * (shared + jnp.where(speed > 0.0, from_left, from_right))
+
     def flux(speed, behind, centre3, onward3, beyond):
-        positive = speed > 0.0
-        near = jnp.where(positive, centre3, onward3)
-        far = jnp.where(positive, behind, beyond)
-        return speed * ((centre3 + onward3) + (near - far))
+        return upwind(speed, centre3 + onward3, centre3 - behind, onward3 - beyond)
 
     def advance(field, step, carry, finish):
         carry = list(carry)
@@ -449,12 +451,13 @@
                 centre = field[f, x + 2]
                 onward3 = 3.0 * field[f, x + 3]
                 leaving = flux(faces_x[f, x + 1], field[f, x + 1], centre3, onward3, field[f, x + 4])
-                up1 = jnp.where(lane_wide < LANES - 1, pltpu.roll(centre, LANES - 1, 1), 0.0)
-                up2 = jnp.where(lane_wide < LANES - 2, pltpu.roll(centre, LANES - 2, 1), 0.0)
-                down1 = jnp.where(lane_wide > 0, pltpu.roll(centre, 1, 1), 0.0)
-                down2 = jnp.where(lane_wide > 1, pltpu.roll(centre, 2, 1), 0.0)
-                right = flux(faces_y[f, 0, x], down1, centre3, 3.0 * up1, up2)
-                left = flux(faces_y[f, 1, x], down2, 3.0 * down1, centre3, up1)
+                up = jnp.where(not_last, pltpu.roll(centre, LANES - 1, 1), 0.0)
+                down = jnp.where(not_first, pltpu.roll(centre, 1, 1), 0.0)
+                from_left, from_right = centre3 - down, centre3 - up
+                next_right = jnp.where(not_last, pltpu.roll(from_right, LANES - 1, 1), 0.0)
+                last_left = jnp.where(not_first, pltpu.roll(from_left, 1, 1), 0.0)
+                right = upwind(faces_y[f, 0, x], centre3 + 3.0 * up, from_left, next_right)
+                left = upwind(faces_y[f, 1, x], centre3 + 3.0 * down, last_left, from_right)
                 finish(f, x, (centre - (leaving - entering) - (right - left)) * sea)
                 carry[f] = leaving, onward3
         return tuple(carry)
@@ -476,9 +479,12 @@
             at = (f * DIR + g * 8) * pitch + x
             moved_ref[pl.ds(at, 8, stride=pitch), :] = moved[g * 8 : g * 8 + 8]
 
-    def copy_out(step):
-        part = pl.ds(pl.multiple_of(step * BLOCK, BLOCK), BLOCK)
-        return pltpu.make_async_copy(done_ref.at[:, part, :], out_ref.at[:, part, :], sems.at[step])
+    def copy_out(f, block):
+        comps = pl.ds(f * DIR, DIR)
+        part = pl.ds(pl.multiple_of(block * BLOCK, BLOCK), BLOCK)
+        return pltpu.make_async_copy(
+            done_ref.at[comps, part, :], out_ref.at[comps, part, :], sems.at[f, block]
+        )
 
     def final(block, carry):
         carry = advance(second, block, carry, turn)
@@ -491,7 +497,7 @@
                 for k in (0, 1, 3, 4):
                     bent = bent + weights[k] * ring[(d + k - 2) % DIR]
                 done_ref[f * DIR + d, pl.ds(at, BLOCK), :] = bent
-        copy_out(block).start()
+            copy_out(f, block).start()
         return carry
 
     def sweep(one_block, carry):
@@ -505,7 +511,8 @@
     sweep(lambda block, carry: advance(first, block, carry, store), enter(first))
     sweep(final, enter(second))
     for block in range(slab_rows // BLOCK):
-        copy_out(block).wait()
+        for f in range(freqs):
+            copy_out(f, block).wait()
 
 
 def slab_plan(spectra, wind, growth, damping, row_cell, group_speed, current, turning):
@@ -537,7 +544,7 @@
             pltpu.VMEM((freqs, 2, slab_rows, DIR, LANES), jnp.float32),
             pltpu.VMEM((freqs * DIR * (slab_rows + 1), LANES), jnp.float32),
             pltpu.VMEM((freqs * DIR, slab_rows, LANES), jnp.float32),
-            pltpu.SemaphoreType.DMA((slab_rows // BLOCK,)),
+            pltpu.SemaphoreType.DMA((freqs, slab_rows // BLOCK)),
         ],
         compiler_params=pltpu.CompilerParams(vmem_limit_bytes=32 * 1024 * 1024),
         name="slab",

time: 30.2 us -> 30.9 us (1.023)
  Pallas kernels: 6.33 us -> 7.08 us
    pallas_call x1, Pallas kernels: 4.5 us -> 5.24 us  [slab_plan(): pl.pallas_call(functools.partial(slab_kernel, parts, tile_rows, full, fre...]
where the time goes in v17:
time: 30.9 us; the launch traced here: 30.7 us
  blocking collectives  23.6 us (76%)
  Pallas kernels  7.08 us (23%)
    all_to_all x1, blocking collectives, slab_plan(): lax.all_to_all(packed, GROUP, split_axis=0, concat_axis=0, tiled=True)  23.6 us
    pallas_call x1, Pallas kernels, slab_plan(): pl.pallas_call(functools.partial(slab_kernel, parts, tile_rows, full, fre...  5.24 us
    pallas_call x1, Pallas kernels, slab_plan(): pl.pallas_call(functools.partial(pack_kernel, parts, freqs), out_shape=pl...  1.84 us

profile of v17, /device:TPU:0, one launch (start us, length us, event | category | flops | bytes accessed | tf_op | source)
XLA Modules:
  0.0 30.7 jit_solution(17913656112533275182)
XLA Ops:
  0.0 1.8 %pack.1 = f32[8,144,128]{2,1,0:T(8,128)S(1)} custom-call(f32[320,384]{1,0:T(8,128)} %spectra_ref.1, f32[320]{0:T(512)} %wind_ref.1, f32[384]{0:T(512)} %growth_ref.1, f32[384]{0:T(512)} %damping_ref.1, s32[320]{0:T(512)} %cell_ref.1, f32[16,4,128]{2,1,0:T(4,128)} %speed_ref.1, f32[2,4,128]{2,1,0:T(4,128)} %current_ref.1, f32[4,128]{1,0:T(4,128)} %turning_ref.1), custom_call_target="tpu_custom_call" | custom-call | tf_op jit(solution)/shard_map/pack/pallas_call | solution.py:527
  1.8 23.6 %all_to_all.5.recv_ref = f32[8,144,128]{2,1,0:T(8,128)S(1)} all-to-all(f32[8,144,128]{2,1,0:T(8,128)S(1)} %pack.1), channel_id=1, replica_groups=mesh['groups'=2,'pts'=4,'comp'=2,'sub'=2] {'pts','comp'}, dimensions={0} | all-to-all | bytes 1179648 | tf_op jit(solution)/shard_map/all_to_all | solution.py:533
  25.5 5.2 %slab.1 = f32[48,32,128]{2,1,0:T(8,128)} custom-call(f32[8,144,128]{2,1,0:T(8,128)S(1)} %all_to_all.5.recv_ref), custom_call_target="tpu_custom_call" | custom-call | tf_op jit(solution)/shard_map/slab/pallas_call | solution.py:534

commit v18 on v15

--- a/solution.py
+++ b/solution.py
@@ -441,22 +441,30 @@
 
     def advance(field, step, carry, finish):
         carry = list(carry)
-        for i in range(BLOCK):
+        order = [(i, f) for i in range(BLOCK) for f in range(freqs)]
+
+        def rotations(i, f):
+            centre = field[f, step * BLOCK + i + 2]
+            return [centre] + [pltpu.roll(centre, k, 1) for k in (LANES - 1, LANES - 2, 1, 2)]
+
+        ahead = [rotations(*order[0]), rotations(*order[1])]
+        for at, (i, f) in enumerate(order):
             x = step * BLOCK + i
+            if at + 2 < len(order):
+                ahead.append(rotations(*order[at + 2]))
+            centre, up1, up2, down1, down2 = ahead.pop(0)
             sea = row(land_slots[i % 2], step * (BLOCK // 2) + i // 2)
-            for f in range(freqs):
-                entering, centre3 = carry[f]
-                centre = field[f, x + 2]
-                onward3 = 3.0 * field[f, x + 3]
-                leaving = flux(faces_x[f, x + 1], field[f, x + 1], centre3, onward3, field[f, x + 4])
-                up1 = jnp.where(lane_wide < LANES - 1, pltpu.roll(centre, LANES - 1, 1), 0.0)
-                up2 = jnp.where(lane_wide < LANES - 2, pltpu.roll(centre, LANES - 2, 1), 0.0)
-                down1 = jnp.where(lane_wide > 0, pltpu.roll(centre, 1, 1), 0.0)
-                down2 = jnp.where(lane_wide > 1, pltpu.roll(centre, 2, 1), 0.0)
-                right = flux(faces_y[f, 0, x], down1, centre3, 3.0 * up1, up2)
-                left = flux(faces_y[f, 1, x], down2, 3.0 * down1, centre3, up1)
-                finish(f, x, (centre - (leaving - entering) - (right - left)) * sea)
-                carry[f] = leaving, onward3
+            entering, centre3 = carry[f]
+            onward3 = 3.0 * field[f, x + 3]
+            leaving = flux(faces_x[f, x + 1], field[f, x + 1], centre3, onward3, field[f, x + 4])
+            up1 = jnp.where(lane_wide < LANES - 1, up1, 0.0)
+            up2 = jnp.where(lane_wide < LANES - 2, up2, 0.0)
+            down1 = jnp.where(lane_wide > 0, down1, 0.0)
+            down2 = jnp.where(lane_wide > 1, down2, 0.0)
+            right = flux(faces_y[f, 0, x], down1, centre3, 3.0 * up1, up2)
+            left = flux(faces_y[f, 1, x], down2, 3.0 * down1, centre3, up1)
+            finish(f, x, (centre - (leaving - entering) - (right - left)) * sea)
+            carry[f] = leaving, onward3
         return tuple(carry)
 
     def enter(field):

time: 30.2 us -> 30.2 us (level)
  no operation moved by 1% of the time
where the time goes in v18:
time: 30.2 us; the launch traced here: 30 us
  blocking collectives  23.6 us (78%)
  Pallas kernels  6.34 us (21%)
    all_to_all x1, blocking collectives, slab_plan(): lax.all_to_all(packed, GROUP, split_axis=0, concat_axis=0, tiled=True)  23.6 us
    pallas_call x1, Pallas kernels, slab_plan(): pl.pallas_call(functools.partial(slab_kernel, parts, tile_rows, full, fre...  4.5 us
    pallas_call x1, Pallas kernels, slab_plan(): pl.pallas_call(functools.partial(pack_kernel, parts, freqs), out_shape=pl...  1.84 us

profile of v18, /device:TPU:0, one launch (start us, length us, event | category | flops | bytes accessed | tf_op | source)
XLA Modules:
  0.0 30.0 jit_solution(7421921454929653960)
XLA Ops:
  0.0 1.8 %pack.1 = f32[8,144,128]{2,1,0:T(8,128)S(1)} custom-call(f32[320,384]{1,0:T(8,128)} %spectra_ref.1, f32[320]{0:T(512)} %wind_ref.1, f32[384]{0:T(512)} %growth_ref.1, f32[384]{0:T(512)} %damping_ref.1, s32[320]{0:T(512)} %cell_ref.1, f32[16,4,128]{2,1,0:T(4,128)} %speed_ref.1, f32[2,4,128]{2,1,0:T(4,128)} %current_ref.1, f32[4,128]{1,0:T(4,128)} %turning_ref.1), custom_call_target="tpu_custom_call" | custom-call | tf_op jit(solution)/shard_map/pack/pallas_call | solution.py:528
  1.8 23.6 %all_to_all.5.recv_ref = f32[8,144,128]{2,1,0:T(8,128)S(1)} all-to-all(f32[8,144,128]{2,1,0:T(8,128)S(1)} %pack.1), channel_id=1, replica_groups=mesh['groups'=2,'pts'=4,'comp'=2,'sub'=2] {'pts','comp'}, dimensions={0} | all-to-all | bytes 1179648 | tf_op jit(solution)/shard_map/all_to_all | solution.py:534
  25.5 4.5 %slab.1 = f32[48,32,128]{2,1,0:T(8,128)} custom-call(f32[8,144,128]{2,1,0:T(8,128)S(1)} %all_to_all.5.recv_ref), custom_call_target="tpu_custom_call" | custom-call | tf_op jit(solution)/shard_map/slab/pallas_call | solution.py:535

commit v19 on v15

--- a/solution.py
+++ b/solution.py
@@ -476,9 +476,12 @@
             at = (f * DIR + g * 8) * pitch + x
             moved_ref[pl.ds(at, 8, stride=pitch), :] = moved[g * 8 : g * 8 + 8]
 
-    def copy_out(step):
-        part = pl.ds(pl.multiple_of(step * BLOCK, BLOCK), BLOCK)
-        return pltpu.make_async_copy(done_ref.at[:, part, :], out_ref.at[:, part, :], sems.at[step])
+    def copy_out(f, block):
+        comps = pl.ds(f * DIR, DIR)
+        part = pl.ds(pl.multiple_of(block * BLOCK, BLOCK), BLOCK)
+        return pltpu.make_async_copy(
+            done_ref.at[comps, part, :], out_ref.at[comps, part, :], sems.at[f, block]
+        )
 
     def final(block, carry):
         carry = advance(second, block, carry, turn)
@@ -491,7 +494,7 @@
                 for k in (0, 1, 3, 4):
                     bent = bent + weights[k] * ring[(d + k - 2) % DIR]
                 done_ref[f * DIR + d, pl.ds(at, BLOCK), :] = bent
-        copy_out(block).start()
+            copy_out(f, block).start()
         return carry
 
     def sweep(one_block, carry):
@@ -505,7 +508,8 @@
     sweep(lambda block, carry: advance(first, block, carry, store), enter(first))
     sweep(final, enter(second))
     for block in range(slab_rows // BLOCK):
-        copy_out(block).wait()
+        for f in range(freqs):
+            copy_out(f, block).wait()
 
 
 def slab_plan(spectra, wind, growth, damping, row_cell, group_speed, current, turning):
@@ -537,7 +541,7 @@
             pltpu.VMEM((freqs, 2, slab_rows, DIR, LANES), jnp.float32),
             pltpu.VMEM((freqs * DIR * (slab_rows + 1), LANES), jnp.float32),
             pltpu.VMEM((freqs * DIR, slab_rows, LANES), jnp.float32),
-            pltpu.SemaphoreType.DMA((slab_rows // BLOCK,)),
+            pltpu.SemaphoreType.DMA((freqs, slab_rows // BLOCK)),
         ],
         compiler_params=pltpu.CompilerParams(vmem_limit_bytes=32 * 1024 * 1024),
         name="slab",

time: 30.2 us -> 30.2 us (level)
  no operation moved by 1% of the time
where the time goes in v19:
time: 30.2 us; the launch traced here: 30 us
  blocking collectives  23.6 us (78%)
  Pallas kernels  6.33 us (21%)
    all_to_all x1, blocking collectives, slab_plan(): lax.all_to_all(packed, GROUP, split_axis=0, concat_axis=0, tiled=True)  23.6 us
    pallas_call x1, Pallas kernels, slab_plan(): pl.pallas_call(functools.partial(slab_kernel, parts, tile_rows, full, fre...  4.49 us
    pallas_call x1, Pallas kernels, slab_plan(): pl.pallas_call(functools.partial(pack_kernel, parts, freqs), out_shape=pl...  1.84 us

profile of v19, /device:TPU:0, one launch (start us, length us, event | category | flops | bytes accessed | tf_op | source)
XLA Modules:
  0.0 30.0 jit_solution(16554704608604928190)
XLA Ops:
  0.0 1.8 %pack.1 = f32[8,144,128]{2,1,0:T(8,128)S(1)} custom-call(f32[320,384]{1,0:T(8,128)} %spectra_ref.1, f32[320]{0:T(512)} %wind_ref.1, f32[384]{0:T(512)} %growth_ref.1, f32[384]{0:T(512)} %damping_ref.1, s32[320]{0:T(512)} %cell_ref.1, f32[16,4,128]{2,1,0:T(4,128)} %speed_ref.1, f32[2,4,128]{2,1,0:T(4,128)} %current_ref.1, f32[4,128]{1,0:T(4,128)} %turning_ref.1), custom_call_target="tpu_custom_call" | custom-call | tf_op jit(solution)/shard_map/pack/pallas_call | solution.py:524
  1.8 23.6 %all_to_all.5.recv_ref = f32[8,144,128]{2,1,0:T(8,128)S(1)} all-to-all(f32[8,144,128]{2,1,0:T(8,128)S(1)} %pack.1), channel_id=1, replica_groups=mesh['groups'=2,'pts'=4,'comp'=2,'sub'=2] {'pts','comp'}, dimensions={0} | all-to-all | bytes 1179648 | tf_op jit(solution)/shard_map/all_to_all | solution.py:530
  25.5 4.5 %slab.1 = f32[48,32,128]{2,1,0:T(8,128)} custom-call(f32[8,144,128]{2,1,0:T(8,128)S(1)} %all_to_all.5.recv_ref), custom_call_target="tpu_custom_call" | custom-call | tf_op jit(solution)/shard_map/slab/pallas_call | solution.py:531
